TPU v7x, 128 devices: a whole 4x4x4 slice. The times are simulated.
128 devices in a mesh: tm: 16 (over y, x), lane: 8 (over z, core).
Axes of the slice: x: 4, y: 4, z: 4, core: 2. Of those that a mesh axis runs over, the one named last changes fastest.
Arguments:
- replay: bfloat16 [8, 16, 1024, 1024], P('lane', 'tm'), may hold values from -6 to 6
- block_owner: int32 [16, 8, 8, 1], P('tm'), may hold values from 0 to 7; in each aligned block of 8 rows (0 to 7, 8 to 15, ..., all dimensions but the last counted through in order) at most 2 rows name the same one
- block_slot: int32 [16, 8, 8], P('tm'), may hold values from 0 to 3
- block_fill: int32 [8, 16, 8], P('lane', 'tm'), may hold values from 64 to 256
- log_decay: float32 [8, 16, 32768], P('lane', None, 'tm'), may hold values from -2 to 0
- resets: int32 [8, 32768], P('lane', 'tm'), may hold values from 0 to 1, as said below
- cotangent: bfloat16 [8, 32768, 1024], P('lane', 'tm'), may hold values from -6 to 6
- w_in: bfloat16 [1024, 1024], replicated, may hold values from -0.1875 to 0.1875
- w_bc: bfloat16 [1024, 128], replicated, may hold values from -0.01171875 to 0.01171875
- w_out: bfloat16 [1024, 1024], replicated, may hold values from -0.1875 to 0.1875
Outputs:
- grad_in: float32 [1024, 1024], P(('tm', 'lane'))
- grad_bc: float32 [1024, 128], P(('tm', 'lane'))
- grad_out: float32 [1024, 1024], P(('tm', 'lane'))
Inputs may be any that keep to these rules, and one draw needn't show every extreme that they name: `block_owner`: among the 8 blocks of one segment on one time shard, no owner is named more than 2 times. `resets`: exactly one step of each segment is flagged.
All inputs are finite; a program needn't handle non-finite values.
Results may differ from a plain program's by a relative error of at most 0.0057.
Values may be sent and summed in bfloat16 or wider, within the bound.
No kernel may reach another device: no remote copies, remote signals or barrier semaphores. Data moves between devices by JAX's collectives and lax.ppermute only.
A program may use at most 192 MiB of HBM per device.

v0:
```python
import math

import jax
import jax.numpy as jnp
from jax import lax
from jax.experimental import pallas as pl
from jax.experimental.pallas import tpu as pltpu
from jax.sharding import Mesh
from jax.sharding import PartitionSpec as P

D = 1024
HEAD = 64
HEADS = 16
STATE = 64
BLOCK = 256
BUFCH = 4
TM = ("y", "x")
LOG2E = math.log2(math.e)
FAR = -1e4
F32, BF16 = jnp.float32, jnp.bfloat16
CNT, OPEN, CLOSE = 16, 32, 48
NT = (((1,), (1,)), ((), ()))
TN = (((0,), (0,)), ((), ()))
NN = (((1,), (0,)), ((), ()))
VMEM_LIMIT = 56 * 1024 * 1024


def mm(a, b, dims=NN):
    return lax.dot_general(a, b, dims, preferred_element_type=F32)


def split(x):
    high = x.astype(BF16)
    return jnp.concatenate([high, (x - high.astype(F32)).astype(BF16)], axis=1)


def spread_matrix():
    row = lax.broadcasted_iota(jnp.int32, (2 * 128, D), 0) & 127
    head = lax.broadcasted_iota(jnp.int32, (2 * 128, D), 1) >> 6
    return jnp.where(row == head, 1.0, 0.0).astype(BF16)


def spread(table, base, matrix):
    return mm(split(pltpu.roll(table, 128 - base, 1)), matrix)


def call(kernel, name, out_shape, grid_spec, flops, nbytes):
    return pl.pallas_call(
        kernel,
        out_shape=out_shape,
        grid_spec=grid_spec,
        name=name,
        compiler_params=pltpu.CompilerParams(vmem_limit_bytes=VMEM_LIMIT),
        cost_estimate=pl.CostEstimate(flops=flops, bytes_accessed=nbytes, transcendentals=0),
    )


def shape(dims, kind):
    return jax.ShapeDtypeStruct(dims, kind)


def valid_rows(fill, width):
    return lax.broadcasted_iota(jnp.int32, (BLOCK, width), 0) < fill


def upstream_kernel(fill, decay, resets, cot, w_out, up, rows, cols, ends):
    b = pl.program_id(0)
    upper = lax.broadcasted_iota(jnp.int32, (BLOCK, BLOCK), 0) <= lax.broadcasted_iota(
        jnp.int32, (BLOCK, BLOCK), 1
    )
    upper = jnp.where(upper, 1.0, 0.0)
    both = jnp.concatenate(
        [decay[...] * LOG2E, jnp.broadcast_to(resets[0].astype(F32), (8, BLOCK))], axis=0
    )
    summed = lax.dot_general(
        both, upper, NN, precision=lax.Precision.HIGHEST, preferred_element_type=F32
    )
    cum, count = summed[:HEADS], summed[HEADS : HEADS + 8]
    two = jnp.concatenate([count, count], axis=0)
    opening = jnp.where(two == 0.0, jnp.exp2(cum), 0.0)
    last = jnp.broadcast_to(cum[:, BLOCK - 1 :], (HEADS, BLOCK))
    last_two = jnp.broadcast_to(two[:, BLOCK - 1 :], (HEADS, BLOCK))
    closing = jnp.where(two == last_two, jnp.exp2(last - cum), 0.0)
    table = jnp.concatenate(
        [cum, two, opening, closing, jnp.zeros((64, BLOCK), F32)], axis=0
    )
    rows[...] = table[:32]
    turned = table.T
    cols[...] = turned
    ends[0] = jnp.broadcast_to(turned[BLOCK - 1 :], (8, 128))
    masked = jnp.where(valid_rows(fill[b], D), cot[0], jnp.zeros((), BF16))
    up[...] = mm(masked, w_out[...], NT).astype(BF16)


def inside(inner, keys, up, rows, cols, ro, gi, pair):
    at = lax.broadcasted_iota(jnp.int32, (BLOCK, BLOCK), 0)
    to = lax.broadcasted_iota(jnp.int32, (BLOCK, BLOCK), 1)
    linked = (to <= at) & (cols[:, CNT : CNT + 1] == rows[CNT : CNT + 1, :])
    bias = jnp.where(linked, 0.0, FAR)
    k = keys[...]
    scores = mm(k[:, STATE:], k[:, :STATE], NT)
    left = lax.broadcasted_iota(jnp.int32, (BLOCK, 128), 1) < HEAD
    zero = jnp.zeros((), BF16)
    paired = jnp.zeros((BLOCK, BLOCK), F32)
    for q in range(HEADS // 2):
        lanes = slice(128 * q, 128 * q + 128)
        x, u = inner[:, lanes], up[:, lanes]
        readout = grad = None
        for s in range(2):
            h = 2 * q + s
            mine = left if s == 0 else ~left
            xs, us = jnp.where(mine, x, zero), jnp.where(mine, u, zero)
            decays = jnp.exp2(cols[:, h : h + 1] - rows[h : h + 1, :] + bias)
            mixing = (decays * scores).astype(BF16)
            paired = paired + decays * mm(us, x, NT)
            r, g = mm(mixing, xs), mm(mixing, us, TN)
            readout = r if s == 0 else readout + r
            grad = g if s == 0 else grad + g
        ro[:, lanes] = readout.astype(BF16)
        gi[:, lanes] = grad.astype(BF16)
    pair[0] = paired.astype(BF16)


def stage_kernel(count, number, block, source, index, fill, *refs):
    picks = refs[:number]
    w_in, w_bc, up, rows, cols = refs[number : number + 5]
    outs = refs[-9:]
    taken, inner, keys, ro, gi, pair, push_in, push_out, matrix = outs
    i = pl.program_id(0)

    @pl.when(i == 0)
    def _():
        matrix[...] = spread_matrix()

    @pl.when(i < count[0])
    def _():
        raw = picks[0][...]
        for n in range(1, number):
            raw = jnp.where(jnp.full((BLOCK, D), source[i], jnp.int32) == n, picks[n][...], raw)
        got = jnp.where(valid_rows(fill[jnp.minimum(block[i], fill.shape[0] - 1)], D), raw, jnp.zeros((), BF16))
        taken[...] = got
        x = mm(got, w_in[...]).astype(BF16)
        k = mm(got, w_bc[...]).astype(BF16)
        inner[...] = x
        keys[...] = k
        table = cols[...]
        opening = spread(table, OPEN, matrix[...])
        closing = spread(table, CLOSE, matrix[...])
        into = (closing * x.astype(F32)).astype(BF16)
        out = (opening * up[...].astype(F32)).astype(BF16)
        turned = k.astype(F32).T.astype(BF16)
        push_in[0] = mm(turned[:STATE], into)
        push_out[0] = mm(turned[STATE:], out)
        inside(inner, keys, up, rows, cols, ro, gi, pair)


def local_kernel(push_in, push_out, ends, starts, gains, total, factors, state):
    b = pl.program_id(0)

    @pl.when(b == 0)
    def _():
        table = ends[...].reshape(factors.shape[0], 128)
        factors[...] = spread(table, OPEN, spread_matrix())
        state[...] = jnp.zeros_like(state)

    factor = factors[pl.ds(b * 8, 8)]
    before = jnp.where(b == 0, 1.0, state[128:])
    starts[0] = state[:64]
    gains[0] = jnp.concatenate([factor, before], axis=0)
    state[:64] = state[:64] * factor[:1] + push_in[0]
    state[64:128] = state[64:128] + before[:1] * push_out[0]
    state[128:] = before * factor

    @pl.when(b == pl.num_programs(0) - 1)
    def _():
        gain = state[128:]
        high = gain.astype(BF16).astype(F32)
        top = lax.broadcasted_iota(jnp.int32, gain.shape, 0) == 0
        gain = jnp.where(top, high, gain - high)
        for n in range(total.shape[0]):
            total[n] = jnp.concatenate([state[8 * n : 8 * n + 8], gain], axis=0).astype(BF16)


def scan_kernel(which, terms, entering, forth):
    shards = terms.shape[0]
    part = lambda t: terms[t].astype(F32)
    gain = lambda v: v[8:9] + v[9:10]
    state = jnp.zeros((8, D), F32)
    for t in range(shards):
        forth[t] = state
        v = part(t)
        state = state * gain(v) + v[:8]
    back = jnp.zeros((8, D), F32)
    ahead = jnp.full((8, D), which[0], jnp.int32) < shards // 2
    for t in reversed(range(shards)):
        entering[t] = jnp.where(ahead, forth[t], back).astype(BF16)
        v = part(t)
        back = back * gain(v) + v[:8]


def store_halves(core, acc, keep, give):
    scale = 1.0 / 512.0
    keep[...] = (acc[:, core[0]] * scale).reshape(keep.shape)
    give[...] = (acc[:, 1 - core[0]] * scale).reshape(give.shape).astype(BF16)


def readout_kernel(core, fill, cot, keys, cols, ro, starts, gains, enter, keep, give, acc, left, right, matrix):
    step = pl.program_id(0)

    @pl.when(step == 0)
    def _():
        matrix[...] = spread_matrix()
        acc[...] = jnp.zeros_like(acc)

    for n in range(2):
        at = slice(n * BLOCK, n * BLOCK + BLOCK)
        start = (starts[n] + gains[n, 8:9] * enter[:64].astype(F32)).astype(BF16)
        opening = spread(cols[at], OPEN, matrix[...])
        left[at] = (ro[at].astype(F32) + opening * mm(keys[at, STATE:], start)).astype(BF16)
        right[at] = jnp.where(valid_rows(fill[2 * step + n], D), cot[0, at], jnp.zeros((), BF16))
    acc[...] += mm(left[...], right[...], TN).reshape(acc.shape)

    @pl.when(step == pl.num_programs(0) - 1)
    def _():
        store_halves(core, acc, keep, give)


def gradient_kernel(
    core, taken, inner, up, keys, cols, gi, pair, starts, push_out, gains, enter,
    keep, give, acc, right, finish, matrix,
):
    step = pl.program_id(0)

    @pl.when(step == 0)
    def _():
        matrix[...] = spread_matrix()
        finish[...] = enter[64:].astype(F32)
        acc[...] = jnp.zeros_like(acc)

    for n in (1, 0):
        at = slice(n * BLOCK, n * BLOCK + BLOCK)
        factor, before = gains[n, 0:1], gains[n, 8:9]
        start = (starts[n] + before * enter[:64].astype(F32)).astype(BF16)
        end = finish[...].astype(BF16)
        finish[...] = finish[...] * factor + push_out[n]
        table = cols[at]
        opening = spread(table, OPEN, matrix[...])
        closing = spread(table, CLOSE, matrix[...])
        k = keys[at]
        write, read = k[:, :STATE], k[:, STATE:]
        right[at, :D] = (gi[at].astype(F32) + closing * mm(write, end)).astype(BF16)
        into = (closing * inner[at].astype(F32)).astype(BF16)
        out = (opening * up[at].astype(F32)).astype(BF16)
        g = pair[n]
        grad_write = mm(g, read, TN) + mm(into, end, NT)
        grad_read = mm(g, write) + mm(out, start, NT)
        right[at, D:] = jnp.concatenate([grad_write, grad_read], axis=1).astype(BF16)
    acc[...] += mm(taken[...], right[...], TN).reshape(acc.shape)

    @pl.when(step == pl.num_programs(0) - 1)
    def _():
        store_halves(core, acc, keep, give)


def ring(axis, by):
    size = lax.axis_size(axis)
    return [(k, (k + by) % size) for k in range(size)]


CHIPS = ("y", "x", "z")


def over_chip(keep, give):
    got = lax.ppermute(give, "c", ring("c", 1))
    half = (keep + got.astype(F32)).astype(BF16)
    return half.reshape(lax.axis_size(CHIPS), 8, -1)


def over_chips(half):
    return lax.all_to_all(half, CHIPS, 0, 0).astype(F32).sum(0)


def on_device(
    replay, block_owner, block_slot, block_fill, log_decay, resets, cotangent, w_in, w_bc, w_out
):
    shards = lax.axis_size(TM)
    core, z = lax.axis_index("c"), lax.axis_index("z")
    my_lane = z * 2 + core
    blocks = block_fill.shape[2]
    steps = blocks * BLOCK
    fill = block_fill[0, 0]
    owner = lax.dynamic_index_in_dim(block_owner[0, :, :, 0], my_lane, 0, keepdims=False)
    slot = lax.dynamic_index_in_dim(block_slot[0], my_lane, 0, keepdims=False)

    mine = replay[0, 0].reshape(BUFCH, BLOCK, D)
    swap = lambda v: lax.ppermute(v, "c", ring("c", 1))
    up_z = lambda v: lax.ppermute(v, "z", ring("z", 1))
    down_z = lambda v: lax.ppermute(v, "z", ring("z", -1))
    first, second = mine[:2], mine[2:]
    below_a, above_a = up_z(first), down_z(second)
    other = swap(mine)
    away = (owner // 2 - z) % 4
    same = owner % 2 == core
    low = slot < 2
    stage = jnp.where(away == 0, 0, jnp.where(away == 2, 3, jnp.where((away == 3) == low, 1, 2)))
    side = jnp.where(away == 2, jnp.where(low, 0, 1), jnp.where(away == 3, 0, 1))
    source = jnp.where(away == 0, jnp.where(same, 0, 1), side + jnp.where(same, 0, 2))
    index = jnp.where(away == 0, slot, slot % 2)
    ids = jnp.arange(blocks)
    rank = jnp.sum((stage[None] == stage[:, None]) & (ids[None] < ids[:, None]), axis=1)
    counts = jnp.sum(stage[None] == jnp.arange(4)[:, None], axis=1)
    most = (4, blocks, blocks, 4)
    turn = jnp.minimum(jnp.arange(blocks)[None], counts[:, None] - 1)
    chosen = (stage[None, None] == jnp.arange(4)[:, None, None]) & (rank[None, None] == turn[:, :, None])
    of = lambda v: jnp.sum(jnp.where(chosen, v[None, None], 0), axis=2)
    block = jnp.where(counts[:, None] > 0, of(ids), blocks).astype(jnp.int32)
    source, index = of(source).astype(jnp.int32), of(index).astype(jnp.int32)
    counts = counts.astype(jnp.int32)

    whole = lambda *dims: pl.BlockSpec(dims, lambda b, *_: (0,) * len(dims))
    tall = lambda width: pl.BlockSpec((BLOCK, width), lambda b, *_: (b, 0))
    lead = lambda *dims: pl.BlockSpec((1, *dims), lambda b, *_: (b,) + (0,) * len(dims))
    table_rows = pl.BlockSpec((32, BLOCK), lambda b, *_: (0, b))
    vmem = lambda kind, *dims: pltpu.VMEM(dims, kind)

    up, rows, cols, ends = call(
        upstream_kernel,
        "upstream",
        (
            shape((steps, D), BF16),
            shape((32, steps), F32),
            shape((steps, 128), F32),
            shape((blocks, 8, 128), F32),
        ),
        pltpu.PrefetchScalarGridSpec(
            num_scalar_prefetch=1,
            grid=(blocks,),
            in_specs=[
                pl.BlockSpec((HEADS, BLOCK), lambda b, *_: (0, b)),
                pl.BlockSpec((1, 1, BLOCK), lambda b, *_: (b, 0, 0)),
                pl.BlockSpec((1, BLOCK, D), lambda b, *_: (0, b, 0)),
                whole(D, D),
            ],
            out_specs=[tall(D), table_rows, tall(128), lead(8, 128)],
        ),
        2 * steps * D * D,
        12 << 20,
    )(fill, log_decay[0], resets.reshape(blocks, 1, BLOCK), cotangent, w_out)

    room = steps + BLOCK
    made = None
    for s in range(4):
        if s == 0:
            sources = (mine, other)
        elif s == 1:
            below_a, above_a, second, first, made = lax.optimization_barrier(
                (below_a, above_a, second, first, made)
            )
            below_b, above_b = up_z(second), down_z(first)
            sources = (below_a, above_a, swap(below_a), swap(above_a))
        elif s == 2:
            below_b, above_b, below_a, above_a, made = lax.optimization_barrier(
                (below_b, above_b, below_a, above_a, made)
            )
            far_low, far_high = up_z(below_a), down_z(above_a)
            sources = (below_b, above_b, swap(below_b), swap(above_b))
        else:
            far_low, far_high, made = lax.optimization_barrier((far_low, far_high, made))
            sources = (far_low, far_high, swap(far_low), swap(far_high))
        number = len(sources)
        at = lambda i, block, *_: block[i]
        inside_at = lambda i, block, *_: jnp.minimum(block[i], blocks - 1)
        out_rows = lambda width: pl.BlockSpec((BLOCK, width), lambda i, block, *_: (block[i], 0))
        out_lead = lambda *dims: pl.BlockSpec((1, *dims), lambda i, block, *_: (block[i], 0, 0))
        in_rows = lambda width: pl.BlockSpec(
            (BLOCK, width), lambda i, block, *_: (jnp.minimum(block[i], blocks - 1), 0)
        )
        pick = lambda n: pl.BlockSpec(
            (pl.squeezed, BLOCK, D),
            lambda i, block, source, index, *_: (jnp.where(source[i] == n, index[i], 0), 0, 0),
        )
        kept = [] if made is None else list(made)
        body = lambda block, source, index, fill, count, *refs, number=number: stage_kernel(
            count, number, block, source, index, fill, *refs
        )
        made = pl.pallas_call(
            body,
            out_shape=(
                shape((room, D), BF16),
                shape((room, D), BF16),
                shape((room, 128), BF16),
                shape((room, D), BF16),
                shape((room, D), BF16),
                shape((blocks + 1, BLOCK, BLOCK), BF16),
                shape((blocks + 1, STATE, D), F32),
                shape((blocks + 1, STATE, D), F32),
            ),
            grid_spec=pltpu.PrefetchScalarGridSpec(
                num_scalar_prefetch=5,
                grid=(most[s],),
                in_specs=[pick(n) for n in range(number)]
                + [
                    whole(D, D),
                    whole(D, 128),
                    in_rows(D),
                    pl.BlockSpec((32, BLOCK), lambda i, block, *_: (0, jnp.minimum(block[i], blocks - 1))),
                    in_rows(128),
                ]
                + [pl.BlockSpec(memory_space=pl.ANY)] * len(kept),
                out_specs=[
                    out_rows(D),
                    out_rows(D),
                    out_rows(128),
                    out_rows(D),
                    out_rows(D),
                    out_lead(BLOCK, BLOCK),
                    out_lead(STATE, D),
                    out_lead(STATE, D),
                ],
                scratch_shapes=[vmem(BF16, 256, D)],
            ),
            input_output_aliases={5 + number + 5 + n: n for n in range(len(kept))},
            name=f"stage_{s}",
            compiler_params=pltpu.CompilerParams(vmem_limit_bytes=VMEM_LIMIT),
            cost_estimate=pl.CostEstimate(
                flops=4 * BLOCK * D * (D + 1024) + 4 * HEADS * 3 * BLOCK**3,
                bytes_accessed=16 << 20,
                transcendentals=0,
            ),
        )(block[s], source[s], index[s], fill, counts[s : s + 1], *sources, w_in, w_bc, up, rows, cols, *kept)
    taken, inner, keys, ro, gi, pair, push_in, push_out = made

    starts, gains, total = call(
        local_kernel,
        "local",
        (shape((blocks, STATE, D), F32), shape((blocks, 16, D), F32), shape((shards, 16, D), BF16)),
        pl.GridSpec(
            grid=(blocks,),
            in_specs=[lead(STATE, D), lead(STATE, D), whole(blocks, 8, 128)],
            out_specs=[lead(STATE, D), lead(16, D), whole(shards, 16, D)],
            scratch_shapes=[vmem(F32, blocks * 8, D), vmem(F32, 136, D)],
        ),
        1 << 24,
        7 << 20,
    )(push_in, push_out, ends)

    terms = lax.all_to_all(total, TM, 0, 0)
    entering = call(
        scan_kernel,
        "scan",
        shape((shards, 8, D), BF16),
        pltpu.PrefetchScalarGridSpec(
            num_scalar_prefetch=1,
            grid=(1,),
            in_specs=[whole(shards, 16, D)],
            out_specs=whole(shards, 8, D),
            scratch_shapes=[vmem(F32, shards, 8, D)],
        ),
        1 << 20,
        1 << 20,
    )(lax.axis_index(TM).reshape(1), terms)
    enter = lax.all_to_all(entering, TM, 0, 0).reshape(128, D)

    own_core = core.reshape(1)
    two = lambda width: pl.BlockSpec((2 * BLOCK, width), lambda b, *_: (b, 0))
    pairs = lambda *dims: pl.BlockSpec((2, *dims), lambda b, *_: (b, 0, 0))
    keep_out, give_out = call(
        readout_kernel,
        "readout",
        (shape((D // 2, D), F32), shape((D // 2, D), BF16)),
        pltpu.PrefetchScalarGridSpec(
            num_scalar_prefetch=2,
            grid=(blocks // 2,),
            in_specs=[
                pl.BlockSpec((1, 2 * BLOCK, D), lambda b, *_: (0, b, 0)),
                two(128),
                two(128),
                two(D),
                pairs(STATE, D),
                pairs(16, D),
                whole(128, D),
            ],
            out_specs=[whole(D // 2, D), whole(D // 2, D)],
            scratch_shapes=[
                vmem(F32, D // 16, 2, 8, D),
                vmem(BF16, 2 * BLOCK, D),
                vmem(BF16, 2 * BLOCK, D),
                vmem(BF16, 256, D),
            ],
        ),
        2 * steps * D * (D + 256),
        14 << 20,
    )(own_core, fill, cotangent, keys, cols, ro, starts, gains, enter)

    half_out, enter = lax.optimization_barrier((over_chip(keep_out, give_out), enter))
    back = lambda spec: pl.BlockSpec(
        spec.block_shape, lambda s, *refs: spec.index_map(blocks // 2 - 1 - s, *refs)
    )
    wide = D + 128
    keep_in, give_in = call(
        gradient_kernel,
        "gradient",
        (shape((D // 2, wide), F32), shape((D // 2, wide), BF16)),
        pltpu.PrefetchScalarGridSpec(
            num_scalar_prefetch=1,
            grid=(blocks // 2,),
            in_specs=[
                back(s)
                for s in (
                    two(D),
                    two(D),
                    two(D),
                    two(128),
                    two(128),
                    two(D),
                    pairs(BLOCK, BLOCK),
                    pairs(STATE, D),
                    pairs(STATE, D),
                    pairs(16, D),
                    whole(128, D),
                )
            ],
            out_specs=[whole(D // 2, wide), whole(D // 2, wide)],
            scratch_shapes=[
                vmem(F32, D // 16, 2, 8, wide),
                vmem(BF16, 2 * BLOCK, wide),
                vmem(F32, STATE, D),
                vmem(BF16, 256, D),
            ],
        ),
        2 * steps * D * (D + 1024),
        26 << 20,
    )(own_core, taken, inner, up, keys, cols, gi, pair, starts, push_out, gains, enter)

    grad_out = over_chips(half_out)
    grad_in = over_chips(over_chip(keep_in, give_in))
    return (grad_in[:, :D], grad_in[:, D:], grad_out)


def solution(mesh):
    torus = Mesh(mesh.devices.reshape(4, 4, 4, 2), ("y", "x", "z", "c"))
    lane = ("z", "c")
    every = TM + lane
    return jax.shard_map(
        on_device,
        mesh=torus,
        in_specs=(
            P(lane, TM, None, None),
            P(TM, None, None, None),
            P(TM, None, None),
            P(lane, TM, None),
            P(lane, None, TM),
            P(lane, TM),
            P(lane, TM, None),
            P(),
            P(),
            P(),
        ),
        out_specs=(P(every, None), P(every, None), P(every, None)),
        check_vma=False,
    )
```

profile of v0, /device:TPU:0, one launch (start us, length us, event | category | flops | bytes accessed | tf_op | source)
XLA Modules:
  0.0 248.2 jit_solution(2618825277778628231)
XLA Ops:
  0.6 0.0 copy-start
  0.6 3.2 %fusion.14 = (bf16[1,1,512,1024]{3,2,1,0:T(8,128)(2,1)}, bf16[1,1,512,1024]{3,2,1,0:T(8,128)(2,1)}) fusion(bf16[1,1,1024,1024]{3,2,1,0:T(8,128)(2,1)} %param.10), kind=kLoop, calls=%fused_computation.76 | loop fusion | bytes 4194304 | tf_op jit(solution)/shard_map/slice | solution.py:299
  3.8 2.0 collective-permute-start
  5.8 2.1 collective-permute-start.1
  8.0 0.7 fusion.13
  8.7 0.7 compare_select_fusion.8
  9.4 0.1 convert_reduce_fusion.3
  9.5 0.2 convert_reduce_fusion.2
  9.7 0.1 iota_minimum_fusion
  9.8 0.4 select_reduce_fusion
  10.1 0.1 broadcast_select_fusion
  10.2 0.6 slice_bitcast_fusion
  10.8 0.6 slice_bitcast_fusion.2
  11.4 0.7 fusion.15
  12.1 11.6 %upstream.1 = (bf16[2048,1024]{1,0:T(8,128)(2,1)}, f32[32,2048]{1,0:T(8,128)}, f32[2048,128]{1,0:T(8,128)}, f32[8,8,128]{2,1,0:T(8,128)}) custom-call(s32[8]{0:T(128)} %bitcast.81, f32[16,2048]{1,0:T(8,128)} %bitcast.87, s32[8,1,256]{2,1,0:T(1,128)} %bitcast.88, bf16[1,2048,1024]{2,1,0:T(8,128)(2,1)} %cot.3, bf16[1024,1024]{1,0:T(8,128)(2,1)} %w_out.1), custom_call_target="tpu_custom_call" | custom-call | flops 4294967296 | bytes 12582912 | tf_op jit(solution)/shard_map/upstream/pallas_call | solution.py:326
  23.7 0.0 collective-permute-done.2.refs_1_
  23.7 9.8 %stage_0.1 = (bf16[2304,1024]{1,0:T(8,128)(2,1)}, bf16[2304,1024]{1,0:T(8,128)(2,1)}, bf16[2304,128]{1,0:T(8,128)(2,1)}, bf16[2304,1024]{1,0:T(8,128)(2,1)}, bf1...) custom-call(s32[8]{0:T(128)} %get-tuple-element.179.block, ...), custom_call_target="tpu_custom_call" | custom-call | flops 5368709120 | bytes 16777216 | tf_op jit(solution)/shard_map/stage_0/pallas_call | solution.py:386
  33.6 0.0 collective-permute-done.refs_0_
  33.6 0.0 collective-permute-done.1.refs_1_
  33.6 4.7 %collective-permute-start.5 = (bf16[2,256,1024]{2,1,0:T(8,128)(2,1)S(1)}, bf16[2,256,1024]{2,1,0:T(8,128)(2,1)S(1)}, u32[]{:S(2)}, u32[]{:S(2)}) collective-permute-start(bf16[2,256,1024]{2,1,0:T(8,128)(2,1)S(1)} %collective-permute-done.refs_0_), channel_id=1, source_target_pairs={{0,1},{1,0},{2,3},{3,2},{4,5},{5,4},{6,7},{7,6},{8,9},{9,8},{10,11... | collective-permute-start | bytes 3145736 | tf_op jit(solution)/shard_map/ppermute | solution.py:296
  38.2 0.1 collective-permute-start.6
  38.3 3.7 %collective-permute-start.3 = (bf16[2,256,1024]{2,1,0:T(8,128)(2,1)}, bf16[2,256,1024]{2,1,0:T(8,128)(2,1)S(1)}, u32[]{:S(2)}, u32[]{:S(2)}) collective-permute-start(bf16[2,256,1024]{2,1,0:T(8,128)(2,1)} %bitcast.12), channel_id=1, source_target_pairs={{0,2},{2,4},{4,6},{6,0},{1,3},{3,5},{5,7},{7,1},{8,10},{10,12},{12... | collective-permute-start | bytes 3145736 | tf_op jit(solution)/shard_map/ppermute | solution.py:297
  42.1 0.0 collective-permute-start.4
  42.1 0.0 collective-permute-done.5.refs_2_
  42.1 0.2 collective-permute-done.6.refs_3_
  42.3 0.9 copy-done.8
  43.1 0.3 copy-done.11
  43.4 15.8 %stage_1.1 = (bf16[2304,1024]{1,0:T(8,128)(2,1)}, bf16[2304,1024]{1,0:T(8,128)(2,1)}, bf16[2304,128]{1,0:T(8,128)(2,1)}, bf16[2304,1024]{1,0:T(8,128)(2,1)}, bf1...) custom-call(s32[8]{0:T(128)} %get-tuple-element.178.block, ...), custom_call_target="tpu_custom_call", output_to_operand_aliasing={{0}: (14, {}), {1}: (15, {}), {2}: (16, {}), {3}: (17, {}),... | custom-call | flops 5368709120 | bytes 16777216 | tf_op jit(solution)/shard_map/stage_1/pallas_call | solution.py:386
  59.3 6.1 %collective-permute-done.3.refs_0_ = bf16[2,256,1024]{2,1,0:T(8,128)(2,1)S(1)} collective-permute-done((bf16[2,256,1024]{2,1,0:T(8,128)(2,1)}, bf16[2,256,1024]{2,1,0:T(8,128)(2,1)S(1)}, u32[]{:S(2)}, u32[]{:S(2)}) %collective-permute-start.3) | collective-permute-done | bytes 1048608 | tf_op jit(solution)/shard_map/ppermute | solution.py:297
  65.4 2.1 collective-permute-done.4.refs_1_
  67.5 0.5 collective-permute-start.10
  68.0 0.4 collective-permute-start.7
  68.4 2.9 %collective-permute-start.8 = (bf16[2,256,1024]{2,1,0:T(8,128)(2,1)}, bf16[2,256,1024]{2,1,0:T(8,128)(2,1)S(1)}, u32[]{:S(2)}, u32[]{:S(2)}) collective-permute-start(bf16[2,256,1024]{2,1,0:T(8,128)(2,1)} %collective-permute-done.1.refs_1_), channel_id=1, source_target_pairs={{0,6},{2,0},{4,2},{6,4},{1,7},{3,1},{5,3},{7,5},{8,14},{10,8},{12,... | collective-permute-start | bytes 3145736 | tf_op jit(solution)/shard_map/ppermute | solution.py:298
  71.3 0.4 collective-permute-done.10.refs_3_
  71.7 0.6 copy-done.7
  72.3 0.4 copy-done.9
  72.6 20.0 %stage_2.1 = (bf16[2304,1024]{1,0:T(8,128)(2,1)}, bf16[2304,1024]{1,0:T(8,128)(2,1)}, bf16[2304,128]{1,0:T(8,128)(2,1)}, bf16[2304,1024]{1,0:T(8,128)(2,1)}, bf1...) custom-call(s32[8]{0:T(128)} %get-tuple-element.177.block, ...), custom_call_target="tpu_custom_call", output_to_operand_aliasing={{0}: (14, {}), {1}: (15, {}), {2}: (16, {}), {3}: (17, {}),... | custom-call | flops 5368709120 | bytes 16777216 | tf_op jit(solution)/shard_map/stage_2/pallas_call | solution.py:386
  92.6 1.9 collective-permute-done.7.refs_0_
  94.5 0.1 collective-permute-start.11
  94.6 0.5 collective-permute-start.12
  95.1 2.1 collective-permute-done.11.refs_2_
  97.3 1.5 collective-permute-done.12.refs_3_
  98.8 1.0 copy-done.12
  99.7 14.5 %stage_3.1 = (bf16[2304,1024]{1,0:T(8,128)(2,1)}, bf16[2304,1024]{1,0:T(8,128)(2,1)}, bf16[2304,128]{1,0:T(8,128)(2,1)}, bf16[2304,1024]{1,0:T(8,128)(2,1)}, bf1...) custom-call(s32[8]{0:T(128)} %get-tuple-element.180.block, ...), custom_call_target="tpu_custom_call", output_to_operand_aliasing={{0}: (14, {}), {1}: (15, {}), {2}: (16, {}), {3}: (17, {}),... | custom-call | flops 5368709120 | bytes 16777216 | tf_op jit(solution)/shard_map/stage_3/pallas_call | solution.py:386
  114.2 6.9 %local.1 = (f32[8,64,1024]{2,1,0:T(8,128)}, f32[8,16,1024]{2,1,0:T(8,128)}, bf16[16,16,1024]{2,1,0:T(8,128)(2,1)}) custom-call(f32[9,64,1024]{2,1,0:T(8,128)} %get-tuple-element.148.push_in, f32[9,64,1024]{2,1,0:T(8,128)} %get-tuple-element.149.push_out, f32[8,8,128]{2,1,0:T(8,128)} %get-tuple-element.150.ends), custom_call_target="tpu_custom_call" | custom-call | flops 16777216 | bytes 7340032 | tf_op jit(solution)/shard_map/local/pallas_call | solution.py:433
  121.1 9.7 %all-to-all-start = ((bf16[16,16,1024]{2,1,0:T(8,128)(2,1)}), bf16[16,16,1024]{2,1,0:T(8,128)(2,1)S(1)}, u32[]{:S(2)}, u32[]{:S(2)}) async-start(bf16[16,16,1024]{2,1,0:T(8,128)(2,1)} %get-tuple-element.154), calls=%async_computation | async-start | bytes 1048576 | tf_op jit(solution)/shard_map/all_to_all | solution.py:447
  130.8 10.1 %all-to-all-done.terms = bf16[16,16,1024]{2,1,0:T(8,128)(2,1)S(1)} async-done(((bf16[16,16,1024]{2,1,0:T(8,128)(2,1)}), bf16[16,16,1024]{2,1,0:T(8,128)(2,1)S(1)}, u32[]{:S(2)}, u32[]{:S(2)}) %all-to-all-start) | async-done | bytes 524320 | tf_op jit(solution)/shard_map/all_to_all | solution.py:447
  141.0 0.8 copy-done.1
  141.7 2.0 scan.1
  143.7 12.9 %all_to_all.20 = bf16[16,8,1024]{2,1,0:T(8,128)(2,1)} all-to-all(bf16[16,8,1024]{2,1,0:T(8,128)(2,1)} %scan.1), channel_id=1, replica_groups=mesh['y'=4,'x'=4,'z'=4,'c'=2] {'y','x'}, dimensions={0} | all-to-all | bytes 524288 | tf_op jit(solution)/shard_map/all_to_all | solution.py:462
  156.6 12.6 %readout.1 = (f32[512,1024]{1,0:T(8,128)}, bf16[512,1024]{1,0:T(8,128)(2,1)}) custom-call(s32[1]{0:T(128)} %bitcast.core, s32[8]{0:T(128)} %bitcast.86, bf16[1,2048,1024]{2,1,0:T(8,128)(2,1)} %cot.3, bf16[2304,128]{1,0:T(8,128)(2,1)} %get-tuple-element.145.keys, f32[2048,128]{1,0:T(8,128)} %get-tuple-element.84.refs_6_.refs_8_.cols, ...), custom_call_target="tpu_custom_call" | custom-call | flops 5368709120 | bytes 14680064 | tf_op jit(solution)/shard_map/readout/pallas_call | solution.py:467
  169.2 2.9 %collective-permute-done.13 = bf16[512,1024]{1,0:T(8,128)(2,1)S(1)} collective-permute-done((bf16[512,1024]{1,0:T(8,128)(2,1)}, bf16[512,1024]{1,0:T(8,128)(2,1)S(1)}, u32[]{:S(2)}, u32[]{:S(2)}) %collective-permute-start.13) | collective-permute-done | bytes 1048608 | tf_op jit(solution)/shard_map/ppermute | solution.py:274
  172.0 3.0 %fusion.1 = bf16[64,8,1024]{2,1,0:T(8,128)(2,1)} fusion(f32[512,1024]{1,0:T(8,128)} %get-tuple-element.155, bf16[512,1024]{1,0:T(8,128)(2,1)S(1)} %collective-permute-done.13), kind=kLoop, calls=%fused_computation.5 | loop fusion | flops 1572864 | bytes 4194304 | tf_op jit(solution)/shard_map/reshape | solution.py:276
  175.0 18.1 %gradient.1 = (f32[512,1152]{1,0:T(8,128)}, bf16[512,1152]{1,0:T(8,128)(2,1)}) custom-call(s32[1]{0:T(128)} %bitcast.core, bf16[2304,1024]{1,0:T(8,128)(2,1)} %get-tuple-element.143.taken, bf16[2304,1024]{1,0:T(8,128)(2,1)} %get-tuple-element.144.inner, bf16[2048,1024]{1,0:T(8,128)(2,1)} %get-tuple-element.82.refs_4_.refs_6_.up, ...), custom_call_target="tpu_custom_call" | custom-call | flops 8589934592 | bytes 27262976 | tf_op jit(solution)/shard_map/gradient/pallas_call | solution.py:500
  193.1 0.4 collective-permute-start.14
  193.5 9.9 %all-to-all-start.3 = ((bf16[64,8,1024]{2,1,0:T(8,128)(2,1)}), bf16[64,8,1024]{2,1,0:T(8,128)(2,1)S(1)}, u32[]{:S(2)}, u32[]{:S(2)}) async-start(bf16[64,8,1024]{2,1,0:T(8,128)(2,1)} %fusion.1), calls=%async_computation.3 | async-start | bytes 2097152 | tf_op jit(solution)/shard_map/all_to_all | solution.py:280
  203.4 2.9 %fusion = bf16[64,8,1152]{2,1,0:T(8,128)(2,1)} fusion(f32[512,1152]{1,0:T(8,128)} %get-tuple-element.158, bf16[512,1152]{1,0:T(8,128)(2,1)S(1)} %collective-permute-done.14), kind=kLoop, calls=%fused_computation.4 | loop fusion | flops 1769472 | bytes 4718592 | tf_op jit(solution)/shard_map/reshape | solution.py:276
  206.3 16.3 %all-to-all-done.3 = bf16[64,8,1024]{2,1,0:T(8,128)(2,1)S(1)} async-done(((bf16[64,8,1024]{2,1,0:T(8,128)(2,1)}), bf16[64,8,1024]{2,1,0:T(8,128)(2,1)S(1)}, u32[]{:S(2)}, u32[]{:S(2)}) %all-to-all-start.3) | async-done | bytes 1048608 | tf_op jit(solution)/shard_map/all_to_all | solution.py:280
  222.6 4.7 %all-to-all-start.2 = ((bf16[64,8,1152]{2,1,0:T(8,128)(2,1)}), bf16[64,8,1152]{2,1,0:T(8,128)(2,1)S(1)}, u32[]{:S(2)}, u32[]{:S(2)}) async-start(bf16[64,8,1152]{2,1,0:T(8,128)(2,1)} %fusion), calls=%async_computation.2 | async-start | bytes 2359296 | tf_op jit(solution)/shard_map/all_to_all | solution.py:280
  227.3 0.8 convert_reduce_fusion.1
  228.1 18.7 %all-to-all-done.2 = bf16[64,8,1152]{2,1,0:T(8,128)(2,1)S(1)} async-done(((bf16[64,8,1152]{2,1,0:T(8,128)(2,1)}), bf16[64,8,1152]{2,1,0:T(8,128)(2,1)S(1)}, u32[]{:S(2)}, u32[]{:S(2)}) %all-to-all-start.2) | async-done | bytes 1179680 | tf_op jit(solution)/shard_map/all_to_all | solution.py:280
  246.8 0.2 convert_reduce_fusion
  247.0 0.6 slice.89
  247.6 0.6 slice.88
  (29 shorter events, 0.1 us)
Async XLA Ops:
  0.6 7.3 %copy-start = (bf16[1,1,1024,1024]{3,2,1,0:T(8,128)(2,1)S(1)}, bf16[1,1,1024,1024]{3,2,1,0:T(8,128)(2,1)}, u32[]{:S(2)}) copy-start(bf16[1,1,1024,1024]{3,2,1,0:T(8,128)(2,1)} %param.10) | copy-start | bytes 6291460
  3.8 29.7 %collective-permute-start = (bf16[2,256,1024]{2,1,0:T(8,128)(2,1)}, bf16[2,256,1024]{2,1,0:T(8,128)(2,1)S(1)}, u32[]{:S(2)}, u32[]{:S(2)}) collective-permute-start(bf16[2,256,1024]{2,1,0:T(8,128)(2,1)} %bitcast.11), channel_id=1, source_target_pairs={{0,2},{2,4},{4,6},{6,0},{1,3},{3,5},{5,7},{7,1},{8,10},{10,12},{12... | collective-permute-start | bytes 3145736 | tf_op jit(solution)/shard_map/ppermute | solution.py:297
  5.8 27.8 %collective-permute-start.1 = (bf16[2,256,1024]{2,1,0:T(8,128)(2,1)}, bf16[2,256,1024]{2,1,0:T(8,128)(2,1)}, u32[]{:S(2)}, u32[]{:S(2)}) collective-permute-start(bf16[2,256,1024]{2,1,0:T(8,128)(2,1)} %bitcast.12), channel_id=1, source_target_pairs={{0,6},{2,0},{4,2},{6,4},{1,7},{3,1},{5,3},{7,5},{8,14},{10,8},{12,... | collective-permute-start | bytes 3145736 | tf_op jit(solution)/shard_map/ppermute | solution.py:298
  8.0 15.8 %collective-permute-start.2 = (bf16[4,256,1024]{2,1,0:T(8,128)(2,1)S(1)}, bf16[4,256,1024]{2,1,0:T(8,128)(2,1)}, u32[]{:S(2)}, u32[]{:S(2)}) collective-permute-start(bf16[4,256,1024]{2,1,0:T(8,128)(2,1)S(1)} %bitcast.78), channel_id=1, source_target_pairs={{0,1},{1,0},{2,3},{3,2},{4,5},{5,4},{6,7},{7,6},{8,9},{9,8},{10,11... | collective-permute-start | bytes 6291464 | tf_op jit(solution)/shard_map/ppermute | solution.py:296
  33.6 8.7 %copy-start.2 = (bf16[2,256,1024]{2,1,0:T(8,128)(2,1)}, bf16[2,256,1024]{2,1,0:T(8,128)(2,1)S(1)}, u32[]{:S(2)}) copy-start(bf16[2,256,1024]{2,1,0:T(8,128)(2,1)S(1)} %collective-permute-done.refs_0_) | copy-start | bytes 3145732
  33.6 8.5 %collective-permute-start.5 = (bf16[2,256,1024]{2,1,0:T(8,128)(2,1)S(1)}, bf16[2,256,1024]{2,1,0:T(8,128)(2,1)S(1)}, u32[]{:S(2)}, u32[]{:S(2)}) collective-permute-start(bf16[2,256,1024]{2,1,0:T(8,128)(2,1)S(1)} %collective-permute-done.refs_0_), channel_id=1, source_target_pairs={{0,1},{1,0},{2,3},{3,2},{4,5},{5,4},{6,7},{7,6},{8,9},{9,8},{10,11... | collective-permute-start | bytes 3145736 | tf_op jit(solution)/shard_map/ppermute | solution.py:296
  38.2 4.0 %collective-permute-start.6 = (bf16[2,256,1024]{2,1,0:T(8,128)(2,1)}, bf16[2,256,1024]{2,1,0:T(8,128)(2,1)S(1)}, u32[]{:S(2)}, u32[]{:S(2)}) collective-permute-start(bf16[2,256,1024]{2,1,0:T(8,128)(2,1)} %collective-permute-done.1.refs_1_), channel_id=1, source_target_pairs={{0,1},{1,0},{2,3},{3,2},{4,5},{5,4},{6,7},{7,6},{8,9},{9,8},{10,11... | collective-permute-start | bytes 3145736 | tf_op jit(solution)/shard_map/ppermute | solution.py:296
  38.3 27.1 %collective-permute-start.3 = (bf16[2,256,1024]{2,1,0:T(8,128)(2,1)}, bf16[2,256,1024]{2,1,0:T(8,128)(2,1)S(1)}, u32[]{:S(2)}, u32[]{:S(2)}) collective-permute-start(bf16[2,256,1024]{2,1,0:T(8,128)(2,1)} %bitcast.12), channel_id=1, source_target_pairs={{0,2},{2,4},{4,6},{6,0},{1,3},{3,5},{5,7},{7,1},{8,10},{10,12},{12... | collective-permute-start | bytes 3145736 | tf_op jit(solution)/shard_map/ppermute | solution.py:297
  42.1 25.4 %collective-permute-start.4 = (bf16[2,256,1024]{2,1,0:T(8,128)(2,1)}, bf16[2,256,1024]{2,1,0:T(8,128)(2,1)S(1)}, u32[]{:S(2)}, u32[]{:S(2)}) collective-permute-start(bf16[2,256,1024]{2,1,0:T(8,128)(2,1)} %bitcast.11), channel_id=1, source_target_pairs={{0,6},{2,0},{4,2},{6,4},{1,7},{3,1},{5,3},{7,5},{8,14},{10,8},{12,... | collective-permute-start | bytes 3145736 | tf_op jit(solution)/shard_map/ppermute | solution.py:298
  42.1 1.1 copy-start.8
  42.2 1.2 copy-start.11
  65.4 6.3 %copy-start.3 = (bf16[2,256,1024]{2,1,0:T(8,128)(2,1)}, bf16[2,256,1024]{2,1,0:T(8,128)(2,1)S(1)}, u32[]{:S(2)}) copy-start(bf16[2,256,1024]{2,1,0:T(8,128)(2,1)S(1)} %collective-permute-done.3.refs_0_) | copy-start | bytes 3145732
  67.5 4.2 %copy-start.5 = (bf16[2,256,1024]{2,1,0:T(8,128)(2,1)}, bf16[2,256,1024]{2,1,0:T(8,128)(2,1)S(1)}, u32[]{:S(2)}) copy-start(bf16[2,256,1024]{2,1,0:T(8,128)(2,1)S(1)} %collective-permute-done.4.refs_1_) | copy-start | bytes 3145732
  67.5 3.8 %collective-permute-start.9 = (bf16[2,256,1024]{2,1,0:T(8,128)(2,1)S(1)}, bf16[2,256,1024]{2,1,0:T(8,128)(2,1)S(1)}, u32[]{:S(2)}, u32[]{:S(2)}) collective-permute-start(bf16[2,256,1024]{2,1,0:T(8,128)(2,1)S(1)} %collective-permute-done.3.refs_0_), channel_id=1, source_target_pairs={{0,1},{1,0},{2,3},{3,2},{4,5},{5,4},{6,7},{7,6},{8,9},{9,8},{10,11... | collective-permute-start | bytes 3145736 | tf_op jit(solution)/shard_map/ppermute | solution.py:296
  67.5 4.2 %collective-permute-start.10 = (bf16[2,256,1024]{2,1,0:T(8,128)(2,1)S(1)}, bf16[2,256,1024]{2,1,0:T(8,128)(2,1)S(1)}, u32[]{:S(2)}, u32[]{:S(2)}) collective-permute-start(bf16[2,256,1024]{2,1,0:T(8,128)(2,1)S(1)} %collective-permute-done.4.refs_1_), channel_id=1, source_target_pairs={{0,1},{1,0},{2,3},{3,2},{4,5},{5,4},{6,7},{7,6},{8,9},{9,8},{10,11... | collective-permute-start | bytes 3145736 | tf_op jit(solution)/shard_map/ppermute | solution.py:296
  68.0 26.5 %collective-permute-start.7 = (bf16[2,256,1024]{2,1,0:T(8,128)(2,1)}, bf16[2,256,1024]{2,1,0:T(8,128)(2,1)S(1)}, u32[]{:S(2)}, u32[]{:S(2)}) collective-permute-start(bf16[2,256,1024]{2,1,0:T(8,128)(2,1)} %copy-done.2), channel_id=1, source_target_pairs={{0,2},{2,4},{4,6},{6,0},{1,3},{3,5},{5,7},{7,1},{8,10},{10,12},{12... | collective-permute-start | bytes 3145736 | tf_op jit(solution)/shard_map/ppermute | solution.py:297
  68.4 26.1 %collective-permute-start.8 = (bf16[2,256,1024]{2,1,0:T(8,128)(2,1)}, bf16[2,256,1024]{2,1,0:T(8,128)(2,1)S(1)}, u32[]{:S(2)}, u32[]{:S(2)}) collective-permute-start(bf16[2,256,1024]{2,1,0:T(8,128)(2,1)} %collective-permute-done.1.refs_1_), channel_id=1, source_target_pairs={{0,6},{2,0},{4,2},{6,4},{1,7},{3,1},{5,3},{7,5},{8,14},{10,8},{12,... | collective-permute-start | bytes 3145736 | tf_op jit(solution)/shard_map/ppermute | solution.py:298
  71.3 1.0 copy-start.7
  71.7 1.0 copy-start.9
  94.5 4.2 %copy-start.4 = (bf16[2,256,1024]{2,1,0:T(8,128)(2,1)}, bf16[2,256,1024]{2,1,0:T(8,128)(2,1)S(1)}, u32[]{:S(2)}) copy-start(bf16[2,256,1024]{2,1,0:T(8,128)(2,1)S(1)} %collective-permute-done.7.refs_0_) | copy-start | bytes 3145732
  94.5 4.2 %copy-start.6 = (bf16[2,256,1024]{2,1,0:T(8,128)(2,1)}, bf16[2,256,1024]{2,1,0:T(8,128)(2,1)S(1)}, u32[]{:S(2)}) copy-start(bf16[2,256,1024]{2,1,0:T(8,128)(2,1)S(1)} %collective-permute-done.8.refs_1_) | copy-start | bytes 3145732
  94.5 2.7 %collective-permute-start.11 = (bf16[2,256,1024]{2,1,0:T(8,128)(2,1)S(1)}, bf16[2,256,1024]{2,1,0:T(8,128)(2,1)S(1)}, u32[]{:S(2)}, u32[]{:S(2)}) collective-permute-start(bf16[2,256,1024]{2,1,0:T(8,128)(2,1)S(1)} %collective-permute-done.7.refs_0_), channel_id=1, source_target_pairs={{0,1},{1,0},{2,3},{3,2},{4,5},{5,4},{6,7},{7,6},{8,9},{9,8},{10,11... | collective-permute-start | bytes 3145736 | tf_op jit(solution)/shard_map/ppermute | solution.py:296
  94.6 4.1 %collective-permute-start.12 = (bf16[2,256,1024]{2,1,0:T(8,128)(2,1)S(1)}, bf16[2,256,1024]{2,1,0:T(8,128)(2,1)S(1)}, u32[]{:S(2)}, u32[]{:S(2)}) collective-permute-start(bf16[2,256,1024]{2,1,0:T(8,128)(2,1)S(1)} %collective-permute-done.8.refs_1_), channel_id=1, source_target_pairs={{0,1},{1,0},{2,3},{3,2},{4,5},{5,4},{6,7},{7,6},{8,9},{9,8},{10,11... | collective-permute-start | bytes 3145736 | tf_op jit(solution)/shard_map/ppermute | solution.py:296
  97.2 1.5 copy-start.10
  98.7 1.0 copy-start.12
  121.1 19.8 %all-to-all-start = ((bf16[16,16,1024]{2,1,0:T(8,128)(2,1)}), bf16[16,16,1024]{2,1,0:T(8,128)(2,1)S(1)}, u32[]{:S(2)}, u32[]{:S(2)}) async-start(bf16[16,16,1024]{2,1,0:T(8,128)(2,1)} %get-tuple-element.154), calls=%async_computation | async-start | bytes 1048576 | tf_op jit(solution)/shard_map/all_to_all | solution.py:447
  140.9 0.8 copy-start.1
  169.2 2.9 %collective-permute-start.13 = (bf16[512,1024]{1,0:T(8,128)(2,1)}, bf16[512,1024]{1,0:T(8,128)(2,1)S(1)}, u32[]{:S(2)}, u32[]{:S(2)}) collective-permute-start(bf16[512,1024]{1,0:T(8,128)(2,1)} %get-tuple-element.156), channel_id=1, source_target_pairs={{0,1},{1,0},{2,3},{3,2},{4,5},{5,4},{6,7},{7,6},{8,9},{9,8},{10,11... | collective-permute-start | bytes 3145736 | tf_op jit(solution)/shard_map/ppermute | solution.py:274
  193.1 10.3 %collective-permute-start.14 = (bf16[512,1152]{1,0:T(8,128)(2,1)}, bf16[512,1152]{1,0:T(8,128)(2,1)S(1)}, u32[]{:S(2)}, u32[]{:S(2)}) collective-permute-start(bf16[512,1152]{1,0:T(8,128)(2,1)} %get-tuple-element.159), channel_id=1, source_target_pairs={{0,1},{1,0},{2,3},{3,2},{4,5},{5,4},{6,7},{7,6},{8,9},{9,8},{10,11... | collective-permute-start | bytes 3538952 | tf_op jit(solution)/shard_map/ppermute | solution.py:274
  193.5 29.2 %all-to-all-start.3 = ((bf16[64,8,1024]{2,1,0:T(8,128)(2,1)}), bf16[64,8,1024]{2,1,0:T(8,128)(2,1)S(1)}, u32[]{:S(2)}, u32[]{:S(2)}) async-start(bf16[64,8,1024]{2,1,0:T(8,128)(2,1)} %fusion.1), calls=%async_computation.3 | async-start | bytes 2097152 | tf_op jit(solution)/shard_map/all_to_all | solution.py:280
  222.6 24.2 %all-to-all-start.2 = ((bf16[64,8,1152]{2,1,0:T(8,128)(2,1)}), bf16[64,8,1152]{2,1,0:T(8,128)(2,1)S(1)}, u32[]{:S(2)}, u32[]{:S(2)}) async-start(bf16[64,8,1152]{2,1,0:T(8,128)(2,1)} %fusion), calls=%async_computation.2 | async-start | bytes 2359296 | tf_op jit(solution)/shard_map/all_to_all | solution.py:280
where the time goes:
time: 248 us
  Pallas kernels  111 us (45%)
  waiting for transfers between devices  62.3 us (25%)
  starting transfers between devices  41.6 us (17%)
  blocking collectives  12.9 us (5%)
  local copies, waits for them, and re-layouts  10.2 us (4%)
  other arithmetic  9.09 us (4%)
    pallas_call x4, Pallas kernels, on_device(): pl.pallas_call(body, out_shape=(shape((room, D), BF16), shape((room, D),...  60.2 us
    all_to_all x2, waiting for transfers between devices, over_chips(): return lax.all_to_all(half, CHIPS, 0, 0).astype(F32).sum(0)  35 us
    pallas_call x1, Pallas kernels, on_device(): call(gradient_kernel, 'gradient', (shape((D // 2, wide), F32), shape((D /...  18.1 us
    all_to_all x2, starting transfers between devices, over_chips(): return lax.all_to_all(half, CHIPS, 0, 0).astype(F32).sum(0)  14.6 us
    all_to_all x1, blocking collectives, on_device(): enter = lax.all_to_all(entering, TM, 0, 0).reshape(128, D)  12.9 us
    pallas_call x1, Pallas kernels, on_device(): call(readout_kernel, 'readout', (shape((D // 2, D), F32), shape((D // 2,...  12.6 us
    pallas_call x1, Pallas kernels, on_device(): call(upstream_kernel, 'upstream', (shape((steps, D), BF16), shape((32, st...  11.6 us
    all_to_all x1, waiting for transfers between devices, on_device(): terms = lax.all_to_all(total, TM, 0, 0)  10.1 us
  transfers between devices with their start and end apart: 18, of which 11 were waited for; matrix products, arithmetic and copies ran while one was open for 3% of the time, Pallas kernels for 23%

commit v1 on v0

--- a/solution.py
+++ b/solution.py
@@ -161,15 +161,18 @@
     def _():
         table = ends[...].reshape(factors.shape[0], 128)
         factors[...] = spread(table, OPEN, spread_matrix())
-        state[...] = jnp.zeros_like(state)
-
-    factor = factors[pl.ds(b * 8, 8)]
-    before = jnp.where(b == 0, 1.0, state[128:])
-    starts[0] = state[:64]
-    gains[0] = jnp.concatenate([factor, before], axis=0)
-    state[:64] = state[:64] * factor[:1] + push_in[0]
-    state[64:128] = state[64:128] + before[:1] * push_out[0]
-    state[128:] = before * factor
+        state[:128] = jnp.zeros((128, D), F32)
+        state[128:] = jnp.ones((8, D), F32)
+
+    each = starts.shape[0]
+    for n in range(each):
+        factor = factors[pl.ds((b * each + n) * 8, 8)]
+        before = state[128:]
+        starts[n] = state[:64]
+        gains[n] = jnp.concatenate([factor, before], axis=0)
+        state[:64] = state[:64] * factor[:1] + push_in[n]
+        state[64:128] = state[64:128] + before[:1] * push_out[n]
+        state[128:] = before * factor
 
     @pl.when(b == pl.num_programs(0) - 1)
     def _():
@@ -351,13 +354,13 @@
     made = None
     for s in range(4):
         if s == 0:
-            sources = (mine, other)
-        elif s == 1:
-            below_a, above_a, second, first, made = lax.optimization_barrier(
-                (below_a, above_a, second, first, made)
+            below_a, above_a, second, first, up = lax.optimization_barrier(
+                (below_a, above_a, second, first, up)
             )
             below_b, above_b = up_z(second), down_z(first)
-            sources = (below_a, above_a, swap(below_a), swap(above_a))
+            sources, later = (mine, other), (below_a, above_a, swap(below_a), swap(above_a))
+        elif s == 1:
+            sources = later
         elif s == 2:
             below_b, above_b, below_a, above_a, made = lax.optimization_barrier(
                 (below_b, above_b, below_a, above_a, made)
@@ -430,14 +433,15 @@
         )(block[s], source[s], index[s], fill, counts[s : s + 1], *sources, w_in, w_bc, up, rows, cols, *kept)
     taken, inner, keys, ro, gi, pair, push_in, push_out = made
 
+    some = lambda *dims: pl.BlockSpec((blocks // 2, *dims), lambda b, *_: (b, 0, 0))
     starts, gains, total = call(
         local_kernel,
         "local",
         (shape((blocks, STATE, D), F32), shape((blocks, 16, D), F32), shape((shards, 16, D), BF16)),
         pl.GridSpec(
-            grid=(blocks,),
-            in_specs=[lead(STATE, D), lead(STATE, D), whole(blocks, 8, 128)],
-            out_specs=[lead(STATE, D), lead(16, D), whole(shards, 16, D)],
+            grid=(2,),
+            in_specs=[some(STATE, D), some(STATE, D), whole(blocks, 8, 128)],
+            out_specs=[some(STATE, D), some(16, D), whole(shards, 16, D)],
             scratch_shapes=[vmem(F32, blocks * 8, D), vmem(F32, 136, D)],
         ),
         1 << 24,
@@ -532,7 +536,9 @@
         26 << 20,
     )(own_core, taken, inner, up, keys, cols, gi, pair, starts, push_out, gains, enter)
 
-    grad_out = over_chips(half_out)
+    got_out = lax.all_to_all(half_out, CHIPS, 0, 0)
+    got_out, keep_in, give_in = lax.optimization_barrier((got_out, keep_in, give_in))
+    grad_out = got_out.astype(F32).sum(0)
     grad_in = over_chips(over_chip(keep_in, give_in))
     return (grad_in[:, :D], grad_in[:, D:], grad_out)
 

time: 248 us -> 246 us (level); the launches traced: 248 us -> 243 us
  starting transfers between devices: 41.6 us -> 35.5 us
  waiting for transfers between devices: 62.3 us -> 65.9 us
  Pallas kernels: 111 us -> 108 us
    all_to_all x2 -> x1, waiting for transfers between devices: 35 us -> 19.6 us  [over_chips(): return lax.all_to_all(half, CHIPS, 0, 0).astype(F32).sum(0)]
    ppermute x3, waiting for transfers between devices: 8.01 us -> 23.2 us  [on_device(): up_z = lambda v: lax.ppermute(v, 'z', ring('z', 1))]
    all_to_all x2 -> x1, starting transfers between devices: 14.6 us -> 9.22 us  [over_chips(): return lax.all_to_all(half, CHIPS, 0, 0).astype(F32).sum(0)]
    all_to_all x0 -> x1, starting transfers between devices: none -> 4.65 us  [on_device(): got_out = lax.all_to_all(half_out, CHIPS, 0, 0)]
    ppermute x7, starting transfers between devices: 5.84 us -> 1.67 us  [on_device(): swap = lambda v: lax.ppermute(v, 'c', ring('c', 1))]
    ppermute x2, waiting for transfers between devices: 2.87 us -> 5.92 us  [over_chip(): got = lax.ppermute(give, 'c', ring('c', 1))]
    pallas_call x1, Pallas kernels: 6.88 us -> 3.87 us  [on_device(): call(local_kernel, 'local', (shape((blocks, STATE, D), F32), shape((block...]
  transfers between devices with their start and end apart: 18 -> 18, of which waited for: 11 -> 10; matrix products, arithmetic and copies ran while one was open for 3% -> 2% of each run, Pallas kernels for 23% -> 29%
where the time goes in v1:
time: 246 us; the launch traced here: 243 us
  Pallas kernels  108 us (44%)
  waiting for transfers between devices  65.9 us (27%)
  starting transfers between devices  35.5 us (14%)
  blocking collectives  12.9 us (5%)
  local copies, waits for them, and re-layouts  10.4 us (4%)
  other arithmetic  9.13 us (4%)
    pallas_call x4, Pallas kernels, on_device(): pl.pallas_call(body, out_shape=(shape((room, D), BF16), shape((room, D),...  60.2 us
    ppermute x3, waiting for transfers between devices, on_device(): up_z = lambda v: lax.ppermute(v, 'z', ring('z', 1))  23.2 us
    all_to_all x1, waiting for transfers between devices, over_chips(): return lax.all_to_all(half, CHIPS, 0, 0).astype(F32).sum(0)  19.6 us
    pallas_call x1, Pallas kernels, on_device(): call(gradient_kernel, 'gradient', (shape((D // 2, wide), F32), shape((D /...  18.1 us
    all_to_all x1, blocking collectives, on_device(): enter = lax.all_to_all(entering, TM, 0, 0).reshape(128, D)  12.9 us
    pallas_call x1, Pallas kernels, on_device(): call(readout_kernel, 'readout', (shape((D // 2, D), F32), shape((D // 2,...  12.5 us
    all_to_all x1, waiting for transfers between devices, on_device(): terms = lax.all_to_all(total, TM, 0, 0)  11.9 us
    pallas_call x1, Pallas kernels, on_device(): call(upstream_kernel, 'upstream', (shape((steps, D), BF16), shape((32, st...  11.6 us
  transfers between devices with their start and end apart: 18, of which 10 were waited for; matrix products, arithmetic and copies ran while one was open for 2% of the time, Pallas kernels for 29%

profile of v1, /device:TPU:0, one launch (start us, length us, event | category | flops | bytes accessed | tf_op | source)
XLA Modules:
  0.0 243.0 jit_solution(13238780545645722453)
XLA Ops:
  0.6 0.0 copy-start
  0.6 3.2 %fusion.14 = (bf16[1,1,512,1024]{3,2,1,0:T(8,128)(2,1)}, bf16[1,1,512,1024]{3,2,1,0:T(8,128)(2,1)}) fusion(bf16[1,1,1024,1024]{3,2,1,0:T(8,128)(2,1)} %param.10), kind=kLoop, calls=%fused_computation.76 | loop fusion | bytes 4194304 | tf_op jit(solution)/shard_map/slice | solution.py:302
  3.8 2.0 collective-permute-start
  5.8 2.1 collective-permute-start.1
  7.9 0.0 collective-permute-start.6
  7.9 0.7 fusion.13
  8.7 0.7 compare_select_fusion.8
  9.3 0.1 convert_reduce_fusion.3
  9.5 0.1 iota_minimum_fusion
  9.6 0.2 convert_reduce_fusion.2
  9.7 0.4 select_reduce_fusion
  10.1 0.1 broadcast_select_fusion
  10.2 11.6 %upstream.1 = (bf16[2048,1024]{1,0:T(8,128)(2,1)}, f32[32,2048]{1,0:T(8,128)}, f32[2048,128]{1,0:T(8,128)}, f32[8,8,128]{2,1,0:T(8,128)}) custom-call(s32[8]{0:T(128)} %bitcast.81, f32[16,2048]{1,0:T(8,128)} %bitcast.87, s32[8,1,256]{2,1,0:T(1,128)} %bitcast.88, bf16[1,2048,1024]{2,1,0:T(8,128)(2,1)} %cot.3, bf16[1024,1024]{1,0:T(8,128)(2,1)} %w_out.1), custom_call_target="tpu_custom_call" | custom-call | flops 4294967296 | bytes 12582912 | tf_op jit(solution)/shard_map/upstream/pallas_call | solution.py:329
  21.8 9.5 %collective-permute-done.refs_0_ = bf16[2,256,1024]{2,1,0:T(8,128)(2,1)S(1)} collective-permute-done((bf16[2,256,1024]{2,1,0:T(8,128)(2,1)}, bf16[2,256,1024]{2,1,0:T(8,128)(2,1)S(1)}, u32[]{:S(2)}, u32[]{:S(2)}) %collective-permute-start) | collective-permute-done | bytes 1048608 | tf_op jit(solution)/shard_map/ppermute | solution.py:300
  31.3 0.5 collective-permute-start.5
  31.8 0.6 slice_bitcast_fusion.2
  32.4 0.6 slice_bitcast_fusion
  33.0 1.4 collective-permute-start.2
  34.4 1.9 collective-permute-start.3
  36.3 0.7 fusion.15
  37.0 0.0 collective-permute-done.6.refs_1_
  37.0 13.8 %stage_0.1 = (bf16[2304,1024]{1,0:T(8,128)(2,1)}, bf16[2304,1024]{1,0:T(8,128)(2,1)}, bf16[2304,128]{1,0:T(8,128)(2,1)}, bf16[2304,1024]{1,0:T(8,128)(2,1)}, bf1...) custom-call(s32[8]{0:T(128)} %get-tuple-element.170.block, ...), custom_call_target="tpu_custom_call" | custom-call | flops 5368709120 | bytes 16777216 | tf_op jit(solution)/shard_map/stage_0/pallas_call | solution.py:389
  50.8 0.0 collective-permute-done.5.refs_3_
  50.8 1.1 copy-done.9
  51.9 0.3 copy-done.8
  52.2 19.9 %stage_1.1 = (bf16[2304,1024]{1,0:T(8,128)(2,1)}, bf16[2304,1024]{1,0:T(8,128)(2,1)}, bf16[2304,128]{1,0:T(8,128)(2,1)}, bf16[2304,1024]{1,0:T(8,128)(2,1)}, bf1...) custom-call(s32[8]{0:T(128)} %get-tuple-element.171.block, ...), custom_call_target="tpu_custom_call", output_to_operand_aliasing={{0}: (14, {}), {1}: (15, {}), {2}: (16, {}), {3}: (17, {}),... | custom-call | flops 5368709120 | bytes 16777216 | tf_op jit(solution)/shard_map/stage_1/pallas_call | solution.py:389
  72.1 0.0 collective-permute-done.2.refs_0_
  72.1 0.0 collective-permute-done.3.refs_1_
  72.1 0.1 collective-permute-start.9
  72.2 0.5 collective-permute-start.10
  72.7 0.3 collective-permute-start.7
  73.0 3.0 %collective-permute-start.8 = (bf16[2,256,1024]{2,1,0:T(8,128)(2,1)}, bf16[2,256,1024]{2,1,0:T(8,128)(2,1)S(1)}, u32[]{:S(2)}, u32[]{:S(2)}) collective-permute-start(bf16[2,256,1024]{2,1,0:T(8,128)(2,1)} %collective-permute-done.1.refs_1_), channel_id=1, source_target_pairs={{0,6},{2,0},{4,2},{6,4},{1,7},{3,1},{5,3},{7,5},{8,14},{10,8},{12,... | collective-permute-start | bytes 3145736 | tf_op jit(solution)/shard_map/ppermute | solution.py:301
  75.9 0.0 collective-permute-done.9.refs_2_
  75.9 0.4 collective-permute-done.10.refs_3_
  76.3 0.6 copy-done.10
  76.9 0.5 copy-done.11
  77.4 7.9 %stage_2.1 = (bf16[2304,1024]{1,0:T(8,128)(2,1)}, bf16[2304,1024]{1,0:T(8,128)(2,1)}, bf16[2304,128]{1,0:T(8,128)(2,1)}, bf16[2304,1024]{1,0:T(8,128)(2,1)}, bf1...) custom-call(s32[8]{0:T(128)} %get-tuple-element.169.block, ...), custom_call_target="tpu_custom_call", output_to_operand_aliasing={{0}: (14, {}), {1}: (15, {}), {2}: (16, {}), {3}: (17, {}),... | custom-call | flops 5368709120 | bytes 16777216 | tf_op jit(solution)/shard_map/stage_2/pallas_call | solution.py:389
  85.3 13.8 %collective-permute-done.7.refs_0_ = bf16[2,256,1024]{2,1,0:T(8,128)(2,1)S(1)} collective-permute-done((bf16[2,256,1024]{2,1,0:T(8,128)(2,1)S(1)}, bf16[2,256,1024]{2,1,0:T(8,128)(2,1)S(1)}, u32[]{:S(2)}, u32[]{:S(2)}) %collective-permute-start.7) | collective-permute-done | bytes 1048608 | tf_op jit(solution)/shard_map/ppermute | solution.py:300
  99.1 0.1 collective-permute-start.11
  99.2 0.5 collective-permute-start.12
  99.7 2.1 collective-permute-done.11.refs_2_
  101.8 1.5 collective-permute-done.12.refs_3_
  103.3 1.0 copy-done.13
  104.3 18.6 %stage_3.1 = (bf16[2304,1024]{1,0:T(8,128)(2,1)}, bf16[2304,1024]{1,0:T(8,128)(2,1)}, bf16[2304,128]{1,0:T(8,128)(2,1)}, bf16[2304,1024]{1,0:T(8,128)(2,1)}, bf1...) custom-call(s32[8]{0:T(128)} %get-tuple-element.172.block, ...), custom_call_target="tpu_custom_call", output_to_operand_aliasing={{0}: (14, {}), {1}: (15, {}), {2}: (16, {}), {3}: (17, {}),... | custom-call | flops 5368709120 | bytes 16777216 | tf_op jit(solution)/shard_map/stage_3/pallas_call | solution.py:389
  122.9 3.9 %local.1 = (f32[8,64,1024]{2,1,0:T(8,128)}, f32[8,16,1024]{2,1,0:T(8,128)}, bf16[16,16,1024]{2,1,0:T(8,128)(2,1)}) custom-call(f32[9,64,1024]{2,1,0:T(8,128)} %get-tuple-element.134.push_in, f32[9,64,1024]{2,1,0:T(8,128)} %get-tuple-element.135.push_out, f32[8,8,128]{2,1,0:T(8,128)} %get-tuple-element.136.ends), custom_call_target="tpu_custom_call" | custom-call | flops 16777216 | bytes 7340032 | tf_op jit(solution)/shard_map/local/pallas_call | solution.py:437
  126.7 9.3 %all-to-all-start = ((bf16[16,16,1024]{2,1,0:T(8,128)(2,1)}), bf16[16,16,1024]{2,1,0:T(8,128)(2,1)S(1)}, u32[]{:S(2)}, u32[]{:S(2)}) async-start(bf16[16,16,1024]{2,1,0:T(8,128)(2,1)} %get-tuple-element.139), calls=%async_computation | async-start | bytes 1048576 | tf_op jit(solution)/shard_map/all_to_all | solution.py:451
  136.1 11.9 %all-to-all-done.terms = bf16[16,16,1024]{2,1,0:T(8,128)(2,1)S(1)} async-done(((bf16[16,16,1024]{2,1,0:T(8,128)(2,1)}), bf16[16,16,1024]{2,1,0:T(8,128)(2,1)S(1)}, u32[]{:S(2)}, u32[]{:S(2)}) %all-to-all-start) | async-done | bytes 524320 | tf_op jit(solution)/shard_map/all_to_all | solution.py:451
  148.0 0.8 copy-done.1
  148.8 2.0 scan.1
  150.8 12.9 %all_to_all.20 = bf16[16,8,1024]{2,1,0:T(8,128)(2,1)} all-to-all(bf16[16,8,1024]{2,1,0:T(8,128)(2,1)} %scan.1), channel_id=1, replica_groups=mesh['y'=4,'x'=4,'z'=4,'c'=2] {'y','x'}, dimensions={0} | all-to-all | bytes 524288 | tf_op jit(solution)/shard_map/all_to_all | solution.py:466
  163.6 12.5 %readout.1 = (f32[512,1024]{1,0:T(8,128)}, bf16[512,1024]{1,0:T(8,128)(2,1)}) custom-call(s32[1]{0:T(128)} %bitcast.core, s32[8]{0:T(128)} %bitcast.86, bf16[1,2048,1024]{2,1,0:T(8,128)(2,1)} %cot.3, bf16[2304,128]{1,0:T(8,128)(2,1)} %get-tuple-element.132.keys, f32[2048,128]{1,0:T(8,128)} %get-tuple-element.85.refs_6_.refs_8_.cols, ...), custom_call_target="tpu_custom_call" | custom-call | flops 5368709120 | bytes 14680064 | tf_op jit(solution)/shard_map/readout/pallas_call | solution.py:471
  176.2 2.9 %collective-permute-done.13 = bf16[512,1024]{1,0:T(8,128)(2,1)S(1)} collective-permute-done((bf16[512,1024]{1,0:T(8,128)(2,1)}, bf16[512,1024]{1,0:T(8,128)(2,1)S(1)}, u32[]{:S(2)}, u32[]{:S(2)}) %collective-permute-start.13) | collective-permute-done | bytes 1048608 | tf_op jit(solution)/shard_map/ppermute | solution.py:277
  179.1 3.0 %fusion.1 = bf16[64,8,1024]{2,1,0:T(8,128)(2,1)} fusion(f32[512,1024]{1,0:T(8,128)} %get-tuple-element.140, bf16[512,1024]{1,0:T(8,128)(2,1)S(1)} %collective-permute-done.13), kind=kLoop, calls=%fused_computation.5 | loop fusion | flops 1572864 | bytes 4194304 | tf_op jit(solution)/shard_map/reshape | solution.py:279
  182.0 4.7 %all-to-all-start.2 = ((bf16[64,8,1024]{2,1,0:T(8,128)(2,1)}), bf16[64,8,1024]{2,1,0:T(8,128)(2,1)S(1)}, u32[]{:S(2)}, u32[]{:S(2)}) async-start(bf16[64,8,1024]{2,1,0:T(8,128)(2,1)} %fusion.1), calls=%async_computation.2 | async-start | bytes 2097152 | tf_op jit(solution)/shard_map/all_to_all | solution.py:539
  186.7 18.1 %gradient.1 = (f32[512,1152]{1,0:T(8,128)}, bf16[512,1152]{1,0:T(8,128)(2,1)}) custom-call(s32[1]{0:T(128)} %bitcast.core, bf16[2304,1024]{1,0:T(8,128)(2,1)} %get-tuple-element.143.taken, bf16[2304,1024]{1,0:T(8,128)(2,1)} %get-tuple-element.144.inner, bf16[2048,1024]{1,0:T(8,128)(2,1)} %get-tuple-element.83.refs_4_.refs_6_.up, ...), custom_call_target="tpu_custom_call" | custom-call | flops 8589934592 | bytes 27262976 | tf_op jit(solution)/shard_map/gradient/pallas_call | solution.py:504
  204.8 1.2 all-to-all-done.2
  206.0 3.1 %collective-permute-done.14 = bf16[512,1152]{1,0:T(8,128)(2,1)S(1)} collective-permute-done((bf16[512,1152]{1,0:T(8,128)(2,1)}, bf16[512,1152]{1,0:T(8,128)(2,1)S(1)}, u32[]{:S(2)}, u32[]{:S(2)}) %collective-permute-start.14) | collective-permute-done | bytes 1179680 | tf_op jit(solution)/shard_map/ppermute | solution.py:277
  209.0 3.0 %fusion = bf16[64,8,1152]{2,1,0:T(8,128)(2,1)} fusion(f32[512,1152]{1,0:T(8,128)} %get-tuple-element.150, bf16[512,1152]{1,0:T(8,128)(2,1)S(1)} %collective-permute-done.14), kind=kLoop, calls=%fused_computation.4 | loop fusion | flops 1769472 | bytes 4718592 | tf_op jit(solution)/shard_map/reshape | solution.py:279
  212.0 9.2 %all-to-all-start.3 = ((bf16[64,8,1152]{2,1,0:T(8,128)(2,1)}), bf16[64,8,1152]{2,1,0:T(8,128)(2,1)S(1)}, u32[]{:S(2)}, u32[]{:S(2)}) async-start(bf16[64,8,1152]{2,1,0:T(8,128)(2,1)} %fusion), calls=%async_computation.3 | async-start | bytes 2359296 | tf_op jit(solution)/shard_map/all_to_all | solution.py:283
  221.2 0.8 convert_reduce_fusion.1
  222.0 19.6 %all-to-all-done.3 = bf16[64,8,1152]{2,1,0:T(8,128)(2,1)S(1)} async-done(((bf16[64,8,1152]{2,1,0:T(8,128)(2,1)}), bf16[64,8,1152]{2,1,0:T(8,128)(2,1)S(1)}, u32[]{:S(2)}, u32[]{:S(2)}) %all-to-all-start.3) | async-done | bytes 1179680 | tf_op jit(solution)/shard_map/all_to_all | solution.py:283
  241.6 0.2 convert_reduce_fusion
  241.8 0.6 slice.89
  242.4 0.6 slice.88
  (31 shorter events, 0.1 us)
Async XLA Ops:
  0.6 7.3 %copy-start = (bf16[1,1,1024,1024]{3,2,1,0:T(8,128)(2,1)S(1)}, bf16[1,1,1024,1024]{3,2,1,0:T(8,128)(2,1)}, u32[]{:S(2)}) copy-start(bf16[1,1,1024,1024]{3,2,1,0:T(8,128)(2,1)} %param.10) | copy-start | bytes 6291460
  3.8 27.5 %collective-permute-start = (bf16[2,256,1024]{2,1,0:T(8,128)(2,1)}, bf16[2,256,1024]{2,1,0:T(8,128)(2,1)S(1)}, u32[]{:S(2)}, u32[]{:S(2)}) collective-permute-start(bf16[2,256,1024]{2,1,0:T(8,128)(2,1)} %bitcast.11), channel_id=1, source_target_pairs={{0,2},{2,4},{4,6},{6,0},{1,3},{3,5},{5,7},{7,1},{8,10},{10,12},{12... | collective-permute-start | bytes 3145736 | tf_op jit(solution)/shard_map/ppermute | solution.py:300
  5.8 25.5 %collective-permute-start.1 = (bf16[2,256,1024]{2,1,0:T(8,128)(2,1)}, bf16[2,256,1024]{2,1,0:T(8,128)(2,1)}, u32[]{:S(2)}, u32[]{:S(2)}) collective-permute-start(bf16[2,256,1024]{2,1,0:T(8,128)(2,1)} %bitcast.12), channel_id=1, source_target_pairs={{0,6},{2,0},{4,2},{6,4},{1,7},{3,1},{5,3},{7,5},{8,14},{10,8},{12,... | collective-permute-start | bytes 3145736 | tf_op jit(solution)/shard_map/ppermute | solution.py:301
  7.9 29.0 %collective-permute-start.6 = (bf16[4,256,1024]{2,1,0:T(8,128)(2,1)S(1)}, bf16[4,256,1024]{2,1,0:T(8,128)(2,1)}, u32[]{:S(2)}, u32[]{:S(2)}) collective-permute-start(bf16[4,256,1024]{2,1,0:T(8,128)(2,1)S(1)} %bitcast.78), channel_id=1, source_target_pairs={{0,1},{1,0},{2,3},{3,2},{4,5},{5,4},{6,7},{7,6},{8,9},{9,8},{10,11... | collective-permute-start | bytes 6291464 | tf_op jit(solution)/shard_map/ppermute | solution.py:299
  31.3 19.5 %copy-start.2 = (bf16[2,256,1024]{2,1,0:T(8,128)(2,1)}, bf16[2,256,1024]{2,1,0:T(8,128)(2,1)S(1)}, u32[]{:S(2)}) copy-start(bf16[2,256,1024]{2,1,0:T(8,128)(2,1)S(1)} %collective-permute-done.refs_0_) | copy-start | bytes 3145732
  31.3 19.5 %collective-permute-start.4 = (bf16[2,256,1024]{2,1,0:T(8,128)(2,1)S(1)}, bf16[2,256,1024]{2,1,0:T(8,128)(2,1)S(1)}, u32[]{:S(2)}, u32[]{:S(2)}) collective-permute-start(bf16[2,256,1024]{2,1,0:T(8,128)(2,1)S(1)} %collective-permute-done.refs_0_), channel_id=1, source_target_pairs={{0,1},{1,0},{2,3},{3,2},{4,5},{5,4},{6,7},{7,6},{8,9},{9,8},{10,11... | collective-permute-start | bytes 3145736 | tf_op jit(solution)/shard_map/ppermute | solution.py:299
  31.3 19.5 %collective-permute-start.5 = (bf16[2,256,1024]{2,1,0:T(8,128)(2,1)}, bf16[2,256,1024]{2,1,0:T(8,128)(2,1)S(1)}, u32[]{:S(2)}, u32[]{:S(2)}) collective-permute-start(bf16[2,256,1024]{2,1,0:T(8,128)(2,1)} %collective-permute-done.1.refs_1_), channel_id=1, source_target_pairs={{0,1},{1,0},{2,3},{3,2},{4,5},{5,4},{6,7},{7,6},{8,9},{9,8},{10,11... | collective-permute-start | bytes 3145736 | tf_op jit(solution)/shard_map/ppermute | solution.py:299
  33.0 39.1 %collective-permute-start.2 = (bf16[2,256,1024]{2,1,0:T(8,128)(2,1)}, bf16[2,256,1024]{2,1,0:T(8,128)(2,1)S(1)}, u32[]{:S(2)}, u32[]{:S(2)}) collective-permute-start(bf16[2,256,1024]{2,1,0:T(8,128)(2,1)} %bitcast.12), channel_id=1, source_target_pairs={{0,2},{2,4},{4,6},{6,0},{1,3},{3,5},{5,7},{7,1},{8,10},{10,12},{12... | collective-permute-start | bytes 3145736 | tf_op jit(solution)/shard_map/ppermute | solution.py:300
  34.4 37.7 %collective-permute-start.3 = (bf16[2,256,1024]{2,1,0:T(8,128)(2,1)}, bf16[2,256,1024]{2,1,0:T(8,128)(2,1)S(1)}, u32[]{:S(2)}, u32[]{:S(2)}) collective-permute-start(bf16[2,256,1024]{2,1,0:T(8,128)(2,1)} %bitcast.11), channel_id=1, source_target_pairs={{0,6},{2,0},{4,2},{6,4},{1,7},{3,1},{5,3},{7,5},{8,14},{10,8},{12,... | collective-permute-start | bytes 3145736 | tf_op jit(solution)/shard_map/ppermute | solution.py:301
  50.8 1.4 copy-start.8
  50.8 1.1 copy-start.9
  52.2 20.5 %copy-start.3 = (bf16[2,256,1024]{2,1,0:T(8,128)(2,1)S(1)}, bf16[2,256,1024]{2,1,0:T(8,128)(2,1)}, u32[]{:S(2)}) copy-start(bf16[2,256,1024]{2,1,0:T(8,128)(2,1)} %copy-done.2) | copy-start | bytes 3145732
  72.1 4.3 %copy-start.4 = (bf16[2,256,1024]{2,1,0:T(8,128)(2,1)}, bf16[2,256,1024]{2,1,0:T(8,128)(2,1)S(1)}, u32[]{:S(2)}) copy-start(bf16[2,256,1024]{2,1,0:T(8,128)(2,1)S(1)} %collective-permute-done.2.refs_0_) | copy-start | bytes 3145732
  72.1 4.3 %copy-start.5 = (bf16[2,256,1024]{2,1,0:T(8,128)(2,1)}, bf16[2,256,1024]{2,1,0:T(8,128)(2,1)S(1)}, u32[]{:S(2)}) copy-start(bf16[2,256,1024]{2,1,0:T(8,128)(2,1)S(1)} %collective-permute-done.3.refs_1_) | copy-start | bytes 3145732
  72.1 3.8 %collective-permute-start.9 = (bf16[2,256,1024]{2,1,0:T(8,128)(2,1)S(1)}, bf16[2,256,1024]{2,1,0:T(8,128)(2,1)S(1)}, u32[]{:S(2)}, u32[]{:S(2)}) collective-permute-start(bf16[2,256,1024]{2,1,0:T(8,128)(2,1)S(1)} %collective-permute-done.2.refs_0_), channel_id=1, source_target_pairs={{0,1},{1,0},{2,3},{3,2},{4,5},{5,4},{6,7},{7,6},{8,9},{9,8},{10,11... | collective-permute-start | bytes 3145736 | tf_op jit(solution)/shard_map/ppermute | solution.py:299
  72.2 4.1 %collective-permute-start.10 = (bf16[2,256,1024]{2,1,0:T(8,128)(2,1)S(1)}, bf16[2,256,1024]{2,1,0:T(8,128)(2,1)S(1)}, u32[]{:S(2)}, u32[]{:S(2)}) collective-permute-start(bf16[2,256,1024]{2,1,0:T(8,128)(2,1)S(1)} %collective-permute-done.3.refs_1_), channel_id=1, source_target_pairs={{0,1},{1,0},{2,3},{3,2},{4,5},{5,4},{6,7},{7,6},{8,9},{9,8},{10,11... | collective-permute-start | bytes 3145736 | tf_op jit(solution)/shard_map/ppermute | solution.py:299
  72.7 26.4 %collective-permute-start.7 = (bf16[2,256,1024]{2,1,0:T(8,128)(2,1)S(1)}, bf16[2,256,1024]{2,1,0:T(8,128)(2,1)S(1)}, u32[]{:S(2)}, u32[]{:S(2)}) collective-permute-start(bf16[2,256,1024]{2,1,0:T(8,128)(2,1)S(1)} %copy-done.3), channel_id=1, source_target_pairs={{0,2},{2,4},{4,6},{6,0},{1,3},{3,5},{5,7},{7,1},{8,10},{10,12},{12... | collective-permute-start | bytes 3145736 | tf_op jit(solution)/shard_map/ppermute | solution.py:300
  73.0 26.1 %collective-permute-start.8 = (bf16[2,256,1024]{2,1,0:T(8,128)(2,1)}, bf16[2,256,1024]{2,1,0:T(8,128)(2,1)S(1)}, u32[]{:S(2)}, u32[]{:S(2)}) collective-permute-start(bf16[2,256,1024]{2,1,0:T(8,128)(2,1)} %collective-permute-done.1.refs_1_), channel_id=1, source_target_pairs={{0,6},{2,0},{4,2},{6,4},{1,7},{3,1},{5,3},{7,5},{8,14},{10,8},{12,... | collective-permute-start | bytes 3145736 | tf_op jit(solution)/shard_map/ppermute | solution.py:301
  75.9 1.0 copy-start.10
  76.3 1.0 copy-start.11
  99.1 4.2 %copy-start.6 = (bf16[2,256,1024]{2,1,0:T(8,128)(2,1)}, bf16[2,256,1024]{2,1,0:T(8,128)(2,1)S(1)}, u32[]{:S(2)}) copy-start(bf16[2,256,1024]{2,1,0:T(8,128)(2,1)S(1)} %collective-permute-done.7.refs_0_) | copy-start | bytes 3145732
  99.1 4.2 %copy-start.7 = (bf16[2,256,1024]{2,1,0:T(8,128)(2,1)}, bf16[2,256,1024]{2,1,0:T(8,128)(2,1)S(1)}, u32[]{:S(2)}) copy-start(bf16[2,256,1024]{2,1,0:T(8,128)(2,1)S(1)} %collective-permute-done.8.refs_1_) | copy-start | bytes 3145732
  99.1 2.7 %collective-permute-start.11 = (bf16[2,256,1024]{2,1,0:T(8,128)(2,1)S(1)}, bf16[2,256,1024]{2,1,0:T(8,128)(2,1)S(1)}, u32[]{:S(2)}, u32[]{:S(2)}) collective-permute-start(bf16[2,256,1024]{2,1,0:T(8,128)(2,1)S(1)} %collective-permute-done.7.refs_0_), channel_id=1, source_target_pairs={{0,1},{1,0},{2,3},{3,2},{4,5},{5,4},{6,7},{7,6},{8,9},{9,8},{10,11... | collective-permute-start | bytes 3145736 | tf_op jit(solution)/shard_map/ppermute | solution.py:299
  99.2 4.1 %collective-permute-start.12 = (bf16[2,256,1024]{2,1,0:T(8,128)(2,1)S(1)}, bf16[2,256,1024]{2,1,0:T(8,128)(2,1)S(1)}, u32[]{:S(2)}, u32[]{:S(2)}) collective-permute-start(bf16[2,256,1024]{2,1,0:T(8,128)(2,1)S(1)} %collective-permute-done.8.refs_1_), channel_id=1, source_target_pairs={{0,1},{1,0},{2,3},{3,2},{4,5},{5,4},{6,7},{7,6},{8,9},{9,8},{10,11... | collective-permute-start | bytes 3145736 | tf_op jit(solution)/shard_map/ppermute | solution.py:299
  101.8 1.5 copy-start.12
  103.3 1.0 copy-start.13
  126.7 21.2 %all-to-all-start = ((bf16[16,16,1024]{2,1,0:T(8,128)(2,1)}), bf16[16,16,1024]{2,1,0:T(8,128)(2,1)S(1)}, u32[]{:S(2)}, u32[]{:S(2)}) async-start(bf16[16,16,1024]{2,1,0:T(8,128)(2,1)} %get-tuple-element.139), calls=%async_computation | async-start | bytes 1048576 | tf_op jit(solution)/shard_map/all_to_all | solution.py:451
  148.0 0.8 copy-start.1
  176.2 2.9 %collective-permute-start.13 = (bf16[512,1024]{1,0:T(8,128)(2,1)}, bf16[512,1024]{1,0:T(8,128)(2,1)S(1)}, u32[]{:S(2)}, u32[]{:S(2)}) collective-permute-start(bf16[512,1024]{1,0:T(8,128)(2,1)} %get-tuple-element.141), channel_id=1, source_target_pairs={{0,1},{1,0},{2,3},{3,2},{4,5},{5,4},{6,7},{7,6},{8,9},{9,8},{10,11... | collective-permute-start | bytes 3145736 | tf_op jit(solution)/shard_map/ppermute | solution.py:277
  182.0 24.0 %all-to-all-start.2 = ((bf16[64,8,1024]{2,1,0:T(8,128)(2,1)}), bf16[64,8,1024]{2,1,0:T(8,128)(2,1)S(1)}, u32[]{:S(2)}, u32[]{:S(2)}) async-start(bf16[64,8,1024]{2,1,0:T(8,128)(2,1)} %fusion.1), calls=%async_computation.2 | async-start | bytes 2097152 | tf_op jit(solution)/shard_map/all_to_all | solution.py:539
  206.0 3.1 %collective-permute-start.14 = (bf16[512,1152]{1,0:T(8,128)(2,1)}, bf16[512,1152]{1,0:T(8,128)(2,1)S(1)}, u32[]{:S(2)}, u32[]{:S(2)}) collective-permute-start(bf16[512,1152]{1,0:T(8,128)(2,1)} %get-tuple-element.151), channel_id=1, source_target_pairs={{0,1},{1,0},{2,3},{3,2},{4,5},{5,4},{6,7},{7,6},{8,9},{9,8},{10,11... | collective-permute-start | bytes 3538952 | tf_op jit(solution)/shard_map/ppermute | solution.py:277
  212.0 29.6 %all-to-all-start.3 = ((bf16[64,8,1152]{2,1,0:T(8,128)(2,1)}), bf16[64,8,1152]{2,1,0:T(8,128)(2,1)S(1)}, u32[]{:S(2)}, u32[]{:S(2)}) async-start(bf16[64,8,1152]{2,1,0:T(8,128)(2,1)} %fusion), calls=%async_computation.3 | async-start | bytes 2359296 | tf_op jit(solution)/shard_map/all_to_all | solution.py:283

commit v2 on v1

--- a/solution.py
+++ b/solution.py
@@ -93,32 +93,43 @@
 
 
 def inside(inner, keys, up, rows, cols, ro, gi, pair):
+    half = BLOCK // 2
     at = lax.broadcasted_iota(jnp.int32, (BLOCK, BLOCK), 0)
     to = lax.broadcasted_iota(jnp.int32, (BLOCK, BLOCK), 1)
     linked = (to <= at) & (cols[:, CNT : CNT + 1] == rows[CNT : CNT + 1, :])
     bias = jnp.where(linked, 0.0, FAR)
     k = keys[...]
     scores = mm(k[:, STATE:], k[:, :STATE], NT)
+    bias_a, bias_b = bias[:half, :half], bias[half:]
+    scores_a, scores_b = scores[:half, :half], scores[half:]
     left = lax.broadcasted_iota(jnp.int32, (BLOCK, 128), 1) < HEAD
     zero = jnp.zeros((), BF16)
-    paired = jnp.zeros((BLOCK, BLOCK), F32)
+    turned = up[...].T
+    paired_a, paired_b = jnp.zeros((half, half), F32), jnp.zeros((half, BLOCK), F32)
     for q in range(HEADS // 2):
         lanes = slice(128 * q, 128 * q + 128)
         x, u = inner[:, lanes], up[:, lanes]
-        readout = grad = None
+        grads = []
         for s in range(2):
             h = 2 * q + s
             mine = left if s == 0 else ~left
             xs, us = jnp.where(mine, x, zero), jnp.where(mine, u, zero)
-            decays = jnp.exp2(cols[:, h : h + 1] - rows[h : h + 1, :] + bias)
-            mixing = (decays * scores).astype(BF16)
-            paired = paired + decays * mm(us, x, NT)
-            r, g = mm(mixing, xs), mm(mixing, us, TN)
-            readout = r if s == 0 else readout + r
-            grad = g if s == 0 else grad + g
-        ro[:, lanes] = readout.astype(BF16)
-        gi[:, lanes] = grad.astype(BF16)
-    pair[0] = paired.astype(BF16)
+            decays_a = jnp.exp2(cols[:half, h : h + 1] - rows[h : h + 1, :half] + bias_a)
+            decays_b = jnp.exp2(cols[half:, h : h + 1] - rows[h : h + 1, :] + bias_b)
+            mixing_a, mixing_b = (decays_a * scores_a).astype(BF16), (decays_b * scores_b).astype(BF16)
+            paired_a = paired_a + decays_a * mm(us[:half], x[:half], NT)
+            paired_b = paired_b + decays_b * mm(us[half:], x, NT)
+            a, b = mm(mixing_a, xs[:half]), mm(mixing_b, xs)
+            readout_a, readout_b = (a, b) if s == 0 else (readout_a + a, readout_b + b)
+            head = turned[HEAD * h : HEAD * h + HEAD]
+            g = mm(head[:, half:], mixing_b)
+            grads.append(jnp.concatenate([g[:, :half] + mm(head[:, :half], mixing_a), g[:, half:]], axis=1))
+        ro[:half, lanes] = readout_a.astype(BF16)
+        ro[half:, lanes] = readout_b.astype(BF16)
+        gi[:, lanes] = jnp.concatenate(grads, axis=0).astype(BF16).T
+    pair[0, :half, :half] = paired_a.astype(BF16)
+    pair[0, :half, half:] = jnp.zeros((half, half), BF16)
+    pair[0, half:] = paired_b.astype(BF16)
 
 
 def stage_kernel(count, number, block, source, index, fill, *refs):
@@ -134,11 +145,14 @@
 
     @pl.when(i < count[0])
     def _():
-        raw = picks[0][...]
-        for n in range(1, number):
-            raw = jnp.where(jnp.full((BLOCK, D), source[i], jnp.int32) == n, picks[n][...], raw)
-        got = jnp.where(valid_rows(fill[jnp.minimum(block[i], fill.shape[0] - 1)], D), raw, jnp.zeros((), BF16))
-        taken[...] = got
+        valid = valid_rows(fill[jnp.minimum(block[i], fill.shape[0] - 1)], D)
+        for n in range(number):
+
+            @pl.when(source[i] == n)
+            def _(n=n):
+                taken[...] = jnp.where(valid, picks[n][...], jnp.zeros((), BF16))
+
+        got = taken[...]
         x = mm(got, w_in[...]).astype(BF16)
         k = mm(got, w_bc[...]).astype(BF16)
         inner[...] = x
@@ -207,38 +221,19 @@
     give[...] = (acc[:, 1 - core[0]] * scale).reshape(give.shape).astype(BF16)
 
 
-def readout_kernel(core, fill, cot, keys, cols, ro, starts, gains, enter, keep, give, acc, left, right, matrix):
-    step = pl.program_id(0)
-
-    @pl.when(step == 0)
-    def _():
-        matrix[...] = spread_matrix()
-        acc[...] = jnp.zeros_like(acc)
-
-    for n in range(2):
-        at = slice(n * BLOCK, n * BLOCK + BLOCK)
-        start = (starts[n] + gains[n, 8:9] * enter[:64].astype(F32)).astype(BF16)
-        opening = spread(cols[at], OPEN, matrix[...])
-        left[at] = (ro[at].astype(F32) + opening * mm(keys[at, STATE:], start)).astype(BF16)
-        right[at] = jnp.where(valid_rows(fill[2 * step + n], D), cot[0, at], jnp.zeros((), BF16))
-    acc[...] += mm(left[...], right[...], TN).reshape(acc.shape)
-
-    @pl.when(step == pl.num_programs(0) - 1)
-    def _():
-        store_halves(core, acc, keep, give)
-
-
 def gradient_kernel(
-    core, taken, inner, up, keys, cols, gi, pair, starts, push_out, gains, enter,
-    keep, give, acc, right, finish, matrix,
+    core, fill, cot, taken, inner, up, keys, cols, ro, gi, pair, starts, push_out, gains, enter,
+    keep, give, acc_in, acc_out, left, right, masked, finish, matrix,
 ):
     step = pl.program_id(0)
+    last = pl.num_programs(0) - 1
 
     @pl.when(step == 0)
     def _():
         matrix[...] = spread_matrix()
         finish[...] = enter[64:].astype(F32)
-        acc[...] = jnp.zeros_like(acc)
+        acc_in[...] = jnp.zeros_like(acc_in)
+        acc_out[...] = jnp.zeros_like(acc_out)
 
     for n in (1, 0):
         at = slice(n * BLOCK, n * BLOCK + BLOCK)
@@ -251,6 +246,8 @@
         closing = spread(table, CLOSE, matrix[...])
         k = keys[at]
         write, read = k[:, :STATE], k[:, STATE:]
+        left[at] = (ro[at].astype(F32) + opening * mm(read, start)).astype(BF16)
+        masked[at] = jnp.where(valid_rows(fill[2 * (last - step) + n], D), cot[0, at], jnp.zeros((), BF16))
         right[at, :D] = (gi[at].astype(F32) + closing * mm(write, end)).astype(BF16)
         into = (closing * inner[at].astype(F32)).astype(BF16)
         out = (opening * up[at].astype(F32)).astype(BF16)
@@ -258,11 +255,16 @@
         grad_write = mm(g, read, TN) + mm(into, end, NT)
         grad_read = mm(g, write) + mm(out, start, NT)
         right[at, D:] = jnp.concatenate([grad_write, grad_read], axis=1).astype(BF16)
-    acc[...] += mm(taken[...], right[...], TN).reshape(acc.shape)
-
-    @pl.when(step == pl.num_programs(0) - 1)
+    acc_out[...] += mm(left[...], masked[...], TN).reshape(acc_out.shape)
+    acc_in[...] += mm(taken[...], right[...], TN).reshape(acc_in.shape)
+
+    @pl.when(step == last)
     def _():
-        store_halves(core, acc, keep, give)
+        scale = 1.0 / 512.0
+        for acc, columns in ((acc_in, slice(0, D + 128)), (acc_out, slice(D + 128, None))):
+            mine, other = acc[:, core[0]] * scale, acc[:, 1 - core[0]] * scale
+            keep[:, columns] = mine.reshape(keep.shape[0], -1)
+            give[:, columns] = other.reshape(give.shape[0], -1).astype(BF16)
 
 
 def ring(axis, by):
@@ -305,16 +307,19 @@
     away = (owner // 2 - z) % 4
     same = owner % 2 == core
     low = slot < 2
-    stage = jnp.where(away == 0, 0, jnp.where(away == 2, 3, jnp.where((away == 3) == low, 1, 2)))
+    stage = jnp.where(away == 0, 0, jnp.where(away == 2, 2, 1))
     side = jnp.where(away == 2, jnp.where(low, 0, 1), jnp.where(away == 3, 0, 1))
-    source = jnp.where(away == 0, jnp.where(same, 0, 1), side + jnp.where(same, 0, 2))
+    late = (away % 2 == 1) & ((away == 3) != low)
+    source = jnp.where(away == 0, 0, side + jnp.where(late, 4, 0)) + jnp.where(
+        same, 0, jnp.where(away == 0, 1, 2)
+    )
     index = jnp.where(away == 0, slot, slot % 2)
     ids = jnp.arange(blocks)
     rank = jnp.sum((stage[None] == stage[:, None]) & (ids[None] < ids[:, None]), axis=1)
-    counts = jnp.sum(stage[None] == jnp.arange(4)[:, None], axis=1)
-    most = (4, blocks, blocks, 4)
+    counts = jnp.sum(stage[None] == jnp.arange(3)[:, None], axis=1)
+    most = (4, blocks, 4)
     turn = jnp.minimum(jnp.arange(blocks)[None], counts[:, None] - 1)
-    chosen = (stage[None, None] == jnp.arange(4)[:, None, None]) & (rank[None, None] == turn[:, :, None])
+    chosen = (stage[None, None] == jnp.arange(3)[:, None, None]) & (rank[None, None] == turn[:, :, None])
     of = lambda v: jnp.sum(jnp.where(chosen, v[None, None], 0), axis=2)
     block = jnp.where(counts[:, None] > 0, of(ids), blocks).astype(jnp.int32)
     source, index = of(source).astype(jnp.int32), of(index).astype(jnp.int32)
@@ -352,21 +357,19 @@
 
     room = steps + BLOCK
     made = None
-    for s in range(4):
+    for s in range(3):
         if s == 0:
             below_a, above_a, second, first, up = lax.optimization_barrier(
                 (below_a, above_a, second, first, up)
             )
             below_b, above_b = up_z(second), down_z(first)
-            sources, later = (mine, other), (below_a, above_a, swap(below_a), swap(above_a))
+            sources, near = (mine, other), (below_a, above_a, swap(below_a), swap(above_a))
         elif s == 1:
-            sources = later
-        elif s == 2:
             below_b, above_b, below_a, above_a, made = lax.optimization_barrier(
                 (below_b, above_b, below_a, above_a, made)
             )
             far_low, far_high = up_z(below_a), down_z(above_a)
-            sources = (below_b, above_b, swap(below_b), swap(above_b))
+            sources = (*near, below_b, above_b, swap(below_b), swap(above_b))
         else:
             far_low, far_high, made = lax.optimization_barrier((far_low, far_high, made))
             sources = (far_low, far_high, swap(far_low), swap(far_high))
@@ -468,54 +471,28 @@
     own_core = core.reshape(1)
     two = lambda width: pl.BlockSpec((2 * BLOCK, width), lambda b, *_: (b, 0))
     pairs = lambda *dims: pl.BlockSpec((2, *dims), lambda b, *_: (b, 0, 0))
-    keep_out, give_out = call(
-        readout_kernel,
-        "readout",
-        (shape((D // 2, D), F32), shape((D // 2, D), BF16)),
+    back = lambda spec: pl.BlockSpec(
+        spec.block_shape, lambda s, *refs: spec.index_map(blocks // 2 - 1 - s, *refs)
+    )
+    wide = D + 128
+    both = wide + D
+    keep, give = call(
+        gradient_kernel,
+        "gradient",
+        (shape((D // 2, both), F32), shape((D // 2, both), BF16)),
         pltpu.PrefetchScalarGridSpec(
             num_scalar_prefetch=2,
             grid=(blocks // 2,),
             in_specs=[
-                pl.BlockSpec((1, 2 * BLOCK, D), lambda b, *_: (0, b, 0)),
-                two(128),
-                two(128),
-                two(D),
-                pairs(STATE, D),
-                pairs(16, D),
-                whole(128, D),
-            ],
-            out_specs=[whole(D // 2, D), whole(D // 2, D)],
-            scratch_shapes=[
-                vmem(F32, D // 16, 2, 8, D),
-                vmem(BF16, 2 * BLOCK, D),
-                vmem(BF16, 2 * BLOCK, D),
-                vmem(BF16, 256, D),
-            ],
-        ),
-        2 * steps * D * (D + 256),
-        14 << 20,
-    )(own_core, fill, cotangent, keys, cols, ro, starts, gains, enter)
-
-    half_out, enter = lax.optimization_barrier((over_chip(keep_out, give_out), enter))
-    back = lambda spec: pl.BlockSpec(
-        spec.block_shape, lambda s, *refs: spec.index_map(blocks // 2 - 1 - s, *refs)
-    )
-    wide = D + 128
-    keep_in, give_in = call(
-        gradient_kernel,
-        "gradient",
-        (shape((D // 2, wide), F32), shape((D // 2, wide), BF16)),
-        pltpu.PrefetchScalarGridSpec(
-            num_scalar_prefetch=1,
-            grid=(blocks // 2,),
-            in_specs=[
                 back(s)
                 for s in (
+                    pl.BlockSpec((1, 2 * BLOCK, D), lambda b, *_: (0, b, 0)),
                     two(D),
                     two(D),
                     two(D),
                     two(128),
                     two(128),
+                    two(D),
                     two(D),
                     pairs(BLOCK, BLOCK),
                     pairs(STATE, D),
@@ -524,23 +501,23 @@
                     whole(128, D),
                 )
             ],
-            out_specs=[whole(D // 2, wide), whole(D // 2, wide)],
+            out_specs=[whole(D // 2, both), whole(D // 2, both)],
             scratch_shapes=[
                 vmem(F32, D // 16, 2, 8, wide),
+                vmem(F32, D // 16, 2, 8, D),
+                vmem(BF16, 2 * BLOCK, D),
                 vmem(BF16, 2 * BLOCK, wide),
+                vmem(BF16, 2 * BLOCK, D),
                 vmem(F32, STATE, D),
                 vmem(BF16, 256, D),
             ],
         ),
-        2 * steps * D * (D + 1024),
-        26 << 20,
-    )(own_core, taken, inner, up, keys, cols, gi, pair, starts, push_out, gains, enter)
-
-    got_out = lax.all_to_all(half_out, CHIPS, 0, 0)
-    got_out, keep_in, give_in = lax.optimization_barrier((got_out, keep_in, give_in))
-    grad_out = got_out.astype(F32).sum(0)
-    grad_in = over_chips(over_chip(keep_in, give_in))
-    return (grad_in[:, :D], grad_in[:, D:], grad_out)
+        2 * steps * D * (2 * D + 1280),
+        36 << 20,
+    )(own_core, fill, cotangent, taken, inner, up, keys, cols, ro, gi, pair, starts, push_out, gains, enter)
+
+    grads = over_chips(over_chip(keep, give))
+    return (grads[:, :D], grads[:, D:wide], grads[:, wide:])
 
 
 def solution(mesh):

time: 246 us -> 219 us (0.89)
  blocking collectives: 12.9 us -> 49.9 us
  waiting for transfers between devices: 65.9 us -> 38.7 us
  starting transfers between devices: 35.5 us -> 20.1 us
  Pallas kernels: 108 us -> 93.3 us
  other arithmetic: 9.13 us -> 6.01 us
    all_to_all x0 -> x1, blocking collectives: none -> 37 us  [over_chips(): return lax.all_to_all(half, CHIPS, 0, 0).astype(F32).sum(0)]
    all_to_all x2 -> x0, waiting for transfers between devices: 20.8 us -> none  [the longest x1 19.6 us: over_chips(): return lax.all_to_all(half, CHIPS, 0, 0).astype(F32).sum(0)]
    all_to_all x2 -> x0, starting transfers between devices: 13.9 us -> none  [the longest x1 9.22 us: over_chips(): return lax.all_to_all(half, CHIPS, 0, 0).astype(F32).sum(0)]
    pallas_call x4 -> x3, Pallas kernels: 60.2 us -> 49.2 us  [on_device(): pl.pallas_call(body, out_shape=(shape((room, D), BF16), shape((room, D),...]
    ppermute x3, waiting for transfers between devices: 23.2 us -> 18.3 us  [on_device(): up_z = lambda v: lax.ppermute(v, 'z', ring('z', 1))]
    pallas_call x2 -> x1, Pallas kernels: 30.6 us -> 26.6 us  [on_device(): call(gradient_kernel, 'gradient', (shape((D // 2, both), F32), shape((D /...]
    reshape x2 -> x1, other arithmetic: 5.92 us -> 2.78 us  [over_chip(): return half.reshape(lax.axis_size(CHIPS), 8, -1)]
    ppermute x2 -> x1, waiting for transfers between devices: 5.92 us -> 4.54 us  [over_chip(): got = lax.ppermute(give, 'c', ring('c', 1))]
  transfers between devices with their start and end apart: 18 -> 15, of which waited for: 10 -> 8; matrix products, arithmetic and copies ran while one was open for 2% -> 2% of each run, Pallas kernels for 29% -> 20%
where the time goes in v2:
time: 219 us; the launch traced here: 218 us
  Pallas kernels  93.3 us (43%)
  blocking collectives  49.9 us (23%)
  waiting for transfers between devices  38.7 us (18%)
  starting transfers between devices  20.1 us (9%)
  local copies, waits for them, and re-layouts  9.03 us (4%)
  other arithmetic  6.01 us (3%)
    pallas_call x3, Pallas kernels, on_device(): pl.pallas_call(body, out_shape=(shape((room, D), BF16), shape((room, D),...  49.2 us
    all_to_all x1, blocking collectives, over_chips(): return lax.all_to_all(half, CHIPS, 0, 0).astype(F32).sum(0)  37 us
    pallas_call x1, Pallas kernels, on_device(): call(gradient_kernel, 'gradient', (shape((D // 2, both), F32), shape((D /...  26.6 us
    ppermute x3, waiting for transfers between devices, on_device(): up_z = lambda v: lax.ppermute(v, 'z', ring('z', 1))  18.3 us
    all_to_all x1, blocking collectives, on_device(): enter = lax.all_to_all(entering, TM, 0, 0).reshape(128, D)  12.9 us
    all_to_all x1, waiting for transfers between devices, on_device(): terms = lax.all_to_all(total, TM, 0, 0)  11.8 us
    pallas_call x1, Pallas kernels, on_device(): call(upstream_kernel, 'upstream', (shape((steps, D), BF16), shape((32, st...  11.6 us
    all_to_all x1, starting transfers between devices, on_device(): terms = lax.all_to_all(total, TM, 0, 0)  7.79 us
  transfers between devices with their start and end apart: 15, of which 8 were waited for; matrix products, arithmetic and copies ran while one was open for 2% of the time, Pallas kernels for 20%

profile of v2, /device:TPU:0, one launch (start us, length us, event | category | flops | bytes accessed | tf_op | source)
XLA Modules:
  0.0 217.8 jit_solution(1272843017994409168)
XLA Ops:
  0.6 0.0 copy-start
  0.6 3.2 %fusion.12 = (bf16[1,1,512,1024]{3,2,1,0:T(8,128)(2,1)}, bf16[1,1,512,1024]{3,2,1,0:T(8,128)(2,1)}) fusion(bf16[1,1,1024,1024]{3,2,1,0:T(8,128)(2,1)} %param.10), kind=kLoop, calls=%fused_computation.67 | loop fusion | bytes 4194304 | tf_op jit(solution)/shard_map/slice | solution.py:304
  3.8 2.0 collective-permute-start
  5.8 2.1 collective-permute-start.1
  7.9 0.0 copy-done
  7.9 0.0 collective-permute-start.4
  8.0 0.7 compare_select_fusion.11
  8.6 0.7 fusion.11
  9.3 0.7 fusion.10
  10.1 0.1 convert_reduce_fusion.2
  10.2 0.1 iota_minimum_fusion
  10.3 0.2 convert_reduce_fusion.1
  10.4 0.3 select_reduce_fusion
  10.8 0.1 broadcast_select_fusion
  10.9 11.6 %upstream.1 = (bf16[2048,1024]{1,0:T(8,128)(2,1)}, f32[32,2048]{1,0:T(8,128)}, f32[2048,128]{1,0:T(8,128)}, f32[8,8,128]{2,1,0:T(8,128)}) custom-call(s32[8]{0:T(128)} %bitcast.64, f32[16,2048]{1,0:T(8,128)} %bitcast.69, s32[8,1,256]{2,1,0:T(1,128)} %bitcast.70, bf16[1,2048,1024]{2,1,0:T(8,128)(2,1)} %cot.3, bf16[1024,1024]{1,0:T(8,128)(2,1)} %w_out.1), custom_call_target="tpu_custom_call" | custom-call | flops 4294967296 | bytes 12582912 | tf_op jit(solution)/shard_map/upstream/pallas_call | solution.py:334
  22.5 8.8 %collective-permute-done.refs_0_ = bf16[2,256,1024]{2,1,0:T(8,128)(2,1)S(1)} collective-permute-done((bf16[2,256,1024]{2,1,0:T(8,128)(2,1)}, bf16[2,256,1024]{2,1,0:T(8,128)(2,1)S(1)}, u32[]{:S(2)}, u32[]{:S(2)}) %collective-permute-start) | collective-permute-done | bytes 1048608 | tf_op jit(solution)/shard_map/ppermute | solution.py:302
  31.3 0.0 collective-permute-done.1.refs_1_
  31.3 1.4 collective-permute-start.2
  32.7 1.9 collective-permute-start.3
  34.6 0.6 slice_bitcast_fusion.2
  35.1 0.6 slice_bitcast_fusion
  35.8 0.0 collective-permute-start.7
  35.8 0.6 fusion.14
  36.4 0.5 collective-permute-start.8
  36.9 0.0 collective-permute-done.4.refs_1_
  36.9 12.9 %stage_0.1 = (bf16[2304,1024]{1,0:T(8,128)(2,1)}, bf16[2304,1024]{1,0:T(8,128)(2,1)}, bf16[2304,128]{1,0:T(8,128)(2,1)}, bf16[2304,1024]{1,0:T(8,128)(2,1)}, bf1...) custom-call(s32[8]{0:T(128)} %get-tuple-element.139.block, ...), custom_call_target="tpu_custom_call" | custom-call | flops 5368709120 | bytes 16777216 | tf_op jit(solution)/shard_map/stage_0/pallas_call | solution.py:392
  49.9 7.2 %collective-permute-done.2.refs_4_ = bf16[2,256,1024]{2,1,0:T(8,128)(2,1)S(1)} collective-permute-done((bf16[2,256,1024]{2,1,0:T(8,128)(2,1)}, bf16[2,256,1024]{2,1,0:T(8,128)(2,1)S(1)}, u32[]{:S(2)}, u32[]{:S(2)}) %collective-permute-start.2) | collective-permute-done | bytes 1048608 | tf_op jit(solution)/shard_map/ppermute | solution.py:302
  57.1 0.0 collective-permute-done.3.refs_5_
  57.1 0.1 collective-permute-start.10
  57.2 0.5 collective-permute-start.9
  57.7 0.0 copy-done.2
  57.7 0.8 collective-permute-start.5
  58.5 0.0 collective-permute-done.7.refs_2_
  58.5 2.4 %collective-permute-start.6 = (bf16[2,256,1024]{2,1,0:T(8,128)(2,1)}, bf16[2,256,1024]{2,1,0:T(8,128)(2,1)S(1)}, u32[]{:S(2)}, u32[]{:S(2)}) collective-permute-start(bf16[2,256,1024]{2,1,0:T(8,128)(2,1)} %collective-permute-done.1.refs_1_), channel_id=1, source_target_pairs={{0,6},{2,0},{4,2},{6,4},{1,7},{3,1},{5,3},{7,5},{8,14},{10,8},{12,... | collective-permute-start | bytes 3145736 | tf_op jit(solution)/shard_map/ppermute | solution.py:303
  60.9 0.0 collective-permute-done.8.refs_3_
  60.9 0.0 collective-permute-done.10.refs_7_
  60.9 0.4 collective-permute-done.9.refs_6_
  61.3 1.0 copy-done.9
  62.3 0.0 copy-done.3
  62.3 0.0 copy-done.6
  62.3 19.4 %stage_1.1 = (bf16[2304,1024]{1,0:T(8,128)(2,1)}, bf16[2304,1024]{1,0:T(8,128)(2,1)}, bf16[2304,128]{1,0:T(8,128)(2,1)}, bf16[2304,1024]{1,0:T(8,128)(2,1)}, bf1...) custom-call(s32[8]{0:T(128)} %get-tuple-element.138.block, ...), custom_call_target="tpu_custom_call", output_to_operand_aliasing={{0}: (18, {}), {1}: (19, {}), {2}: (20, {}), {3}: (21, {}),... | custom-call | flops 5368709120 | bytes 16777216 | tf_op jit(solution)/shard_map/stage_1/pallas_call | solution.py:392
  81.8 2.3 %collective-permute-done.5.refs_0_ = bf16[2,256,1024]{2,1,0:T(8,128)(2,1)S(1)} collective-permute-done((bf16[2,256,1024]{2,1,0:T(8,128)(2,1)S(1)}, bf16[2,256,1024]{2,1,0:T(8,128)(2,1)S(1)}, u32[]{:S(2)}, u32[]{:S(2)}) %collective-permute-start.5) | collective-permute-done | bytes 1048608 | tf_op jit(solution)/shard_map/ppermute | solution.py:302
  84.0 0.0 collective-permute-done.6.refs_1_
  84.1 0.1 collective-permute-start.11
  84.1 0.5 collective-permute-start.12
  84.6 2.1 collective-permute-done.11.refs_2_
  86.8 1.5 collective-permute-done.12.refs_3_
  88.3 0.0 copy-done.5
  88.3 1.0 copy-done.11
  89.3 16.8 %stage_2.1 = (bf16[2304,1024]{1,0:T(8,128)(2,1)}, bf16[2304,1024]{1,0:T(8,128)(2,1)}, bf16[2304,128]{1,0:T(8,128)(2,1)}, bf16[2304,1024]{1,0:T(8,128)(2,1)}, bf1...) custom-call(s32[8]{0:T(128)} %get-tuple-element.140.block, ...), custom_call_target="tpu_custom_call", output_to_operand_aliasing={{0}: (14, {}), {1}: (15, {}), {2}: (16, {}), {3}: (17, {}),... | custom-call | flops 5368709120 | bytes 16777216 | tf_op jit(solution)/shard_map/stage_2/pallas_call | solution.py:392
  106.1 3.9 %local.1 = (f32[8,64,1024]{2,1,0:T(8,128)}, f32[8,16,1024]{2,1,0:T(8,128)}, bf16[16,16,1024]{2,1,0:T(8,128)(2,1)}) custom-call(f32[9,64,1024]{2,1,0:T(8,128)} %get-tuple-element.115.push_in, f32[9,64,1024]{2,1,0:T(8,128)} %get-tuple-element.116.push_out, f32[8,8,128]{2,1,0:T(8,128)} %get-tuple-element.117.ends), custom_call_target="tpu_custom_call" | custom-call | flops 16777216 | bytes 7340032 | tf_op jit(solution)/shard_map/local/pallas_call | solution.py:440
  109.9 7.8 %all-to-all-start = ((bf16[16,16,1024]{2,1,0:T(8,128)(2,1)}), bf16[16,16,1024]{2,1,0:T(8,128)(2,1)S(1)}, u32[]{:S(2)}, u32[]{:S(2)}) async-start(bf16[16,16,1024]{2,1,0:T(8,128)(2,1)} %get-tuple-element.120), calls=%async_computation | async-start | bytes 1048576 | tf_op jit(solution)/shard_map/all_to_all | solution.py:454
  117.7 11.8 %all-to-all-done.terms = bf16[16,16,1024]{2,1,0:T(8,128)(2,1)S(1)} async-done(((bf16[16,16,1024]{2,1,0:T(8,128)(2,1)}), bf16[16,16,1024]{2,1,0:T(8,128)(2,1)S(1)}, u32[]{:S(2)}, u32[]{:S(2)}) %all-to-all-start) | async-done | bytes 524320 | tf_op jit(solution)/shard_map/all_to_all | solution.py:454
  129.5 0.8 copy-done.1
  130.3 2.0 scan.1
  132.3 12.9 %all_to_all.15 = bf16[16,8,1024]{2,1,0:T(8,128)(2,1)} all-to-all(bf16[16,8,1024]{2,1,0:T(8,128)(2,1)} %scan.1), channel_id=1, replica_groups=mesh['y'=4,'x'=4,'z'=4,'c'=2] {'y','x'}, dimensions={0} | all-to-all | bytes 524288 | tf_op jit(solution)/shard_map/all_to_all | solution.py:469
  145.2 26.6 %gradient.1 = (f32[512,2176]{1,0:T(8,128)}, bf16[512,2176]{1,0:T(8,128)(2,1)}) custom-call(s32[1]{0:T(128)} %bitcast.core, s32[8]{0:T(128)} %bitcast.68, bf16[1,2048,1024]{2,1,0:T(8,128)(2,1)} %cot.3, bf16[2304,1024]{1,0:T(8,128)(2,1)} %get-tuple-element.109.taken, bf16[2304,1024]{1,0:T(8,128)(2,1)} %get-tuple-element.110.inner, ...), custom_call_target="tpu_custom_call" | custom-call | flops 13958643712 | bytes 37748736 | tf_op jit(solution)/shard_map/gradient/pallas_call | solution.py:479
  171.8 0.1 collective-permute-start.13
  171.9 4.5 %collective-permute-done.13 = bf16[512,2176]{1,0:T(8,128)(2,1)S(1)} collective-permute-done((bf16[512,2176]{1,0:T(8,128)(2,1)}, bf16[512,2176]{1,0:T(8,128)(2,1)S(1)}, u32[]{:S(2)}, u32[]{:S(2)}) %collective-permute-start.13) | collective-permute-done | bytes 2228256 | tf_op jit(solution)/shard_map/ppermute | solution.py:279
  176.4 2.8 %fusion = bf16[64,8,2176]{2,1,0:T(8,128)(2,1)S(1)} fusion(f32[512,2176]{1,0:T(8,128)} %get-tuple-element.121, bf16[512,2176]{1,0:T(8,128)(2,1)S(1)} %collective-permute-done.13), kind=kLoop, calls=%fused_computation.2 | loop fusion | flops 3342336 | bytes 8912896 | tf_op jit(solution)/shard_map/reshape | solution.py:281
  179.2 37.0 %all_to_all.16 = bf16[64,8,2176]{2,1,0:T(8,128)(2,1)S(1)} all-to-all(bf16[64,8,2176]{2,1,0:T(8,128)(2,1)S(1)} %fusion), channel_id=1, replica_groups=mesh['y'=4,'x'=4,'z'=4,'c'=2] {'y','x','z'}, dimensions={0} | all-to-all | bytes 4456448 | tf_op jit(solution)/shard_map/all_to_all | solution.py:285
  216.3 0.3 convert_reduce_fusion
  216.6 0.6 fusion.13
  217.2 0.6 slice.77
  (18 shorter events, 0.0 us)
Async XLA Ops:
  0.6 7.3 %copy-start = (bf16[1,1,1024,1024]{3,2,1,0:T(8,128)(2,1)S(1)}, bf16[1,1,1024,1024]{3,2,1,0:T(8,128)(2,1)}, u32[]{:S(2)}) copy-start(bf16[1,1,1024,1024]{3,2,1,0:T(8,128)(2,1)} %param.10) | copy-start | bytes 6291460
  3.8 27.5 %collective-permute-start = (bf16[2,256,1024]{2,1,0:T(8,128)(2,1)}, bf16[2,256,1024]{2,1,0:T(8,128)(2,1)S(1)}, u32[]{:S(2)}, u32[]{:S(2)}) collective-permute-start(bf16[2,256,1024]{2,1,0:T(8,128)(2,1)} %bitcast.9), channel_id=1, source_target_pairs={{0,2},{2,4},{4,6},{6,0},{1,3},{3,5},{5,7},{7,1},{8,10},{10,12},{12... | collective-permute-start | bytes 3145736 | tf_op jit(solution)/shard_map/ppermute | solution.py:302
  5.8 25.5 %collective-permute-start.1 = (bf16[2,256,1024]{2,1,0:T(8,128)(2,1)}, bf16[2,256,1024]{2,1,0:T(8,128)(2,1)}, u32[]{:S(2)}, u32[]{:S(2)}) collective-permute-start(bf16[2,256,1024]{2,1,0:T(8,128)(2,1)} %bitcast.10), channel_id=1, source_target_pairs={{0,6},{2,0},{4,2},{6,4},{1,7},{3,1},{5,3},{7,5},{8,14},{10,8},{12,... | collective-permute-start | bytes 3145736 | tf_op jit(solution)/shard_map/ppermute | solution.py:303
  7.9 29.0 %collective-permute-start.4 = (bf16[4,256,1024]{2,1,0:T(8,128)(2,1)S(1)}, bf16[4,256,1024]{2,1,0:T(8,128)(2,1)}, u32[]{:S(2)}, u32[]{:S(2)}) collective-permute-start(bf16[4,256,1024]{2,1,0:T(8,128)(2,1)S(1)} %bitcast.62), channel_id=1, source_target_pairs={{0,1},{1,0},{2,3},{3,2},{4,5},{5,4},{6,7},{7,6},{8,9},{9,8},{10,11... | collective-permute-start | bytes 6291464 | tf_op jit(solution)/shard_map/ppermute | solution.py:301
  31.3 26.4 %copy-start.2 = (bf16[2,256,1024]{2,1,0:T(8,128)(2,1)}, bf16[2,256,1024]{2,1,0:T(8,128)(2,1)S(1)}, u32[]{:S(2)}) copy-start(bf16[2,256,1024]{2,1,0:T(8,128)(2,1)S(1)} %collective-permute-done.refs_0_) | copy-start | bytes 3145732
  31.3 25.8 %collective-permute-start.2 = (bf16[2,256,1024]{2,1,0:T(8,128)(2,1)}, bf16[2,256,1024]{2,1,0:T(8,128)(2,1)S(1)}, u32[]{:S(2)}, u32[]{:S(2)}) collective-permute-start(bf16[2,256,1024]{2,1,0:T(8,128)(2,1)} %bitcast.10), channel_id=1, source_target_pairs={{0,2},{2,4},{4,6},{6,0},{1,3},{3,5},{5,7},{7,1},{8,10},{10,12},{12... | collective-permute-start | bytes 3145736 | tf_op jit(solution)/shard_map/ppermute | solution.py:302
  32.7 24.4 %collective-permute-start.3 = (bf16[2,256,1024]{2,1,0:T(8,128)(2,1)}, bf16[2,256,1024]{2,1,0:T(8,128)(2,1)S(1)}, u32[]{:S(2)}, u32[]{:S(2)}) collective-permute-start(bf16[2,256,1024]{2,1,0:T(8,128)(2,1)} %bitcast.9), channel_id=1, source_target_pairs={{0,6},{2,0},{4,2},{6,4},{1,7},{3,1},{5,3},{7,5},{8,14},{10,8},{12,... | collective-permute-start | bytes 3145736 | tf_op jit(solution)/shard_map/ppermute | solution.py:303
  35.8 22.8 %collective-permute-start.7 = (bf16[2,256,1024]{2,1,0:T(8,128)(2,1)S(1)}, bf16[2,256,1024]{2,1,0:T(8,128)(2,1)S(1)}, u32[]{:S(2)}, u32[]{:S(2)}) collective-permute-start(bf16[2,256,1024]{2,1,0:T(8,128)(2,1)S(1)} %collective-permute-done.refs_0_), channel_id=1, source_target_pairs={{0,1},{1,0},{2,3},{3,2},{4,5},{5,4},{6,7},{7,6},{8,9},{9,8},{10,11... | collective-permute-start | bytes 3145736 | tf_op jit(solution)/shard_map/ppermute | solution.py:301
  36.4 24.5 %collective-permute-start.8 = (bf16[2,256,1024]{2,1,0:T(8,128)(2,1)}, bf16[2,256,1024]{2,1,0:T(8,128)(2,1)}, u32[]{:S(2)}, u32[]{:S(2)}) collective-permute-start(bf16[2,256,1024]{2,1,0:T(8,128)(2,1)} %collective-permute-done.1.refs_1_), channel_id=1, source_target_pairs={{0,1},{1,0},{2,3},{3,2},{4,5},{5,4},{6,7},{7,6},{8,9},{9,8},{10,11... | collective-permute-start | bytes 3145736 | tf_op jit(solution)/shard_map/ppermute | solution.py:301
  57.1 5.2 %copy-start.3 = (bf16[2,256,1024]{2,1,0:T(8,128)(2,1)}, bf16[2,256,1024]{2,1,0:T(8,128)(2,1)S(1)}, u32[]{:S(2)}) copy-start(bf16[2,256,1024]{2,1,0:T(8,128)(2,1)S(1)} %collective-permute-done.2.refs_4_) | copy-start | bytes 3145732
  57.1 5.2 %copy-start.4 = (bf16[2,256,1024]{2,1,0:T(8,128)(2,1)}, bf16[2,256,1024]{2,1,0:T(8,128)(2,1)S(1)}, u32[]{:S(2)}) copy-start(bf16[2,256,1024]{2,1,0:T(8,128)(2,1)S(1)} %collective-permute-done.3.refs_5_) | copy-start | bytes 3145732
  57.1 3.8 %collective-permute-start.10 = (bf16[2,256,1024]{2,1,0:T(8,128)(2,1)S(1)}, bf16[2,256,1024]{2,1,0:T(8,128)(2,1)S(1)}, u32[]{:S(2)}, u32[]{:S(2)}) collective-permute-start(bf16[2,256,1024]{2,1,0:T(8,128)(2,1)S(1)} %collective-permute-done.3.refs_5_), channel_id=1, source_target_pairs={{0,1},{1,0},{2,3},{3,2},{4,5},{5,4},{6,7},{7,6},{8,9},{9,8},{10,11... | collective-permute-start | bytes 3145736 | tf_op jit(solution)/shard_map/ppermute | solution.py:301
  57.2 4.1 %collective-permute-start.9 = (bf16[2,256,1024]{2,1,0:T(8,128)(2,1)S(1)}, bf16[2,256,1024]{2,1,0:T(8,128)(2,1)S(1)}, u32[]{:S(2)}, u32[]{:S(2)}) collective-permute-start(bf16[2,256,1024]{2,1,0:T(8,128)(2,1)S(1)} %collective-permute-done.2.refs_4_), channel_id=1, source_target_pairs={{0,1},{1,0},{2,3},{3,2},{4,5},{5,4},{6,7},{7,6},{8,9},{9,8},{10,11... | collective-permute-start | bytes 3145736 | tf_op jit(solution)/shard_map/ppermute | solution.py:301
  57.7 26.4 %collective-permute-start.5 = (bf16[2,256,1024]{2,1,0:T(8,128)(2,1)S(1)}, bf16[2,256,1024]{2,1,0:T(8,128)(2,1)S(1)}, u32[]{:S(2)}, u32[]{:S(2)}) collective-permute-start(bf16[2,256,1024]{2,1,0:T(8,128)(2,1)S(1)} %collective-permute-done.refs_0_), channel_id=1, source_target_pairs={{0,2},{2,4},{4,6},{6,0},{1,3},{3,5},{5,7},{7,1},{8,10},{10,12},{12... | collective-permute-start | bytes 3145736 | tf_op jit(solution)/shard_map/ppermute | solution.py:302
  58.5 3.8 %copy-start.6 = (bf16[2,256,1024]{2,1,0:T(8,128)(2,1)}, bf16[2,256,1024]{2,1,0:T(8,128)(2,1)S(1)}, u32[]{:S(2)}) copy-start(bf16[2,256,1024]{2,1,0:T(8,128)(2,1)S(1)} %collective-permute-done.7.refs_2_) | copy-start | bytes 3145732
  58.5 25.5 %collective-permute-start.6 = (bf16[2,256,1024]{2,1,0:T(8,128)(2,1)}, bf16[2,256,1024]{2,1,0:T(8,128)(2,1)S(1)}, u32[]{:S(2)}, u32[]{:S(2)}) collective-permute-start(bf16[2,256,1024]{2,1,0:T(8,128)(2,1)} %collective-permute-done.1.refs_1_), channel_id=1, source_target_pairs={{0,6},{2,0},{4,2},{6,4},{1,7},{3,1},{5,3},{7,5},{8,14},{10,8},{12,... | collective-permute-start | bytes 3145736 | tf_op jit(solution)/shard_map/ppermute | solution.py:303
  60.9 1.4 copy-start.8
  61.3 1.0 copy-start.9
  84.0 4.2 %copy-start.5 = (bf16[2,256,1024]{2,1,0:T(8,128)(2,1)}, bf16[2,256,1024]{2,1,0:T(8,128)(2,1)S(1)}, u32[]{:S(2)}) copy-start(bf16[2,256,1024]{2,1,0:T(8,128)(2,1)S(1)} %collective-permute-done.5.refs_0_) | copy-start | bytes 3145732
  84.0 4.2 %copy-start.7 = (bf16[2,256,1024]{2,1,0:T(8,128)(2,1)}, bf16[2,256,1024]{2,1,0:T(8,128)(2,1)S(1)}, u32[]{:S(2)}) copy-start(bf16[2,256,1024]{2,1,0:T(8,128)(2,1)S(1)} %collective-permute-done.6.refs_1_) | copy-start | bytes 3145732
  84.1 2.7 %collective-permute-start.11 = (bf16[2,256,1024]{2,1,0:T(8,128)(2,1)S(1)}, bf16[2,256,1024]{2,1,0:T(8,128)(2,1)S(1)}, u32[]{:S(2)}, u32[]{:S(2)}) collective-permute-start(bf16[2,256,1024]{2,1,0:T(8,128)(2,1)S(1)} %collective-permute-done.5.refs_0_), channel_id=1, source_target_pairs={{0,1},{1,0},{2,3},{3,2},{4,5},{5,4},{6,7},{7,6},{8,9},{9,8},{10,11... | collective-permute-start | bytes 3145736 | tf_op jit(solution)/shard_map/ppermute | solution.py:301
  84.1 4.1 %collective-permute-start.12 = (bf16[2,256,1024]{2,1,0:T(8,128)(2,1)S(1)}, bf16[2,256,1024]{2,1,0:T(8,128)(2,1)S(1)}, u32[]{:S(2)}, u32[]{:S(2)}) collective-permute-start(bf16[2,256,1024]{2,1,0:T(8,128)(2,1)S(1)} %collective-permute-done.6.refs_1_), channel_id=1, source_target_pairs={{0,1},{1,0},{2,3},{3,2},{4,5},{5,4},{6,7},{7,6},{8,9},{9,8},{10,11... | collective-permute-start | bytes 3145736 | tf_op jit(solution)/shard_map/ppermute | solution.py:301
  86.8 1.5 copy-start.10
  88.3 1.0 copy-start.11
  109.9 19.6 %all-to-all-start = ((bf16[16,16,1024]{2,1,0:T(8,128)(2,1)}), bf16[16,16,1024]{2,1,0:T(8,128)(2,1)S(1)}, u32[]{:S(2)}, u32[]{:S(2)}) async-start(bf16[16,16,1024]{2,1,0:T(8,128)(2,1)} %get-tuple-element.120), calls=%async_computation | async-start | bytes 1048576 | tf_op jit(solution)/shard_map/all_to_all | solution.py:454
  129.5 0.8 copy-start.1
  171.8 4.6 %collective-permute-start.13 = (bf16[512,2176]{1,0:T(8,128)(2,1)}, bf16[512,2176]{1,0:T(8,128)(2,1)S(1)}, u32[]{:S(2)}, u32[]{:S(2)}) collective-permute-start(bf16[512,2176]{1,0:T(8,128)(2,1)} %get-tuple-element.122), channel_id=1, source_target_pairs={{0,1},{1,0},{2,3},{3,2},{4,5},{5,4},{6,7},{7,6},{8,9},{9,8},{10,11... | collective-permute-start | bytes 6684680 | tf_op jit(solution)/shard_map/ppermute | solution.py:279

commit v3 on v2

--- a/solution.py
+++ b/solution.py
@@ -22,7 +22,8 @@
 NT = (((1,), (1,)), ((), ()))
 TN = (((0,), (0,)), ((), ()))
 NN = (((1,), (0,)), ((), ()))
-VMEM_LIMIT = 56 * 1024 * 1024
+MIB = 1024 * 1024
+GRADIENT_ROOM = 36
 
 
 def mm(a, b, dims=NN):
@@ -44,13 +45,13 @@
     return mm(split(pltpu.roll(table, 128 - base, 1)), matrix)
 
 
-def call(kernel, name, out_shape, grid_spec, flops, nbytes):
+def call(kernel, name, out_shape, grid_spec, flops, nbytes, room=24):
     return pl.pallas_call(
         kernel,
         out_shape=out_shape,
         grid_spec=grid_spec,
         name=name,
-        compiler_params=pltpu.CompilerParams(vmem_limit_bytes=VMEM_LIMIT),
+        compiler_params=pltpu.CompilerParams(vmem_limit_bytes=room * MIB),
         cost_estimate=pl.CostEstimate(flops=flops, bytes_accessed=nbytes, transcendentals=0),
     )
 
@@ -223,7 +224,7 @@
 
 def gradient_kernel(
     core, fill, cot, taken, inner, up, keys, cols, ro, gi, pair, starts, push_out, gains, enter,
-    keep, give, acc_in, acc_out, left, right, masked, finish, matrix,
+    keep, give, acc_in, acc_out, left, right, masked, took, finish, matrix,
 ):
     step = pl.program_id(0)
     last = pl.num_programs(0) - 1
@@ -235,28 +236,31 @@
         acc_in[...] = jnp.zeros_like(acc_in)
         acc_out[...] = jnp.zeros_like(acc_out)
 
-    for n in (1, 0):
-        at = slice(n * BLOCK, n * BLOCK + BLOCK)
-        factor, before = gains[n, 0:1], gains[n, 8:9]
-        start = (starts[n] + before * enter[:64].astype(F32)).astype(BF16)
-        end = finish[...].astype(BF16)
-        finish[...] = finish[...] * factor + push_out[n]
-        table = cols[at]
-        opening = spread(table, OPEN, matrix[...])
-        closing = spread(table, CLOSE, matrix[...])
-        k = keys[at]
-        write, read = k[:, :STATE], k[:, STATE:]
-        left[at] = (ro[at].astype(F32) + opening * mm(read, start)).astype(BF16)
-        masked[at] = jnp.where(valid_rows(fill[2 * (last - step) + n], D), cot[0, at], jnp.zeros((), BF16))
-        right[at, :D] = (gi[at].astype(F32) + closing * mm(write, end)).astype(BF16)
-        into = (closing * inner[at].astype(F32)).astype(BF16)
-        out = (opening * up[at].astype(F32)).astype(BF16)
-        g = pair[n]
-        grad_write = mm(g, read, TN) + mm(into, end, NT)
-        grad_read = mm(g, write) + mm(out, start, NT)
-        right[at, D:] = jnp.concatenate([grad_write, grad_read], axis=1).astype(BF16)
-    acc_out[...] += mm(left[...], masked[...], TN).reshape(acc_out.shape)
-    acc_in[...] += mm(taken[...], right[...], TN).reshape(acc_in.shape)
+    at = pl.ds(pl.multiple_of((step & 1) * BLOCK, BLOCK), BLOCK)
+    factor, before = gains[0, 0:1], gains[0, 8:9]
+    start = (starts[0] + before * enter[:64].astype(F32)).astype(BF16)
+    end = finish[...].astype(BF16)
+    finish[...] = finish[...] * factor + push_out[0]
+    table = cols[...]
+    opening = spread(table, OPEN, matrix[...])
+    closing = spread(table, CLOSE, matrix[...])
+    k = keys[...]
+    write, read = k[:, :STATE], k[:, STATE:]
+    left[at] = (ro[...].astype(F32) + opening * mm(read, start)).astype(BF16)
+    masked[at] = jnp.where(valid_rows(fill[last - step], D), cot[0], jnp.zeros((), BF16))
+    took[at] = taken[...]
+    right[at, :D] = (gi[...].astype(F32) + closing * mm(write, end)).astype(BF16)
+    into = (closing * inner[...].astype(F32)).astype(BF16)
+    out = (opening * up[...].astype(F32)).astype(BF16)
+    g = pair[0]
+    grad_write = mm(g, read, TN) + mm(into, end, NT)
+    grad_read = mm(g, write) + mm(out, start, NT)
+    right[at, D:] = jnp.concatenate([grad_write, grad_read], axis=1).astype(BF16)
+
+    @pl.when((step & 1) == 1)
+    def _():
+        acc_out[...] += mm(left[...], masked[...], TN).reshape(acc_out.shape)
+        acc_in[...] += mm(took[...], right[...], TN).reshape(acc_in.shape)
 
     @pl.when(step == last)
     def _():
@@ -427,7 +431,7 @@
             ),
             input_output_aliases={5 + number + 5 + n: n for n in range(len(kept))},
             name=f"stage_{s}",
-            compiler_params=pltpu.CompilerParams(vmem_limit_bytes=VMEM_LIMIT),
+            compiler_params=pltpu.CompilerParams(vmem_limit_bytes=32 * MIB),
             cost_estimate=pl.CostEstimate(
                 flops=4 * BLOCK * D * (D + 1024) + 4 * HEADS * 3 * BLOCK**3,
                 bytes_accessed=16 << 20,
@@ -469,10 +473,8 @@
     enter = lax.all_to_all(entering, TM, 0, 0).reshape(128, D)
 
     own_core = core.reshape(1)
-    two = lambda width: pl.BlockSpec((2 * BLOCK, width), lambda b, *_: (b, 0))
-    pairs = lambda *dims: pl.BlockSpec((2, *dims), lambda b, *_: (b, 0, 0))
     back = lambda spec: pl.BlockSpec(
-        spec.block_shape, lambda s, *refs: spec.index_map(blocks // 2 - 1 - s, *refs)
+        spec.block_shape, lambda s, *refs: spec.index_map(blocks - 1 - s, *refs)
     )
     wide = D + 128
     both = wide + D
@@ -482,22 +484,22 @@
         (shape((D // 2, both), F32), shape((D // 2, both), BF16)),
         pltpu.PrefetchScalarGridSpec(
             num_scalar_prefetch=2,
-            grid=(blocks // 2,),
+            grid=(blocks,),
             in_specs=[
                 back(s)
                 for s in (
-                    pl.BlockSpec((1, 2 * BLOCK, D), lambda b, *_: (0, b, 0)),
-                    two(D),
-                    two(D),
-                    two(D),
-                    two(128),
-                    two(128),
-                    two(D),
-                    two(D),
-                    pairs(BLOCK, BLOCK),
-                    pairs(STATE, D),
-                    pairs(STATE, D),
-                    pairs(16, D),
+                    pl.BlockSpec((1, BLOCK, D), lambda b, *_: (0, b, 0)),
+                    tall(D),
+                    tall(D),
+                    tall(D),
+                    tall(128),
+                    tall(128),
+                    tall(D),
+                    tall(D),
+                    lead(BLOCK, BLOCK),
+                    lead(STATE, D),
+                    lead(STATE, D),
+                    lead(16, D),
                     whole(128, D),
                 )
             ],
@@ -508,12 +510,14 @@
                 vmem(BF16, 2 * BLOCK, D),
                 vmem(BF16, 2 * BLOCK, wide),
                 vmem(BF16, 2 * BLOCK, D),
+                vmem(BF16, 2 * BLOCK, D),
                 vmem(F32, STATE, D),
                 vmem(BF16, 256, D),
             ],
         ),
         2 * steps * D * (2 * D + 1280),
         36 << 20,
+        room=GRADIENT_ROOM,
     )(own_core, fill, cotangent, taken, inner, up, keys, cols, ro, gi, pair, starts, push_out, gains, enter)
 
     grads = over_chips(over_chip(keep, give))

time: 219 us -> 221 us (level)
  Pallas kernels: 93.3 us -> 76.3 us
  local copies, waits for them, and re-layouts: 9.03 us -> 21.2 us
  waiting for transfers between devices: 38.7 us -> 44.2 us
  blocking collectives: 49.9 us -> 53.4 us
    unnamed x24 -> x42, local copies, waits for them, and re-layouts: 2.77 us -> 16.1 us
    pallas_call x3, Pallas kernels: 49.2 us -> 39.5 us  [on_device(): pl.pallas_call(body, out_shape=(shape((room, D), BF16), shape((room, D),...]
    ppermute x3, waiting for transfers between devices: 18.3 us -> 23.9 us  [on_device(): up_z = lambda v: lax.ppermute(v, 'z', ring('z', 1))]
    all_to_all x1, blocking collectives: 37 us -> 41.8 us  [over_chips(): return lax.all_to_all(half, CHIPS, 0, 0).astype(F32).sum(0)]
    pallas_call x1, Pallas kernels: 11.6 us -> 7.47 us  [on_device(): call(upstream_kernel, 'upstream', (shape((steps, D), BF16), shape((32, st...]
    pallas_call x1, Pallas kernels: 3.86 us -> 1 us  [on_device(): call(local_kernel, 'local', (shape((blocks, STATE, D), F32), shape((block...]
  transfers between devices with their start and end apart: 15 -> 15, of which waited for: 8 -> 8; matrix products, arithmetic and copies ran while one was open for 2% -> 2% of each run, Pallas kernels for 20% -> 17%
where the time goes in v3:
time: 221 us
  Pallas kernels  76.3 us (35%)
  blocking collectives  53.4 us (24%)
  waiting for transfers between devices  44.2 us (20%)
  local copies, waits for them, and re-layouts  21.2 us (10%)
  starting transfers between devices  19.3 us (9%)
  other arithmetic  6.01 us (3%)
    all_to_all x1, blocking collectives, over_chips(): return lax.all_to_all(half, CHIPS, 0, 0).astype(F32).sum(0)  41.8 us
    pallas_call x3, Pallas kernels, on_device(): pl.pallas_call(body, out_shape=(shape((room, D), BF16), shape((room, D),...  39.5 us
    pallas_call x1, Pallas kernels, on_device(): call(gradient_kernel, 'gradient', (shape((D // 2, both), F32), shape((D /...  27.1 us
    ppermute x3, waiting for transfers between devices, on_device(): up_z = lambda v: lax.ppermute(v, 'z', ring('z', 1))  23.9 us
    unnamed x42, local copies, waits for them, and re-layouts  16.1 us
    all_to_all x1, waiting for transfers between devices, on_device(): terms = lax.all_to_all(total, TM, 0, 0)  11.9 us
    all_to_all x1, blocking collectives, on_device(): enter = lax.all_to_all(entering, TM, 0, 0).reshape(128, D)  11.6 us
    pallas_call x1, Pallas kernels, on_device(): call(upstream_kernel, 'upstream', (shape((steps, D), BF16), shape((32, st...  7.47 us
  transfers between devices with their start and end apart: 15, of which 8 were waited for; matrix products, arithmetic and copies ran while one was open for 2% of the time, Pallas kernels for 17%

profile of v3, /device:TPU:0, one launch (start us, length us, event | category | flops | bytes accessed | tf_op | source)
XLA Modules:
  0.0 221.2 jit_solution(12034454577044972812)
XLA Ops:
  0.6 0.0 copy-start.7
  0.7 3.3 %fusion.12 = (bf16[1,1,512,1024]{3,2,1,0:T(8,128)(2,1)}, bf16[1,1,512,1024]{3,2,1,0:T(8,128)(2,1)}) fusion(bf16[1,1,1024,1024]{3,2,1,0:T(8,128)(2,1)} %param.10), kind=kLoop, calls=%fused_computation.67 | loop fusion | bytes 4194304 | tf_op jit(solution)/shard_map/slice | solution.py:308
  3.9 2.0 collective-permute-start
  5.9 2.1 collective-permute-start.1
  8.1 0.0 collective-permute-start.4
  8.1 0.7 compare_select_fusion.11
  8.7 0.7 fusion.11
  9.5 0.7 fusion.10
  10.2 0.1 convert_reduce_fusion.2
  10.3 0.1 iota_minimum_fusion
  10.4 0.2 convert_reduce_fusion.1
  10.6 0.3 select_reduce_fusion
  10.9 0.1 broadcast_select_fusion
  11.0 0.0 copy-done.20
  11.0 0.0 copy-start.12
  11.0 2.2 copy-done.12
  13.2 1.6 copy-done.14
  14.8 7.5 %upstream.1 = (bf16[2048,1024]{1,0:T(8,128)(2,1)S(1)}, f32[32,2048]{1,0:T(8,128)S(1)}, f32[2048,128]{1,0:T(8,128)S(1)}, f32[8,8,128]{2,1,0:T(8,128)S(1)}) custom-call(s32[8]{0:T(128)S(1)} %bitcast.64, f32[16,2048]{1,0:T(8,128)S(1)} %bitcast.69, s32[8,1,256]{2,1,0:T(1,128)S(1)} %bitcast.70, bf16[1,2048,1024]{2,1,0:T(8,128)(2,1)S(1)} %copy-done.12, ...), custom_call_target="tpu_custom_call" | custom-call | flops 4294967296 | bytes 12582912 | tf_op jit(solution)/shard_map/upstream/pallas_call | solution.py:338
  22.3 9.3 %collective-permute-done.refs_0_ = bf16[2,256,1024]{2,1,0:T(8,128)(2,1)} collective-permute-done((bf16[2,256,1024]{2,1,0:T(8,128)(2,1)}, bf16[2,256,1024]{2,1,0:T(8,128)(2,1)}, u32[]{:S(2)}, u32[]{:S(2)}) %collective-permute-start) | collective-permute-done | bytes 1048608 | tf_op jit(solution)/shard_map/ppermute | solution.py:306
  31.5 0.0 collective-permute-done.1.refs_1_
  31.5 1.3 collective-permute-start.2
  32.8 2.0 collective-permute-start.3
  34.8 0.1 collective-permute-start.7
  34.9 0.6 fusion.14
  35.5 0.5 collective-permute-start.8
  36.0 0.0 collective-permute-done.4.refs_1_
  36.0 10.8 %stage_0.1 = (bf16[2304,1024]{1,0:T(8,128)(2,1)}, bf16[2304,1024]{1,0:T(8,128)(2,1)}, bf16[2304,128]{1,0:T(8,128)(2,1)S(1)}, bf16[2304,1024]{1,0:T(8,128)(2,1)},...) custom-call(s32[8]{0:T(128)S(1)} %get-tuple-element.139.block, ...), custom_call_target="tpu_custom_call" | custom-call | flops 5368709120 | bytes 16777216 | tf_op jit(solution)/shard_map/stage_0/pallas_call | solution.py:396
  46.8 10.5 %collective-permute-done.2.refs_4_ = bf16[2,256,1024]{2,1,0:T(8,128)(2,1)S(1)} collective-permute-done((bf16[2,256,1024]{2,1,0:T(8,128)(2,1)}, bf16[2,256,1024]{2,1,0:T(8,128)(2,1)S(1)}, u32[]{:S(2)}, u32[]{:S(2)}) %collective-permute-start.2) | collective-permute-done | bytes 1048608 | tf_op jit(solution)/shard_map/ppermute | solution.py:306
  57.3 0.0 collective-permute-done.3.refs_5_
  57.3 0.0 collective-permute-start.10
  57.3 0.5 collective-permute-start.9
  57.8 0.8 collective-permute-start.5
  58.6 0.0 collective-permute-done.7.refs_2_
  58.6 2.4 %collective-permute-start.6 = (bf16[2,256,1024]{2,1,0:T(8,128)(2,1)}, bf16[2,256,1024]{2,1,0:T(8,128)(2,1)S(1)}, u32[]{:S(2)}, u32[]{:S(2)}) collective-permute-start(bf16[2,256,1024]{2,1,0:T(8,128)(2,1)} %collective-permute-done.1.refs_1_), channel_id=1, source_target_pairs={{0,6},{2,0},{4,2},{6,4},{1,7},{3,1},{5,3},{7,5},{8,14},{10,8},{12,... | collective-permute-start | bytes 3145736 | tf_op jit(solution)/shard_map/ppermute | solution.py:307
  61.1 0.4 collective-permute-done.9.refs_6_
  61.5 18.7 %stage_1.1 = (bf16[2304,1024]{1,0:T(8,128)(2,1)}, bf16[2304,1024]{1,0:T(8,128)(2,1)}, bf16[2304,128]{1,0:T(8,128)(2,1)S(1)}, bf16[2304,1024]{1,0:T(8,128)(2,1)},...) custom-call(s32[8]{0:T(128)S(1)} %get-tuple-element.138.block, ...), custom_call_target="tpu_custom_call", output_to_operand_aliasing={{0}: (18, {}), {1}: (19, {}), {2}: (20, {}), {3}: (21, {}),... | custom-call | flops 5368709120 | bytes 16777216 | tf_op jit(solution)/shard_map/stage_1/pallas_call | solution.py:396
  80.2 4.1 %collective-permute-done.5.refs_0_ = bf16[2,256,1024]{2,1,0:T(8,128)(2,1)S(1)} collective-permute-done((bf16[2,256,1024]{2,1,0:T(8,128)(2,1)}, bf16[2,256,1024]{2,1,0:T(8,128)(2,1)S(1)}, u32[]{:S(2)}, u32[]{:S(2)}) %collective-permute-start.5) | collective-permute-done | bytes 1048608 | tf_op jit(solution)/shard_map/ppermute | solution.py:306
  84.3 0.0 collective-permute-done.6.refs_1_
  84.3 0.0 collective-permute-start.11
  84.3 0.5 collective-permute-start.12
  84.8 2.1 collective-permute-done.11.refs_2_
  87.0 1.5 collective-permute-done.12.refs_3_
  88.5 9.9 %stage_2.1 = (bf16[2304,1024]{1,0:T(8,128)(2,1)}, bf16[2304,1024]{1,0:T(8,128)(2,1)}, bf16[2304,128]{1,0:T(8,128)(2,1)S(1)}, bf16[2304,1024]{1,0:T(8,128)(2,1)},...) custom-call(s32[8]{0:T(128)S(1)} %get-tuple-element.140.block, ...), custom_call_target="tpu_custom_call", output_to_operand_aliasing={{0}: (14, {}), {1}: (15, {}), {2}: (16, {}), {3}: (17, {}),... | custom-call | flops 5368709120 | bytes 16777216 | tf_op jit(solution)/shard_map/stage_2/pallas_call | solution.py:396
  98.4 1.0 local.1
  99.4 0.8 copy-done.10
  100.2 1.4 copy-done.15
  101.6 0.8 copy-done.17
  102.4 7.1 %all-to-all-start = ((bf16[16,16,1024]{2,1,0:T(8,128)(2,1)}), bf16[16,16,1024]{2,1,0:T(8,128)(2,1)}, u32[]{:S(2)}, u32[]{:S(2)}) async-start(bf16[16,16,1024]{2,1,0:T(8,128)(2,1)} %copy-done.10), calls=%async_computation | async-start | bytes 1048576 | tf_op jit(solution)/shard_map/all_to_all | solution.py:458
  109.5 11.9 %all-to-all-done.terms = bf16[16,16,1024]{2,1,0:T(8,128)(2,1)} async-done(((bf16[16,16,1024]{2,1,0:T(8,128)(2,1)}), bf16[16,16,1024]{2,1,0:T(8,128)(2,1)}, u32[]{:S(2)}, u32[]{:S(2)}) %all-to-all-start) | async-done | bytes 524320 | tf_op jit(solution)/shard_map/all_to_all | solution.py:458
  121.4 1.3 scan.1
  122.7 11.6 %all_to_all.15 = bf16[16,8,1024]{2,1,0:T(8,128)(2,1)S(1)} all-to-all(bf16[16,8,1024]{2,1,0:T(8,128)(2,1)S(1)} %scan.1), channel_id=1, replica_groups=mesh['y'=4,'x'=4,'z'=4,'c'=2] {'y','x'}, dimensions={0} | all-to-all | bytes 524288 | tf_op jit(solution)/shard_map/all_to_all | solution.py:473
  134.3 2.2 copy-done.1
  136.5 1.2 copy-done.4
  137.7 1.1 copy-done.6
  138.8 2.2 copy-done.13
  141.0 1.6 copy-done.16
  142.6 1.0 copy-done.18
  143.6 27.1 %gradient.1 = (f32[512,2176]{1,0:T(8,128)}, bf16[512,2176]{1,0:T(8,128)(2,1)S(1)}) custom-call(s32[1]{0:T(128)} %bitcast.core, s32[8]{0:T(128)S(1)} %bitcast.68, bf16[1,2048,1024]{2,1,0:T(8,128)(2,1)S(1)} %copy-done.13, bf16[2304,1024]{1,0:T(8,128)(2,1)} %get-tuple-element.109.taken, bf16[2304,1024]{1,0:T(8,128)(2,1)} %get-tuple-element.110.inner, ...), custom_call_target="tpu_custom_call" | custom-call | flops 13958643712 | bytes 37748736 | tf_op jit(solution)/shard_map/gradient/pallas_call | solution.py:481
  170.7 4.3 %collective-permute-done.13 = bf16[512,2176]{1,0:T(8,128)(2,1)S(1)} collective-permute-done((bf16[512,2176]{1,0:T(8,128)(2,1)S(1)}, bf16[512,2176]{1,0:T(8,128)(2,1)S(1)}, u32[]{:S(2)}, u32[]{:S(2)}) %collective-permute-start.13) | collective-permute-done | bytes 2228256 | tf_op jit(solution)/shard_map/ppermute | solution.py:283
  175.1 2.8 %fusion = bf16[64,8,2176]{2,1,0:T(8,128)(2,1)S(1)} fusion(f32[512,2176]{1,0:T(8,128)} %get-tuple-element.121, bf16[512,2176]{1,0:T(8,128)(2,1)S(1)} %collective-permute-done.13), kind=kLoop, calls=%fused_computation.2 | loop fusion | flops 3342336 | bytes 8912896 | tf_op jit(solution)/shard_map/reshape | solution.py:285
  177.9 41.8 %all_to_all.16 = bf16[64,8,2176]{2,1,0:T(8,128)(2,1)S(1)} all-to-all(bf16[64,8,2176]{2,1,0:T(8,128)(2,1)S(1)} %fusion), channel_id=1, replica_groups=mesh['y'=4,'x'=4,'z'=4,'c'=2] {'y','x','z'}, dimensions={0} | all-to-all | bytes 4456448 | tf_op jit(solution)/shard_map/all_to_all | solution.py:289
  219.7 0.3 convert_reduce_fusion
  220.0 0.6 fusion.13
  220.6 0.6 slice.77
  (36 shorter events, 0.1 us)
Async XLA Ops:
  0.6 7.4 %copy-start.7 = (bf16[1,1,1024,1024]{3,2,1,0:T(8,128)(2,1)S(1)}, bf16[1,1,1024,1024]{3,2,1,0:T(8,128)(2,1)}, u32[]{:S(2)}) copy-start(bf16[1,1,1024,1024]{3,2,1,0:T(8,128)(2,1)} %param.10) | copy-start | bytes 6291460
  0.6 10.3 %copy-start.11 = (s32[1,1,8]{2,1,0:T(1,128)S(1)}, s32[1,1,8]{2,1,0:T(1,128)}, u32[]{:S(2)}) copy-start(s32[1,1,8]{2,1,0:T(1,128)} %param.13) | copy-start | bytes 100
  0.7 10.3 %copy-start.19 = (f32[1,16,2048]{2,1,0:T(8,128)S(1)}, f32[1,16,2048]{2,1,0:T(8,128)}, u32[]{:S(2)}) copy-start(f32[1,16,2048]{2,1,0:T(8,128)} %param.14) | copy-start | bytes 393220
  0.7 10.3 %copy-start.20 = (s32[1,2048]{1,0:T(1,128)S(1)}, s32[1,2048]{1,0:T(1,128)}, u32[]{:S(2)}) copy-start(s32[1,2048]{1,0:T(1,128)} %param.15) | copy-start | bytes 24580
  3.9 27.6 %collective-permute-start = (bf16[2,256,1024]{2,1,0:T(8,128)(2,1)}, bf16[2,256,1024]{2,1,0:T(8,128)(2,1)}, u32[]{:S(2)}, u32[]{:S(2)}) collective-permute-start(bf16[2,256,1024]{2,1,0:T(8,128)(2,1)} %bitcast.9), channel_id=1, source_target_pairs={{0,2},{2,4},{4,6},{6,0},{1,3},{3,5},{5,7},{7,1},{8,10},{10,12},{12... | collective-permute-start | bytes 3145736 | tf_op jit(solution)/shard_map/ppermute | solution.py:306
  5.9 25.6 %collective-permute-start.1 = (bf16[2,256,1024]{2,1,0:T(8,128)(2,1)}, bf16[2,256,1024]{2,1,0:T(8,128)(2,1)}, u32[]{:S(2)}, u32[]{:S(2)}) collective-permute-start(bf16[2,256,1024]{2,1,0:T(8,128)(2,1)} %bitcast.10), channel_id=1, source_target_pairs={{0,6},{2,0},{4,2},{6,4},{1,7},{3,1},{5,3},{7,5},{8,14},{10,8},{12,... | collective-permute-start | bytes 3145736 | tf_op jit(solution)/shard_map/ppermute | solution.py:307
  8.1 27.9 %collective-permute-start.4 = (bf16[4,256,1024]{2,1,0:T(8,128)(2,1)S(1)}, bf16[4,256,1024]{2,1,0:T(8,128)(2,1)}, u32[]{:S(2)}, u32[]{:S(2)}) collective-permute-start(bf16[4,256,1024]{2,1,0:T(8,128)(2,1)S(1)} %bitcast.61), channel_id=1, source_target_pairs={{0,1},{1,0},{2,3},{3,2},{4,5},{5,4},{6,7},{7,6},{8,9},{9,8},{10,11... | collective-permute-start | bytes 6291464 | tf_op jit(solution)/shard_map/ppermute | solution.py:305
  11.0 2.2 copy-start.12
  13.2 1.6 copy-start.14
  14.8 21.2 %copy-start.2 = (bf16[1024,1024]{1,0:T(8,128)(2,1)S(1)}, bf16[1024,1024]{1,0:T(8,128)(2,1)}, u32[]{:S(2)}) copy-start(bf16[1024,1024]{1,0:T(8,128)(2,1)} %refs_4_.1) | copy-start | bytes 6291460
  14.8 21.2 %copy-start.8 = (bf16[1,1,1024,1024]{3,2,1,0:T(8,128)(2,1)S(1)}, bf16[1,1,1024,1024]{3,2,1,0:T(8,128)(2,1)}, u32[]{:S(2)}) copy-start(bf16[1,1,1024,1024]{3,2,1,0:T(8,128)(2,1)} %param.10) | copy-start | bytes 6291460
  14.8 21.2 %copy-start.9 = (bf16[1024,128]{1,0:T(8,128)(2,1)S(1)}, bf16[1024,128]{1,0:T(8,128)(2,1)}, u32[]{:S(2)}) copy-start(bf16[1024,128]{1,0:T(8,128)(2,1)} %refs_5_.1) | copy-start | bytes 786436
  22.3 66.2 %copy-start = (bf16[2048,1024]{1,0:T(8,128)(2,1)}, bf16[2048,1024]{1,0:T(8,128)(2,1)S(1)}, u32[]{:S(2)}) copy-start(bf16[2048,1024]{1,0:T(8,128)(2,1)S(1)} %get-tuple-element.68.refs_4_.refs_10_.refs_6_.up) | copy-start | bytes 12582916
  22.3 66.2 %copy-start.3 = (f32[2048,128]{1,0:T(8,128)}, f32[2048,128]{1,0:T(8,128)S(1)}, u32[]{:S(2)}) copy-start(f32[2048,128]{1,0:T(8,128)S(1)} %get-tuple-element.70.refs_6_.refs_12_.refs_8_.cols) | copy-start | bytes 3145732
  31.5 25.8 %collective-permute-start.2 = (bf16[2,256,1024]{2,1,0:T(8,128)(2,1)}, bf16[2,256,1024]{2,1,0:T(8,128)(2,1)S(1)}, u32[]{:S(2)}, u32[]{:S(2)}) collective-permute-start(bf16[2,256,1024]{2,1,0:T(8,128)(2,1)} %bitcast.10), channel_id=1, source_target_pairs={{0,2},{2,4},{4,6},{6,0},{1,3},{3,5},{5,7},{7,1},{8,10},{10,12},{12... | collective-permute-start | bytes 3145736 | tf_op jit(solution)/shard_map/ppermute | solution.py:306
  32.8 24.5 %collective-permute-start.3 = (bf16[2,256,1024]{2,1,0:T(8,128)(2,1)}, bf16[2,256,1024]{2,1,0:T(8,128)(2,1)S(1)}, u32[]{:S(2)}, u32[]{:S(2)}) collective-permute-start(bf16[2,256,1024]{2,1,0:T(8,128)(2,1)} %bitcast.9), channel_id=1, source_target_pairs={{0,6},{2,0},{4,2},{6,4},{1,7},{3,1},{5,3},{7,5},{8,14},{10,8},{12,... | collective-permute-start | bytes 3145736 | tf_op jit(solution)/shard_map/ppermute | solution.py:307
  34.8 23.9 %collective-permute-start.7 = (bf16[2,256,1024]{2,1,0:T(8,128)(2,1)}, bf16[2,256,1024]{2,1,0:T(8,128)(2,1)S(1)}, u32[]{:S(2)}, u32[]{:S(2)}) collective-permute-start(bf16[2,256,1024]{2,1,0:T(8,128)(2,1)} %collective-permute-done.refs_0_), channel_id=1, source_target_pairs={{0,1},{1,0},{2,3},{3,2},{4,5},{5,4},{6,7},{7,6},{8,9},{9,8},{10,11... | collective-permute-start | bytes 3145736 | tf_op jit(solution)/shard_map/ppermute | solution.py:305
  35.5 25.6 %collective-permute-start.8 = (bf16[2,256,1024]{2,1,0:T(8,128)(2,1)}, bf16[2,256,1024]{2,1,0:T(8,128)(2,1)S(1)}, u32[]{:S(2)}, u32[]{:S(2)}) collective-permute-start(bf16[2,256,1024]{2,1,0:T(8,128)(2,1)} %collective-permute-done.1.refs_1_), channel_id=1, source_target_pairs={{0,1},{1,0},{2,3},{3,2},{4,5},{5,4},{6,7},{7,6},{8,9},{9,8},{10,11... | collective-permute-start | bytes 3145736 | tf_op jit(solution)/shard_map/ppermute | solution.py:305
  57.3 3.8 %collective-permute-start.10 = (bf16[2,256,1024]{2,1,0:T(8,128)(2,1)S(1)}, bf16[2,256,1024]{2,1,0:T(8,128)(2,1)S(1)}, u32[]{:S(2)}, u32[]{:S(2)}) collective-permute-start(bf16[2,256,1024]{2,1,0:T(8,128)(2,1)S(1)} %collective-permute-done.3.refs_5_), channel_id=1, source_target_pairs={{0,1},{1,0},{2,3},{3,2},{4,5},{5,4},{6,7},{7,6},{8,9},{9,8},{10,11... | collective-permute-start | bytes 3145736 | tf_op jit(solution)/shard_map/ppermute | solution.py:305
  57.3 4.2 %collective-permute-start.9 = (bf16[2,256,1024]{2,1,0:T(8,128)(2,1)S(1)}, bf16[2,256,1024]{2,1,0:T(8,128)(2,1)S(1)}, u32[]{:S(2)}, u32[]{:S(2)}) collective-permute-start(bf16[2,256,1024]{2,1,0:T(8,128)(2,1)S(1)} %collective-permute-done.2.refs_4_), channel_id=1, source_target_pairs={{0,1},{1,0},{2,3},{3,2},{4,5},{5,4},{6,7},{7,6},{8,9},{9,8},{10,11... | collective-permute-start | bytes 3145736 | tf_op jit(solution)/shard_map/ppermute | solution.py:305
  57.8 26.5 %collective-permute-start.5 = (bf16[2,256,1024]{2,1,0:T(8,128)(2,1)}, bf16[2,256,1024]{2,1,0:T(8,128)(2,1)S(1)}, u32[]{:S(2)}, u32[]{:S(2)}) collective-permute-start(bf16[2,256,1024]{2,1,0:T(8,128)(2,1)} %collective-permute-done.refs_0_), channel_id=1, source_target_pairs={{0,2},{2,4},{4,6},{6,0},{1,3},{3,5},{5,7},{7,1},{8,10},{10,12},{12... | collective-permute-start | bytes 3145736 | tf_op jit(solution)/shard_map/ppermute | solution.py:306
  58.6 25.7 %collective-permute-start.6 = (bf16[2,256,1024]{2,1,0:T(8,128)(2,1)}, bf16[2,256,1024]{2,1,0:T(8,128)(2,1)S(1)}, u32[]{:S(2)}, u32[]{:S(2)}) collective-permute-start(bf16[2,256,1024]{2,1,0:T(8,128)(2,1)} %collective-permute-done.1.refs_1_), channel_id=1, source_target_pairs={{0,6},{2,0},{4,2},{6,4},{1,7},{3,1},{5,3},{7,5},{8,14},{10,8},{12,... | collective-permute-start | bytes 3145736 | tf_op jit(solution)/shard_map/ppermute | solution.py:307
  84.3 2.7 %collective-permute-start.11 = (bf16[2,256,1024]{2,1,0:T(8,128)(2,1)S(1)}, bf16[2,256,1024]{2,1,0:T(8,128)(2,1)S(1)}, u32[]{:S(2)}, u32[]{:S(2)}) collective-permute-start(bf16[2,256,1024]{2,1,0:T(8,128)(2,1)S(1)} %collective-permute-done.5.refs_0_), channel_id=1, source_target_pairs={{0,1},{1,0},{2,3},{3,2},{4,5},{5,4},{6,7},{7,6},{8,9},{9,8},{10,11... | collective-permute-start | bytes 3145736 | tf_op jit(solution)/shard_map/ppermute | solution.py:305
  84.3 4.2 %collective-permute-start.12 = (bf16[2,256,1024]{2,1,0:T(8,128)(2,1)S(1)}, bf16[2,256,1024]{2,1,0:T(8,128)(2,1)S(1)}, u32[]{:S(2)}, u32[]{:S(2)}) collective-permute-start(bf16[2,256,1024]{2,1,0:T(8,128)(2,1)S(1)} %collective-permute-done.6.refs_1_), channel_id=1, source_target_pairs={{0,1},{1,0},{2,3},{3,2},{4,5},{5,4},{6,7},{7,6},{8,9},{9,8},{10,11... | collective-permute-start | bytes 3145736 | tf_op jit(solution)/shard_map/ppermute | solution.py:305
  98.4 1.0 copy-start.5
  99.4 0.8 copy-start.10
  100.2 1.4 copy-start.15
  101.6 0.8 copy-start.17
  102.4 19.0 %all-to-all-start = ((bf16[16,16,1024]{2,1,0:T(8,128)(2,1)}), bf16[16,16,1024]{2,1,0:T(8,128)(2,1)}, u32[]{:S(2)}, u32[]{:S(2)}) async-start(bf16[16,16,1024]{2,1,0:T(8,128)(2,1)} %copy-done.10), calls=%async_computation | async-start | bytes 1048576 | tf_op jit(solution)/shard_map/all_to_all | solution.py:458
  134.3 2.2 copy-start.1
  136.5 1.2 copy-start.4
  137.7 1.1 copy-start.6
  138.8 2.2 copy-start.13
  141.0 1.6 copy-start.16
  142.6 1.0 copy-start.18
  170.7 4.3 %collective-permute-start.13 = (bf16[512,2176]{1,0:T(8,128)(2,1)S(1)}, bf16[512,2176]{1,0:T(8,128)(2,1)S(1)}, u32[]{:S(2)}, u32[]{:S(2)}) collective-permute-start(bf16[512,2176]{1,0:T(8,128)(2,1)S(1)} %get-tuple-element.122), channel_id=1, source_target_pairs={{0,1},{1,0},{2,3},{3,2},{4,5},{5,4},{6,7},{7,6},{8,9},{9,8},{10,11... | collective-permute-start | bytes 6684680 | tf_op jit(solution)/shard_map/ppermute | solution.py:283

commit v4 on v3

--- a/solution.py
+++ b/solution.py
@@ -23,7 +23,7 @@
 TN = (((0,), (0,)), ((), ()))
 NN = (((1,), (0,)), ((), ()))
 MIB = 1024 * 1024
-GRADIENT_ROOM = 36
+GRADIENT_ROOM = 56
 
 
 def mm(a, b, dims=NN):
@@ -259,14 +259,15 @@
 
     @pl.when((step & 1) == 1)
     def _():
-        acc_out[...] += mm(left[...], masked[...], TN).reshape(acc_out.shape)
-        acc_in[...] += mm(took[...], right[...], TN).reshape(acc_in.shape)
+        acc_out[...] += mm(left[...], masked[...], TN)
+        acc_in[...] += mm(took[...], right[...], TN)
 
     @pl.when(step == last)
     def _():
         scale = 1.0 / 512.0
         for acc, columns in ((acc_in, slice(0, D + 128)), (acc_out, slice(D + 128, None))):
-            mine, other = acc[:, core[0]] * scale, acc[:, 1 - core[0]] * scale
+            halves = acc.reshape(D // 16, 2, 8, acc.shape[1])
+            mine, other = halves[:, core[0]] * scale, halves[:, 1 - core[0]] * scale
             keep[:, columns] = mine.reshape(keep.shape[0], -1)
             give[:, columns] = other.reshape(give.shape[0], -1).astype(BF16)
 
@@ -505,8 +506,8 @@
             ],
             out_specs=[whole(D // 2, both), whole(D // 2, both)],
             scratch_shapes=[
-                vmem(F32, D // 16, 2, 8, wide),
-                vmem(F32, D // 16, 2, 8, D),
+                vmem(F32, D, wide),
+                vmem(F32, D, D),
                 vmem(BF16, 2 * BLOCK, D),
                 vmem(BF16, 2 * BLOCK, wide),
                 vmem(BF16, 2 * BLOCK, D),

time: 221 us -> 214 us (0.968)
  local copies, waits for them, and re-layouts: 21.2 us -> 10.7 us
  Pallas kernels: 76.3 us -> 80.4 us
  waiting for transfers between devices: 44.2 us -> 40.9 us
  starting transfers between devices: 19.3 us -> 22.5 us
    unnamed x42 -> x32, local copies, waits for them, and re-layouts: 16.1 us -> 5.93 us
    pallas_call x1, Pallas kernels: 27.1 us -> 31.1 us  [on_device(): call(gradient_kernel, 'gradient', (shape((D // 2, both), F32), shape((D /...]
    ppermute x3, waiting for transfers between devices: 23.9 us -> 20.2 us  [on_device(): up_z = lambda v: lax.ppermute(v, 'z', ring('z', 1))]
    all_to_all x1, starting transfers between devices: 7.07 us -> 10.2 us  [on_device(): terms = lax.all_to_all(total, TM, 0, 0)]
  transfers between devices with their start and end apart: 15 -> 15, of which waited for: 8 -> 8; matrix products, arithmetic and copies ran while one was open for 2% -> 2% of each run, Pallas kernels for 17% -> 19%
where the time goes in v4:
time: 214 us; the launch traced here: 215 us
  Pallas kernels  80.4 us (38%)
  blocking collectives  53.3 us (25%)
  waiting for transfers between devices  40.9 us (19%)
  starting transfers between devices  22.5 us (11%)
  local copies, waits for them, and re-layouts  10.7 us (5%)
  other arithmetic  6.01 us (3%)
    all_to_all x1, blocking collectives, over_chips(): return lax.all_to_all(half, CHIPS, 0, 0).astype(F32).sum(0)  41.3 us
    pallas_call x3, Pallas kernels, on_device(): pl.pallas_call(body, out_shape=(shape((room, D), BF16), shape((room, D),...  39.5 us
    pallas_call x1, Pallas kernels, on_device(): call(gradient_kernel, 'gradient', (shape((D // 2, both), F32), shape((D /...  31.1 us
    ppermute x3, waiting for transfers between devices, on_device(): up_z = lambda v: lax.ppermute(v, 'z', ring('z', 1))  20.2 us
    all_to_all x1, waiting for transfers between devices, on_device(): terms = lax.all_to_all(total, TM, 0, 0)  12 us
    all_to_all x1, blocking collectives, on_device(): enter = lax.all_to_all(entering, TM, 0, 0).reshape(128, D)  12 us
    all_to_all x1, starting transfers between devices, on_device(): terms = lax.all_to_all(total, TM, 0, 0)  10.2 us
    pallas_call x1, Pallas kernels, on_device(): call(upstream_kernel, 'upstream', (shape((steps, D), BF16), shape((32, st...  7.48 us
  transfers between devices with their start and end apart: 15, of which 8 were waited for; matrix products, arithmetic and copies ran while one was open for 2% of the time, Pallas kernels for 19%

profile of v4, /device:TPU:0, one launch (start us, length us, event | category | flops | bytes accessed | tf_op | source)
XLA Modules:
  0.0 214.5 jit_solution(2272434439833987215)
XLA Ops:
  0.6 0.0 copy-start.6
  0.6 0.0 copy-start.9
  0.7 0.0 copy-start.14
  0.7 0.0 copy-start.15
  0.7 2.8 %fusion.12 = (bf16[1,1,512,1024]{3,2,1,0:T(8,128)(2,1)}, bf16[1,1,512,1024]{3,2,1,0:T(8,128)(2,1)S(1)}) fusion(bf16[1,1,1024,1024]{3,2,1,0:T(8,128)(2,1)} %param.10), kind=kLoop, calls=%fused_computation.67 | loop fusion | bytes 4194304 | tf_op jit(solution)/shard_map/slice | solution.py:309
  3.5 2.0 collective-permute-start
  5.5 2.1 collective-permute-start.1
  7.6 0.0 collective-permute-start.4
  7.6 0.7 compare_select_fusion.11
  8.3 0.7 fusion.11
  9.0 0.7 fusion.10
  9.7 0.1 convert_reduce_fusion.2
  9.9 0.1 iota_minimum_fusion
  9.9 0.2 convert_reduce_fusion.1
  10.1 0.3 select_reduce_fusion
  10.5 0.1 broadcast_select_fusion
  10.5 0.0 copy-done.15
  10.5 0.0 copy-start.10
  10.6 2.2 %copy-done.10 = bf16[1,2048,1024]{2,1,0:T(8,128)(2,1)S(1)} copy-done((bf16[1,2048,1024]{2,1,0:T(8,128)(2,1)S(1)}, bf16[1,2048,1024]{2,1,0:T(8,128)(2,1)}, u32[]{:S(2)}) %copy-start.10) | copy-done | bytes 4194328
  12.7 1.6 copy-done.11
  14.3 7.5 %upstream.1 = (bf16[2048,1024]{1,0:T(8,128)(2,1)S(1)}, f32[32,2048]{1,0:T(8,128)S(1)}, f32[2048,128]{1,0:T(8,128)S(1)}, f32[8,8,128]{2,1,0:T(8,128)S(1)}) custom-call(s32[8]{0:T(128)S(1)} %bitcast.64, f32[16,2048]{1,0:T(8,128)S(1)} %bitcast.68, s32[8,1,256]{2,1,0:T(1,128)S(1)} %bitcast.69, bf16[1,2048,1024]{2,1,0:T(8,128)(2,1)S(1)} %copy-done.10, ...), custom_call_target="tpu_custom_call" | custom-call | flops 4294967296 | bytes 12582912 | tf_op jit(solution)/shard_map/upstream/pallas_call | solution.py:339
  21.8 0.0 copy-start.1
  21.8 9.0 %collective-permute-done.refs_0_ = bf16[2,256,1024]{2,1,0:T(8,128)(2,1)} collective-permute-done((bf16[2,256,1024]{2,1,0:T(8,128)(2,1)S(1)}, bf16[2,256,1024]{2,1,0:T(8,128)(2,1)}, u32[]{:S(2)}, u32[]{:S(2)}) %collective-permute-start) | collective-permute-done | bytes 1048608 | tf_op jit(solution)/shard_map/ppermute | solution.py:307
  30.9 0.0 collective-permute-done.1.refs_1_
  30.9 1.5 collective-permute-start.2
  32.4 1.8 collective-permute-start.3
  34.1 0.1 collective-permute-start.7
  34.2 0.7 fusion.14
  34.9 0.5 collective-permute-start.8
  35.4 0.0 collective-permute-done.4.refs_1_
  35.4 14.2 %stage_0.1 = (bf16[2304,1024]{1,0:T(8,128)(2,1)}, bf16[2304,1024]{1,0:T(8,128)(2,1)}, bf16[2304,128]{1,0:T(8,128)(2,1)S(1)}, bf16[2304,1024]{1,0:T(8,128)(2,1)},...) custom-call(s32[8]{0:T(128)S(1)} %get-tuple-element.139.block, ...), custom_call_target="tpu_custom_call" | custom-call | flops 5368709120 | bytes 16777216 | tf_op jit(solution)/shard_map/stage_0/pallas_call | solution.py:397
  49.6 7.1 %collective-permute-done.2.refs_4_ = bf16[2,256,1024]{2,1,0:T(8,128)(2,1)S(1)} collective-permute-done((bf16[2,256,1024]{2,1,0:T(8,128)(2,1)}, bf16[2,256,1024]{2,1,0:T(8,128)(2,1)S(1)}, u32[]{:S(2)}, u32[]{:S(2)}) %collective-permute-start.2) | collective-permute-done | bytes 1048608 | tf_op jit(solution)/shard_map/ppermute | solution.py:307
  56.7 0.0 collective-permute-done.3.refs_5_
  56.7 0.0 collective-permute-start.10
  56.7 0.5 collective-permute-start.9
  57.2 0.8 collective-permute-start.5
  58.0 0.0 collective-permute-done.7.refs_2_
  58.0 2.4 %collective-permute-start.6 = (bf16[2,256,1024]{2,1,0:T(8,128)(2,1)}, bf16[2,256,1024]{2,1,0:T(8,128)(2,1)S(1)}, u32[]{:S(2)}, u32[]{:S(2)}) collective-permute-start(bf16[2,256,1024]{2,1,0:T(8,128)(2,1)} %collective-permute-done.1.refs_1_), channel_id=1, source_target_pairs={{0,6},{2,0},{4,2},{6,4},{1,7},{3,1},{5,3},{7,5},{8,14},{10,8},{12,... | collective-permute-start | bytes 3145736 | tf_op jit(solution)/shard_map/ppermute | solution.py:308
  60.4 0.0 collective-permute-done.8.refs_3_
  60.4 0.0 collective-permute-done.10.refs_7_
  60.4 0.4 collective-permute-done.9.refs_6_
  60.8 18.7 %stage_1.1 = (bf16[2304,1024]{1,0:T(8,128)(2,1)}, bf16[2304,1024]{1,0:T(8,128)(2,1)}, bf16[2304,128]{1,0:T(8,128)(2,1)S(1)}, bf16[2304,1024]{1,0:T(8,128)(2,1)},...) custom-call(s32[8]{0:T(128)S(1)} %get-tuple-element.138.block, ...), custom_call_target="tpu_custom_call", output_to_operand_aliasing={{0}: (18, {}), {1}: (19, {}), {2}: (20, {}), {3}: (21, {}),... | custom-call | flops 5368709120 | bytes 16777216 | tf_op jit(solution)/shard_map/stage_1/pallas_call | solution.py:397
  79.5 4.1 %collective-permute-done.5.refs_0_ = bf16[2,256,1024]{2,1,0:T(8,128)(2,1)S(1)} collective-permute-done((bf16[2,256,1024]{2,1,0:T(8,128)(2,1)}, bf16[2,256,1024]{2,1,0:T(8,128)(2,1)S(1)}, u32[]{:S(2)}, u32[]{:S(2)}) %collective-permute-start.5) | collective-permute-done | bytes 1048608 | tf_op jit(solution)/shard_map/ppermute | solution.py:307
  83.7 0.0 collective-permute-done.6.refs_1_
  83.7 0.0 collective-permute-start.11
  83.7 0.5 collective-permute-start.12
  84.2 2.1 %collective-permute-done.11.refs_2_ = bf16[2,256,1024]{2,1,0:T(8,128)(2,1)S(1)} collective-permute-done((bf16[2,256,1024]{2,1,0:T(8,128)(2,1)S(1)}, bf16[2,256,1024]{2,1,0:T(8,128)(2,1)S(1)}, u32[]{:S(2)}, u32[]{:S(2)}) %collective-permute-start.11) | collective-permute-done | bytes 1048608 | tf_op jit(solution)/shard_map/ppermute | solution.py:306
  86.3 1.5 collective-permute-done.12.refs_3_
  87.8 6.6 %stage_2.1 = (bf16[2304,1024]{1,0:T(8,128)(2,1)}, bf16[2304,1024]{1,0:T(8,128)(2,1)}, bf16[2304,128]{1,0:T(8,128)(2,1)S(1)}, bf16[2304,1024]{1,0:T(8,128)(2,1)},...) custom-call(s32[8]{0:T(128)S(1)} %get-tuple-element.140.block, ...), custom_call_target="tpu_custom_call", output_to_operand_aliasing={{0}: (14, {}), {1}: (15, {}), {2}: (16, {}), {3}: (17, {}),... | custom-call | flops 5368709120 | bytes 16777216 | tf_op jit(solution)/shard_map/stage_2/pallas_call | solution.py:397
  94.4 2.1 local.1
  96.5 1.3 copy-done.12
  97.8 0.8 copy-done.13
  98.6 10.2 %all-to-all-start = ((bf16[16,16,1024]{2,1,0:T(8,128)(2,1)}), bf16[16,16,1024]{2,1,0:T(8,128)(2,1)S(1)}, u32[]{:S(2)}, u32[]{:S(2)}) async-start(bf16[16,16,1024]{2,1,0:T(8,128)(2,1)} %get-tuple-element.120), calls=%async_computation | async-start | bytes 1048576 | tf_op jit(solution)/shard_map/all_to_all | solution.py:459
  108.9 12.0 %all-to-all-done.terms = bf16[16,16,1024]{2,1,0:T(8,128)(2,1)S(1)} async-done(((bf16[16,16,1024]{2,1,0:T(8,128)(2,1)}), bf16[16,16,1024]{2,1,0:T(8,128)(2,1)S(1)}, u32[]{:S(2)}, u32[]{:S(2)}) %all-to-all-start) | async-done | bytes 524320 | tf_op jit(solution)/shard_map/all_to_all | solution.py:459
  120.9 0.2 scan.1
  121.2 12.0 %all_to_all.15 = bf16[16,8,1024]{2,1,0:T(8,128)(2,1)} all-to-all(bf16[16,8,1024]{2,1,0:T(8,128)(2,1)S(1)} %scan.1), channel_id=1, replica_groups=mesh['y'=4,'x'=4,'z'=4,'c'=2] {'y','x'}, dimensions={0} | all-to-all | bytes 524288 | tf_op jit(solution)/shard_map/all_to_all | solution.py:474
  133.1 31.1 %gradient.1 = (f32[512,2176]{1,0:T(8,128)}, bf16[512,2176]{1,0:T(8,128)(2,1)}) custom-call(s32[1]{0:T(128)} %bitcast.core, s32[8]{0:T(128)} %bitcast.63, bf16[1,2048,1024]{2,1,0:T(8,128)(2,1)} %cot.3, bf16[2304,1024]{1,0:T(8,128)(2,1)} %get-tuple-element.109.taken, bf16[2304,1024]{1,0:T(8,128)(2,1)} %get-tuple-element.110.inner, ...), custom_call_target="tpu_custom_call" | custom-call | flops 13958643712 | bytes 37748736 | tf_op jit(solution)/shard_map/gradient/pallas_call | solution.py:482
  164.2 0.1 collective-permute-start.13
  164.3 4.5 %collective-permute-done.13 = bf16[512,2176]{1,0:T(8,128)(2,1)S(1)} collective-permute-done((bf16[512,2176]{1,0:T(8,128)(2,1)}, bf16[512,2176]{1,0:T(8,128)(2,1)S(1)}, u32[]{:S(2)}, u32[]{:S(2)}) %collective-permute-start.13) | collective-permute-done | bytes 2228256 | tf_op jit(solution)/shard_map/ppermute | solution.py:284
  168.8 2.8 %fusion = bf16[64,8,2176]{2,1,0:T(8,128)(2,1)S(1)} fusion(f32[512,2176]{1,0:T(8,128)} %get-tuple-element.121, bf16[512,2176]{1,0:T(8,128)(2,1)S(1)} %collective-permute-done.13), kind=kLoop, calls=%fused_computation.2 | loop fusion | flops 3342336 | bytes 8912896 | tf_op jit(solution)/shard_map/reshape | solution.py:286
  171.6 41.3 %all_to_all.16 = bf16[64,8,2176]{2,1,0:T(8,128)(2,1)S(1)} all-to-all(bf16[64,8,2176]{2,1,0:T(8,128)(2,1)S(1)} %fusion), channel_id=1, replica_groups=mesh['y'=4,'x'=4,'z'=4,'c'=2] {'y','x','z'}, dimensions={0} | all-to-all | bytes 4456448 | tf_op jit(solution)/shard_map/all_to_all | solution.py:290
  213.0 0.3 convert_reduce_fusion
  213.3 0.6 fusion.13
  213.9 0.6 slice.77
  (26 shorter events, 0.1 us)
Async XLA Ops:
  0.6 7.0 %copy-start.6 = (bf16[1,1,1024,1024]{3,2,1,0:T(8,128)(2,1)S(1)}, bf16[1,1,1024,1024]{3,2,1,0:T(8,128)(2,1)}, u32[]{:S(2)}) copy-start(bf16[1,1,1024,1024]{3,2,1,0:T(8,128)(2,1)} %param.10) | copy-start | bytes 6291460
  0.6 9.9 %copy-start.9 = (s32[1,1,8]{2,1,0:T(1,128)S(1)}, s32[1,1,8]{2,1,0:T(1,128)}, u32[]{:S(2)}) copy-start(s32[1,1,8]{2,1,0:T(1,128)} %param.13) | copy-start | bytes 100
  0.7 9.9 %copy-start.14 = (f32[1,16,2048]{2,1,0:T(8,128)S(1)}, f32[1,16,2048]{2,1,0:T(8,128)}, u32[]{:S(2)}) copy-start(f32[1,16,2048]{2,1,0:T(8,128)} %param.14) | copy-start | bytes 393220
  0.7 9.9 %copy-start.15 = (s32[1,2048]{1,0:T(1,128)S(1)}, s32[1,2048]{1,0:T(1,128)}, u32[]{:S(2)}) copy-start(s32[1,2048]{1,0:T(1,128)} %param.15) | copy-start | bytes 24580
  3.5 27.4 %collective-permute-start = (bf16[2,256,1024]{2,1,0:T(8,128)(2,1)S(1)}, bf16[2,256,1024]{2,1,0:T(8,128)(2,1)}, u32[]{:S(2)}, u32[]{:S(2)}) collective-permute-start(bf16[2,256,1024]{2,1,0:T(8,128)(2,1)S(1)} %bitcast.70), channel_id=1, source_target_pairs={{0,2},{2,4},{4,6},{6,0},{1,3},{3,5},{5,7},{7,1},{8,10},{10,12},{12... | collective-permute-start | bytes 3145736 | tf_op jit(solution)/shard_map/ppermute | solution.py:307
  5.5 25.4 %collective-permute-start.1 = (bf16[2,256,1024]{2,1,0:T(8,128)(2,1)}, bf16[2,256,1024]{2,1,0:T(8,128)(2,1)}, u32[]{:S(2)}, u32[]{:S(2)}) collective-permute-start(bf16[2,256,1024]{2,1,0:T(8,128)(2,1)} %bitcast.10), channel_id=1, source_target_pairs={{0,6},{2,0},{4,2},{6,4},{1,7},{3,1},{5,3},{7,5},{8,14},{10,8},{12,... | collective-permute-start | bytes 3145736 | tf_op jit(solution)/shard_map/ppermute | solution.py:308
  7.6 27.8 %collective-permute-start.4 = (bf16[4,256,1024]{2,1,0:T(8,128)(2,1)S(1)}, bf16[4,256,1024]{2,1,0:T(8,128)(2,1)}, u32[]{:S(2)}, u32[]{:S(2)}) collective-permute-start(bf16[4,256,1024]{2,1,0:T(8,128)(2,1)S(1)} %bitcast.61), channel_id=1, source_target_pairs={{0,1},{1,0},{2,3},{3,2},{4,5},{5,4},{6,7},{7,6},{8,9},{9,8},{10,11... | collective-permute-start | bytes 6291464 | tf_op jit(solution)/shard_map/ppermute | solution.py:306
  10.5 2.2 %copy-start.10 = (bf16[1,2048,1024]{2,1,0:T(8,128)(2,1)S(1)}, bf16[1,2048,1024]{2,1,0:T(8,128)(2,1)}, u32[]{:S(2)}) copy-start(bf16[1,2048,1024]{2,1,0:T(8,128)(2,1)} %cot.3) | copy-start | bytes 12582916
  12.7 1.6 copy-start.11
  14.3 21.1 %copy-start.2 = (bf16[1024,1024]{1,0:T(8,128)(2,1)S(1)}, bf16[1024,1024]{1,0:T(8,128)(2,1)}, u32[]{:S(2)}) copy-start(bf16[1024,1024]{1,0:T(8,128)(2,1)} %refs_4_.1) | copy-start | bytes 6291460
  14.3 21.1 %copy-start.7 = (bf16[1,1,1024,1024]{3,2,1,0:T(8,128)(2,1)S(1)}, bf16[1,1,1024,1024]{3,2,1,0:T(8,128)(2,1)}, u32[]{:S(2)}) copy-start(bf16[1,1,1024,1024]{3,2,1,0:T(8,128)(2,1)} %param.10) | copy-start | bytes 6291460
  14.3 21.1 %copy-start.8 = (bf16[1024,128]{1,0:T(8,128)(2,1)S(1)}, bf16[1024,128]{1,0:T(8,128)(2,1)}, u32[]{:S(2)}) copy-start(bf16[1024,128]{1,0:T(8,128)(2,1)} %refs_5_.1) | copy-start | bytes 786436
  21.8 66.0 %copy-start.1 = (bf16[2048,1024]{1,0:T(8,128)(2,1)}, bf16[2048,1024]{1,0:T(8,128)(2,1)S(1)}, u32[]{:S(2)}) copy-start(bf16[2048,1024]{1,0:T(8,128)(2,1)S(1)} %get-tuple-element.68.refs_4_.refs_10_.refs_6_.up) | copy-start | bytes 12582916
  21.8 66.0 %copy-start.4 = (f32[2048,128]{1,0:T(8,128)}, f32[2048,128]{1,0:T(8,128)S(1)}, u32[]{:S(2)}) copy-start(f32[2048,128]{1,0:T(8,128)S(1)} %get-tuple-element.70.refs_6_.refs_12_.refs_8_.cols) | copy-start | bytes 3145732
  30.9 25.8 %collective-permute-start.2 = (bf16[2,256,1024]{2,1,0:T(8,128)(2,1)}, bf16[2,256,1024]{2,1,0:T(8,128)(2,1)S(1)}, u32[]{:S(2)}, u32[]{:S(2)}) collective-permute-start(bf16[2,256,1024]{2,1,0:T(8,128)(2,1)} %bitcast.10), channel_id=1, source_target_pairs={{0,2},{2,4},{4,6},{6,0},{1,3},{3,5},{5,7},{7,1},{8,10},{10,12},{12... | collective-permute-start | bytes 3145736 | tf_op jit(solution)/shard_map/ppermute | solution.py:307
  32.4 24.3 %collective-permute-start.3 = (bf16[2,256,1024]{2,1,0:T(8,128)(2,1)S(1)}, bf16[2,256,1024]{2,1,0:T(8,128)(2,1)S(1)}, u32[]{:S(2)}, u32[]{:S(2)}) collective-permute-start(bf16[2,256,1024]{2,1,0:T(8,128)(2,1)S(1)} %bitcast.71), channel_id=1, source_target_pairs={{0,6},{2,0},{4,2},{6,4},{1,7},{3,1},{5,3},{7,5},{8,14},{10,8},{12,... | collective-permute-start | bytes 3145736 | tf_op jit(solution)/shard_map/ppermute | solution.py:308
  34.1 23.9 %collective-permute-start.7 = (bf16[2,256,1024]{2,1,0:T(8,128)(2,1)}, bf16[2,256,1024]{2,1,0:T(8,128)(2,1)S(1)}, u32[]{:S(2)}, u32[]{:S(2)}) collective-permute-start(bf16[2,256,1024]{2,1,0:T(8,128)(2,1)} %collective-permute-done.refs_0_), channel_id=1, source_target_pairs={{0,1},{1,0},{2,3},{3,2},{4,5},{5,4},{6,7},{7,6},{8,9},{9,8},{10,11... | collective-permute-start | bytes 3145736 | tf_op jit(solution)/shard_map/ppermute | solution.py:306
  34.9 25.5 %collective-permute-start.8 = (bf16[2,256,1024]{2,1,0:T(8,128)(2,1)}, bf16[2,256,1024]{2,1,0:T(8,128)(2,1)S(1)}, u32[]{:S(2)}, u32[]{:S(2)}) collective-permute-start(bf16[2,256,1024]{2,1,0:T(8,128)(2,1)} %collective-permute-done.1.refs_1_), channel_id=1, source_target_pairs={{0,1},{1,0},{2,3},{3,2},{4,5},{5,4},{6,7},{7,6},{8,9},{9,8},{10,11... | collective-permute-start | bytes 3145736 | tf_op jit(solution)/shard_map/ppermute | solution.py:306
  56.7 3.8 %collective-permute-start.10 = (bf16[2,256,1024]{2,1,0:T(8,128)(2,1)S(1)}, bf16[2,256,1024]{2,1,0:T(8,128)(2,1)S(1)}, u32[]{:S(2)}, u32[]{:S(2)}) collective-permute-start(bf16[2,256,1024]{2,1,0:T(8,128)(2,1)S(1)} %collective-permute-done.3.refs_5_), channel_id=1, source_target_pairs={{0,1},{1,0},{2,3},{3,2},{4,5},{5,4},{6,7},{7,6},{8,9},{9,8},{10,11... | collective-permute-start | bytes 3145736 | tf_op jit(solution)/shard_map/ppermute | solution.py:306
  56.7 4.2 %collective-permute-start.9 = (bf16[2,256,1024]{2,1,0:T(8,128)(2,1)S(1)}, bf16[2,256,1024]{2,1,0:T(8,128)(2,1)S(1)}, u32[]{:S(2)}, u32[]{:S(2)}) collective-permute-start(bf16[2,256,1024]{2,1,0:T(8,128)(2,1)S(1)} %collective-permute-done.2.refs_4_), channel_id=1, source_target_pairs={{0,1},{1,0},{2,3},{3,2},{4,5},{5,4},{6,7},{7,6},{8,9},{9,8},{10,11... | collective-permute-start | bytes 3145736 | tf_op jit(solution)/shard_map/ppermute | solution.py:306
  57.2 26.5 %collective-permute-start.5 = (bf16[2,256,1024]{2,1,0:T(8,128)(2,1)}, bf16[2,256,1024]{2,1,0:T(8,128)(2,1)S(1)}, u32[]{:S(2)}, u32[]{:S(2)}) collective-permute-start(bf16[2,256,1024]{2,1,0:T(8,128)(2,1)} %collective-permute-done.refs_0_), channel_id=1, source_target_pairs={{0,2},{2,4},{4,6},{6,0},{1,3},{3,5},{5,7},{7,1},{8,10},{10,12},{12... | collective-permute-start | bytes 3145736 | tf_op jit(solution)/shard_map/ppermute | solution.py:307
  58.0 25.7 %collective-permute-start.6 = (bf16[2,256,1024]{2,1,0:T(8,128)(2,1)}, bf16[2,256,1024]{2,1,0:T(8,128)(2,1)S(1)}, u32[]{:S(2)}, u32[]{:S(2)}) collective-permute-start(bf16[2,256,1024]{2,1,0:T(8,128)(2,1)} %collective-permute-done.1.refs_1_), channel_id=1, source_target_pairs={{0,6},{2,0},{4,2},{6,4},{1,7},{3,1},{5,3},{7,5},{8,14},{10,8},{12,... | collective-permute-start | bytes 3145736 | tf_op jit(solution)/shard_map/ppermute | solution.py:308
  83.7 2.7 %collective-permute-start.11 = (bf16[2,256,1024]{2,1,0:T(8,128)(2,1)S(1)}, bf16[2,256,1024]{2,1,0:T(8,128)(2,1)S(1)}, u32[]{:S(2)}, u32[]{:S(2)}) collective-permute-start(bf16[2,256,1024]{2,1,0:T(8,128)(2,1)S(1)} %collective-permute-done.5.refs_0_), channel_id=1, source_target_pairs={{0,1},{1,0},{2,3},{3,2},{4,5},{5,4},{6,7},{7,6},{8,9},{9,8},{10,11... | collective-permute-start | bytes 3145736 | tf_op jit(solution)/shard_map/ppermute | solution.py:306
  83.7 4.2 %collective-permute-start.12 = (bf16[2,256,1024]{2,1,0:T(8,128)(2,1)S(1)}, bf16[2,256,1024]{2,1,0:T(8,128)(2,1)S(1)}, u32[]{:S(2)}, u32[]{:S(2)}) collective-permute-start(bf16[2,256,1024]{2,1,0:T(8,128)(2,1)S(1)} %collective-permute-done.6.refs_1_), channel_id=1, source_target_pairs={{0,1},{1,0},{2,3},{3,2},{4,5},{5,4},{6,7},{7,6},{8,9},{9,8},{10,11... | collective-permute-start | bytes 3145736 | tf_op jit(solution)/shard_map/ppermute | solution.py:306
  94.4 2.1 copy-start
  94.4 2.1 copy-start.3
  94.4 2.1 copy-start.5
  96.5 1.3 copy-start.12
  97.8 0.8 copy-start.13
  98.6 22.3 %all-to-all-start = ((bf16[16,16,1024]{2,1,0:T(8,128)(2,1)}), bf16[16,16,1024]{2,1,0:T(8,128)(2,1)S(1)}, u32[]{:S(2)}, u32[]{:S(2)}) async-start(bf16[16,16,1024]{2,1,0:T(8,128)(2,1)} %get-tuple-element.120), calls=%async_computation | async-start | bytes 1048576 | tf_op jit(solution)/shard_map/all_to_all | solution.py:459
  164.2 4.6 %collective-permute-start.13 = (bf16[512,2176]{1,0:T(8,128)(2,1)}, bf16[512,2176]{1,0:T(8,128)(2,1)S(1)}, u32[]{:S(2)}, u32[]{:S(2)}) collective-permute-start(bf16[512,2176]{1,0:T(8,128)(2,1)} %get-tuple-element.122), channel_id=1, source_target_pairs={{0,1},{1,0},{2,3},{3,2},{4,5},{5,4},{6,7},{7,6},{8,9},{9,8},{10,11... | collective-permute-start | bytes 6684680 | tf_op jit(solution)/shard_map/ppermute | solution.py:284

commit v5 on v2

--- a/solution.py
+++ b/solution.py
@@ -22,7 +22,8 @@
 NT = (((1,), (1,)), ((), ()))
 TN = (((0,), (0,)), ((), ()))
 NN = (((1,), (0,)), ((), ()))
-VMEM_LIMIT = 56 * 1024 * 1024
+MIB = 1024 * 1024
+GRADIENT_ROOM = 56
 
 
 def mm(a, b, dims=NN):
@@ -44,13 +45,13 @@
     return mm(split(pltpu.roll(table, 128 - base, 1)), matrix)
 
 
-def call(kernel, name, out_shape, grid_spec, flops, nbytes):
+def call(kernel, name, out_shape, grid_spec, flops, nbytes, room=24):
     return pl.pallas_call(
         kernel,
         out_shape=out_shape,
         grid_spec=grid_spec,
         name=name,
-        compiler_params=pltpu.CompilerParams(vmem_limit_bytes=VMEM_LIMIT),
+        compiler_params=pltpu.CompilerParams(vmem_limit_bytes=room * MIB),
         cost_estimate=pl.CostEstimate(flops=flops, bytes_accessed=nbytes, transcendentals=0),
     )
 
@@ -427,7 +428,7 @@
             ),
             input_output_aliases={5 + number + 5 + n: n for n in range(len(kept))},
             name=f"stage_{s}",
-            compiler_params=pltpu.CompilerParams(vmem_limit_bytes=VMEM_LIMIT),
+            compiler_params=pltpu.CompilerParams(vmem_limit_bytes=32 * MIB),
             cost_estimate=pl.CostEstimate(
                 flops=4 * BLOCK * D * (D + 1024) + 4 * HEADS * 3 * BLOCK**3,
                 bytes_accessed=16 << 20,
@@ -514,6 +515,7 @@
         ),
         2 * steps * D * (2 * D + 1280),
         36 << 20,
+        room=GRADIENT_ROOM,
     )(own_core, fill, cotangent, taken, inner, up, keys, cols, ro, gi, pair, starts, push_out, gains, enter)
 
     grads = over_chips(over_chip(keep, give))

time: 219 us -> 209 us (0.954)
  Pallas kernels: 93.3 us -> 75.9 us
  waiting for transfers between devices: 38.7 us -> 47.2 us
    pallas_call x3, Pallas kernels: 49.2 us -> 39.5 us  [on_device(): pl.pallas_call(body, out_shape=(shape((room, D), BF16), shape((room, D),...]
    ppermute x3, waiting for transfers between devices: 18.3 us -> 27 us  [on_device(): up_z = lambda v: lax.ppermute(v, 'z', ring('z', 1))]
    pallas_call x1, Pallas kernels: 11.6 us -> 7.48 us  [on_device(): call(upstream_kernel, 'upstream', (shape((steps, D), BF16), shape((32, st...]
    unnamed x24 -> x32, local copies, waits for them, and re-layouts: 2.77 us -> 5.93 us
  transfers between devices with their start and end apart: 15 -> 15, of which waited for: 8 -> 8; matrix products, arithmetic and copies ran while one was open for 2% -> 2% of each run, Pallas kernels for 20% -> 16%
where the time goes in v5:
time: 209 us; the launch traced here: 208 us
  Pallas kernels  75.9 us (36%)
  blocking collectives  48.1 us (23%)
  waiting for transfers between devices  47.2 us (23%)
  starting transfers between devices  19.3 us (9%)
  local copies, waits for them, and re-layouts  10.7 us (5%)
  other arithmetic  6.01 us (3%)
    pallas_call x3, Pallas kernels, on_device(): pl.pallas_call(body, out_shape=(shape((room, D), BF16), shape((room, D),...  39.5 us
    all_to_all x1, blocking collectives, over_chips(): return lax.all_to_all(half, CHIPS, 0, 0).astype(F32).sum(0)  36.1 us
    ppermute x3, waiting for transfers between devices, on_device(): up_z = lambda v: lax.ppermute(v, 'z', ring('z', 1))  27 us
    pallas_call x1, Pallas kernels, on_device(): call(gradient_kernel, 'gradient', (shape((D // 2, both), F32), shape((D /...  26.6 us
    all_to_all x1, blocking collectives, on_device(): enter = lax.all_to_all(entering, TM, 0, 0).reshape(128, D)  12 us
    all_to_all x1, waiting for transfers between devices, on_device(): terms = lax.all_to_all(total, TM, 0, 0)  11.6 us
    pallas_call x1, Pallas kernels, on_device(): call(upstream_kernel, 'upstream', (shape((steps, D), BF16), shape((32, st...  7.48 us
    all_to_all x1, starting transfers between devices, on_device(): terms = lax.all_to_all(total, TM, 0, 0)  7.06 us
  transfers between devices with their start and end apart: 15, of which 8 were waited for; matrix products, arithmetic and copies ran while one was open for 2% of the time, Pallas kernels for 16%

profile of v5, /device:TPU:0, one launch (start us, length us, event | category | flops | bytes accessed | tf_op | source)
XLA Modules:
  0.0 208.0 jit_solution(11830195703765495883)
XLA Ops:
  0.6 0.0 copy-start.6
  0.6 0.0 copy-start.9
  0.7 0.0 copy-start.14
  0.7 0.0 copy-start.15
  0.7 2.8 %fusion.12 = (bf16[1,1,512,1024]{3,2,1,0:T(8,128)(2,1)}, bf16[1,1,512,1024]{3,2,1,0:T(8,128)(2,1)S(1)}) fusion(bf16[1,1,1024,1024]{3,2,1,0:T(8,128)(2,1)} %param.10), kind=kLoop, calls=%fused_computation.67 | loop fusion | bytes 4194304 | tf_op jit(solution)/shard_map/slice | solution.py:305
  3.5 2.0 collective-permute-start
  5.5 2.1 %collective-permute-start.1 = (bf16[2,256,1024]{2,1,0:T(8,128)(2,1)}, bf16[2,256,1024]{2,1,0:T(8,128)(2,1)}, u32[]{:S(2)}, u32[]{:S(2)}) collective-permute-start(bf16[2,256,1024]{2,1,0:T(8,128)(2,1)} %bitcast.10), channel_id=1, source_target_pairs={{0,6},{2,0},{4,2},{6,4},{1,7},{3,1},{5,3},{7,5},{8,14},{10,8},{12,... | collective-permute-start | bytes 3145736 | tf_op jit(solution)/shard_map/ppermute | solution.py:304
  7.6 0.0 collective-permute-start.4
  7.6 0.7 compare_select_fusion.11
  8.3 0.7 fusion.11
  9.0 0.7 fusion.10
  9.7 0.1 convert_reduce_fusion.2
  9.9 0.1 iota_minimum_fusion
  9.9 0.2 convert_reduce_fusion.1
  10.1 0.3 select_reduce_fusion
  10.5 0.1 broadcast_select_fusion
  10.5 0.0 copy-done.15
  10.5 0.0 copy-start.10
  10.6 2.2 %copy-done.10 = bf16[1,2048,1024]{2,1,0:T(8,128)(2,1)S(1)} copy-done((bf16[1,2048,1024]{2,1,0:T(8,128)(2,1)S(1)}, bf16[1,2048,1024]{2,1,0:T(8,128)(2,1)}, u32[]{:S(2)}) %copy-start.10) | copy-done | bytes 4194328
  12.7 1.6 copy-done.11
  14.3 7.5 %upstream.1 = (bf16[2048,1024]{1,0:T(8,128)(2,1)S(1)}, f32[32,2048]{1,0:T(8,128)S(1)}, f32[2048,128]{1,0:T(8,128)S(1)}, f32[8,8,128]{2,1,0:T(8,128)S(1)}) custom-call(s32[8]{0:T(128)S(1)} %bitcast.64, f32[16,2048]{1,0:T(8,128)S(1)} %bitcast.68, s32[8,1,256]{2,1,0:T(1,128)S(1)} %bitcast.69, bf16[1,2048,1024]{2,1,0:T(8,128)(2,1)S(1)} %copy-done.10, ...), custom_call_target="tpu_custom_call" | custom-call | flops 4294967296 | bytes 12582912 | tf_op jit(solution)/shard_map/upstream/pallas_call | solution.py:335
  21.8 0.0 copy-start.1
  21.8 9.0 %collective-permute-done.refs_0_ = bf16[2,256,1024]{2,1,0:T(8,128)(2,1)} collective-permute-done((bf16[2,256,1024]{2,1,0:T(8,128)(2,1)S(1)}, bf16[2,256,1024]{2,1,0:T(8,128)(2,1)}, u32[]{:S(2)}, u32[]{:S(2)}) %collective-permute-start) | collective-permute-done | bytes 1048608 | tf_op jit(solution)/shard_map/ppermute | solution.py:303
  30.9 0.0 collective-permute-done.1.refs_1_
  30.9 1.5 collective-permute-start.2
  32.4 1.8 collective-permute-start.3
  34.1 0.1 collective-permute-start.7
  34.2 0.7 fusion.14
  34.9 0.5 collective-permute-start.8
  35.4 0.0 collective-permute-done.4.refs_1_
  35.4 10.9 %stage_0.1 = (bf16[2304,1024]{1,0:T(8,128)(2,1)}, bf16[2304,1024]{1,0:T(8,128)(2,1)}, bf16[2304,128]{1,0:T(8,128)(2,1)S(1)}, bf16[2304,1024]{1,0:T(8,128)(2,1)},...) custom-call(s32[8]{0:T(128)S(1)} %get-tuple-element.139.block, ...), custom_call_target="tpu_custom_call" | custom-call | flops 5368709120 | bytes 16777216 | tf_op jit(solution)/shard_map/stage_0/pallas_call | solution.py:393
  46.3 10.4 %collective-permute-done.2.refs_4_ = bf16[2,256,1024]{2,1,0:T(8,128)(2,1)S(1)} collective-permute-done((bf16[2,256,1024]{2,1,0:T(8,128)(2,1)}, bf16[2,256,1024]{2,1,0:T(8,128)(2,1)S(1)}, u32[]{:S(2)}, u32[]{:S(2)}) %collective-permute-start.2) | collective-permute-done | bytes 1048608 | tf_op jit(solution)/shard_map/ppermute | solution.py:303
  56.7 0.0 collective-permute-done.3.refs_5_
  56.7 0.0 collective-permute-start.10
  56.7 0.5 collective-permute-start.9
  57.2 0.8 collective-permute-start.5
  58.0 0.0 collective-permute-done.7.refs_2_
  58.0 2.4 %collective-permute-start.6 = (bf16[2,256,1024]{2,1,0:T(8,128)(2,1)}, bf16[2,256,1024]{2,1,0:T(8,128)(2,1)S(1)}, u32[]{:S(2)}, u32[]{:S(2)}) collective-permute-start(bf16[2,256,1024]{2,1,0:T(8,128)(2,1)} %collective-permute-done.1.refs_1_), channel_id=1, source_target_pairs={{0,6},{2,0},{4,2},{6,4},{1,7},{3,1},{5,3},{7,5},{8,14},{10,8},{12,... | collective-permute-start | bytes 3145736 | tf_op jit(solution)/shard_map/ppermute | solution.py:304
  60.4 0.0 collective-permute-done.8.refs_3_
  60.4 0.0 collective-permute-done.10.refs_7_
  60.4 0.4 collective-permute-done.9.refs_6_
  60.8 15.3 %stage_1.1 = (bf16[2304,1024]{1,0:T(8,128)(2,1)}, bf16[2304,1024]{1,0:T(8,128)(2,1)}, bf16[2304,128]{1,0:T(8,128)(2,1)S(1)}, bf16[2304,1024]{1,0:T(8,128)(2,1)},...) custom-call(s32[8]{0:T(128)S(1)} %get-tuple-element.138.block, ...), custom_call_target="tpu_custom_call", output_to_operand_aliasing={{0}: (18, {}), {1}: (19, {}), {2}: (20, {}), {3}: (21, {}),... | custom-call | flops 5368709120 | bytes 16777216 | tf_op jit(solution)/shard_map/stage_1/pallas_call | solution.py:393
  76.1 7.5 %collective-permute-done.5.refs_0_ = bf16[2,256,1024]{2,1,0:T(8,128)(2,1)S(1)} collective-permute-done((bf16[2,256,1024]{2,1,0:T(8,128)(2,1)}, bf16[2,256,1024]{2,1,0:T(8,128)(2,1)S(1)}, u32[]{:S(2)}, u32[]{:S(2)}) %collective-permute-start.5) | collective-permute-done | bytes 1048608 | tf_op jit(solution)/shard_map/ppermute | solution.py:303
  83.7 0.0 collective-permute-done.6.refs_1_
  83.7 0.0 collective-permute-start.11
  83.7 0.5 collective-permute-start.12
  84.2 2.1 %collective-permute-done.11.refs_2_ = bf16[2,256,1024]{2,1,0:T(8,128)(2,1)S(1)} collective-permute-done((bf16[2,256,1024]{2,1,0:T(8,128)(2,1)S(1)}, bf16[2,256,1024]{2,1,0:T(8,128)(2,1)S(1)}, u32[]{:S(2)}, u32[]{:S(2)}) %collective-permute-start.11) | collective-permute-done | bytes 1048608 | tf_op jit(solution)/shard_map/ppermute | solution.py:302
  86.3 1.5 collective-permute-done.12.refs_3_
  87.8 13.3 %stage_2.1 = (bf16[2304,1024]{1,0:T(8,128)(2,1)}, bf16[2304,1024]{1,0:T(8,128)(2,1)}, bf16[2304,128]{1,0:T(8,128)(2,1)S(1)}, bf16[2304,1024]{1,0:T(8,128)(2,1)},...) custom-call(s32[8]{0:T(128)S(1)} %get-tuple-element.140.block, ...), custom_call_target="tpu_custom_call", output_to_operand_aliasing={{0}: (14, {}), {1}: (15, {}), {2}: (16, {}), {3}: (17, {}),... | custom-call | flops 5368709120 | bytes 16777216 | tf_op jit(solution)/shard_map/stage_2/pallas_call | solution.py:393
  101.2 2.1 %local.1 = (f32[8,64,1024]{2,1,0:T(8,128)S(1)}, f32[8,16,1024]{2,1,0:T(8,128)S(1)}, bf16[16,16,1024]{2,1,0:T(8,128)(2,1)}) custom-call(f32[9,64,1024]{2,1,0:T(8,128)S(1)} %get-tuple-element.115.push_in, f32[9,64,1024]{2,1,0:T(8,128)S(1)} %get-tuple-element.116.push_out, f32[8,8,128]{2,1,0:T(8,128)S(1)} %get-tuple-element.117.ends), custom_call_target="tpu_custom_call" | custom-call | flops 16777216 | bytes 7340032 | tf_op jit(solution)/shard_map/local/pallas_call | solution.py:441
  103.3 1.3 copy-done.12
  104.6 0.8 copy-done.13
  105.4 7.1 %all-to-all-start = ((bf16[16,16,1024]{2,1,0:T(8,128)(2,1)}), bf16[16,16,1024]{2,1,0:T(8,128)(2,1)S(1)}, u32[]{:S(2)}, u32[]{:S(2)}) async-start(bf16[16,16,1024]{2,1,0:T(8,128)(2,1)} %get-tuple-element.120), calls=%async_computation | async-start | bytes 1048576 | tf_op jit(solution)/shard_map/all_to_all | solution.py:455
  112.5 11.6 %all-to-all-done.terms = bf16[16,16,1024]{2,1,0:T(8,128)(2,1)S(1)} async-done(((bf16[16,16,1024]{2,1,0:T(8,128)(2,1)}), bf16[16,16,1024]{2,1,0:T(8,128)(2,1)S(1)}, u32[]{:S(2)}, u32[]{:S(2)}) %all-to-all-start) | async-done | bytes 524320 | tf_op jit(solution)/shard_map/all_to_all | solution.py:455
  124.1 0.2 scan.1
  124.4 12.0 %all_to_all.15 = bf16[16,8,1024]{2,1,0:T(8,128)(2,1)} all-to-all(bf16[16,8,1024]{2,1,0:T(8,128)(2,1)S(1)} %scan.1), channel_id=1, replica_groups=mesh['y'=4,'x'=4,'z'=4,'c'=2] {'y','x'}, dimensions={0} | all-to-all | bytes 524288 | tf_op jit(solution)/shard_map/all_to_all | solution.py:470
  136.3 26.6 %gradient.1 = (f32[512,2176]{1,0:T(8,128)}, bf16[512,2176]{1,0:T(8,128)(2,1)}) custom-call(s32[1]{0:T(128)} %bitcast.core, s32[8]{0:T(128)} %bitcast.63, bf16[1,2048,1024]{2,1,0:T(8,128)(2,1)} %cot.3, bf16[2304,1024]{1,0:T(8,128)(2,1)} %get-tuple-element.109.taken, bf16[2304,1024]{1,0:T(8,128)(2,1)} %get-tuple-element.110.inner, ...), custom_call_target="tpu_custom_call" | custom-call | flops 13958643712 | bytes 37748736 | tf_op jit(solution)/shard_map/gradient/pallas_call | solution.py:480
  162.9 0.1 collective-permute-start.13
  163.0 4.5 %collective-permute-done.13 = bf16[512,2176]{1,0:T(8,128)(2,1)S(1)} collective-permute-done((bf16[512,2176]{1,0:T(8,128)(2,1)}, bf16[512,2176]{1,0:T(8,128)(2,1)S(1)}, u32[]{:S(2)}, u32[]{:S(2)}) %collective-permute-start.13) | collective-permute-done | bytes 2228256 | tf_op jit(solution)/shard_map/ppermute | solution.py:280
  167.6 2.8 %fusion = bf16[64,8,2176]{2,1,0:T(8,128)(2,1)S(1)} fusion(f32[512,2176]{1,0:T(8,128)} %get-tuple-element.121, bf16[512,2176]{1,0:T(8,128)(2,1)S(1)} %collective-permute-done.13), kind=kLoop, calls=%fused_computation.2 | loop fusion | flops 3342336 | bytes 8912896 | tf_op jit(solution)/shard_map/reshape | solution.py:282
  170.3 36.1 %all_to_all.16 = bf16[64,8,2176]{2,1,0:T(8,128)(2,1)S(1)} all-to-all(bf16[64,8,2176]{2,1,0:T(8,128)(2,1)S(1)} %fusion), channel_id=1, replica_groups=mesh['y'=4,'x'=4,'z'=4,'c'=2] {'y','x','z'}, dimensions={0} | all-to-all | bytes 4456448 | tf_op jit(solution)/shard_map/all_to_all | solution.py:286
  206.4 0.3 convert_reduce_fusion
  206.8 0.6 fusion.13
  207.4 0.6 slice.77
  (26 shorter events, 0.1 us)
Async XLA Ops:
  0.6 7.0 %copy-start.6 = (bf16[1,1,1024,1024]{3,2,1,0:T(8,128)(2,1)S(1)}, bf16[1,1,1024,1024]{3,2,1,0:T(8,128)(2,1)}, u32[]{:S(2)}) copy-start(bf16[1,1,1024,1024]{3,2,1,0:T(8,128)(2,1)} %param.10) | copy-start | bytes 6291460
  0.6 9.9 %copy-start.9 = (s32[1,1,8]{2,1,0:T(1,128)S(1)}, s32[1,1,8]{2,1,0:T(1,128)}, u32[]{:S(2)}) copy-start(s32[1,1,8]{2,1,0:T(1,128)} %param.13) | copy-start | bytes 100
  0.7 9.9 %copy-start.14 = (f32[1,16,2048]{2,1,0:T(8,128)S(1)}, f32[1,16,2048]{2,1,0:T(8,128)}, u32[]{:S(2)}) copy-start(f32[1,16,2048]{2,1,0:T(8,128)} %param.14) | copy-start | bytes 393220
  0.7 9.9 %copy-start.15 = (s32[1,2048]{1,0:T(1,128)S(1)}, s32[1,2048]{1,0:T(1,128)}, u32[]{:S(2)}) copy-start(s32[1,2048]{1,0:T(1,128)} %param.15) | copy-start | bytes 24580
  3.5 27.4 %collective-permute-start = (bf16[2,256,1024]{2,1,0:T(8,128)(2,1)S(1)}, bf16[2,256,1024]{2,1,0:T(8,128)(2,1)}, u32[]{:S(2)}, u32[]{:S(2)}) collective-permute-start(bf16[2,256,1024]{2,1,0:T(8,128)(2,1)S(1)} %bitcast.70), channel_id=1, source_target_pairs={{0,2},{2,4},{4,6},{6,0},{1,3},{3,5},{5,7},{7,1},{8,10},{10,12},{12... | collective-permute-start | bytes 3145736 | tf_op jit(solution)/shard_map/ppermute | solution.py:303
  5.5 25.4 %collective-permute-start.1 = (bf16[2,256,1024]{2,1,0:T(8,128)(2,1)}, bf16[2,256,1024]{2,1,0:T(8,128)(2,1)}, u32[]{:S(2)}, u32[]{:S(2)}) collective-permute-start(bf16[2,256,1024]{2,1,0:T(8,128)(2,1)} %bitcast.10), channel_id=1, source_target_pairs={{0,6},{2,0},{4,2},{6,4},{1,7},{3,1},{5,3},{7,5},{8,14},{10,8},{12,... | collective-permute-start | bytes 3145736 | tf_op jit(solution)/shard_map/ppermute | solution.py:304
  7.6 27.8 %collective-permute-start.4 = (bf16[4,256,1024]{2,1,0:T(8,128)(2,1)S(1)}, bf16[4,256,1024]{2,1,0:T(8,128)(2,1)}, u32[]{:S(2)}, u32[]{:S(2)}) collective-permute-start(bf16[4,256,1024]{2,1,0:T(8,128)(2,1)S(1)} %bitcast.61), channel_id=1, source_target_pairs={{0,1},{1,0},{2,3},{3,2},{4,5},{5,4},{6,7},{7,6},{8,9},{9,8},{10,11... | collective-permute-start | bytes 6291464 | tf_op jit(solution)/shard_map/ppermute | solution.py:302
  10.5 2.2 %copy-start.10 = (bf16[1,2048,1024]{2,1,0:T(8,128)(2,1)S(1)}, bf16[1,2048,1024]{2,1,0:T(8,128)(2,1)}, u32[]{:S(2)}) copy-start(bf16[1,2048,1024]{2,1,0:T(8,128)(2,1)} %cot.3) | copy-start | bytes 12582916
  12.7 1.6 copy-start.11
  14.3 21.1 %copy-start.2 = (bf16[1024,1024]{1,0:T(8,128)(2,1)S(1)}, bf16[1024,1024]{1,0:T(8,128)(2,1)}, u32[]{:S(2)}) copy-start(bf16[1024,1024]{1,0:T(8,128)(2,1)} %refs_4_.1) | copy-start | bytes 6291460
  14.3 21.1 %copy-start.7 = (bf16[1,1,1024,1024]{3,2,1,0:T(8,128)(2,1)S(1)}, bf16[1,1,1024,1024]{3,2,1,0:T(8,128)(2,1)}, u32[]{:S(2)}) copy-start(bf16[1,1,1024,1024]{3,2,1,0:T(8,128)(2,1)} %param.10) | copy-start | bytes 6291460
  14.3 21.1 %copy-start.8 = (bf16[1024,128]{1,0:T(8,128)(2,1)S(1)}, bf16[1024,128]{1,0:T(8,128)(2,1)}, u32[]{:S(2)}) copy-start(bf16[1024,128]{1,0:T(8,128)(2,1)} %refs_5_.1) | copy-start | bytes 786436
  21.8 66.0 %copy-start.1 = (bf16[2048,1024]{1,0:T(8,128)(2,1)}, bf16[2048,1024]{1,0:T(8,128)(2,1)S(1)}, u32[]{:S(2)}) copy-start(bf16[2048,1024]{1,0:T(8,128)(2,1)S(1)} %get-tuple-element.68.refs_4_.refs_10_.refs_6_.up) | copy-start | bytes 12582916
  21.8 66.0 %copy-start.4 = (f32[2048,128]{1,0:T(8,128)}, f32[2048,128]{1,0:T(8,128)S(1)}, u32[]{:S(2)}) copy-start(f32[2048,128]{1,0:T(8,128)S(1)} %get-tuple-element.70.refs_6_.refs_12_.refs_8_.cols) | copy-start | bytes 3145732
  30.9 25.8 %collective-permute-start.2 = (bf16[2,256,1024]{2,1,0:T(8,128)(2,1)}, bf16[2,256,1024]{2,1,0:T(8,128)(2,1)S(1)}, u32[]{:S(2)}, u32[]{:S(2)}) collective-permute-start(bf16[2,256,1024]{2,1,0:T(8,128)(2,1)} %bitcast.10), channel_id=1, source_target_pairs={{0,2},{2,4},{4,6},{6,0},{1,3},{3,5},{5,7},{7,1},{8,10},{10,12},{12... | collective-permute-start | bytes 3145736 | tf_op jit(solution)/shard_map/ppermute | solution.py:303
  32.4 24.3 %collective-permute-start.3 = (bf16[2,256,1024]{2,1,0:T(8,128)(2,1)S(1)}, bf16[2,256,1024]{2,1,0:T(8,128)(2,1)S(1)}, u32[]{:S(2)}, u32[]{:S(2)}) collective-permute-start(bf16[2,256,1024]{2,1,0:T(8,128)(2,1)S(1)} %bitcast.71), channel_id=1, source_target_pairs={{0,6},{2,0},{4,2},{6,4},{1,7},{3,1},{5,3},{7,5},{8,14},{10,8},{12,... | collective-permute-start | bytes 3145736 | tf_op jit(solution)/shard_map/ppermute | solution.py:304
  34.1 23.9 %collective-permute-start.7 = (bf16[2,256,1024]{2,1,0:T(8,128)(2,1)}, bf16[2,256,1024]{2,1,0:T(8,128)(2,1)S(1)}, u32[]{:S(2)}, u32[]{:S(2)}) collective-permute-start(bf16[2,256,1024]{2,1,0:T(8,128)(2,1)} %collective-permute-done.refs_0_), channel_id=1, source_target_pairs={{0,1},{1,0},{2,3},{3,2},{4,5},{5,4},{6,7},{7,6},{8,9},{9,8},{10,11... | collective-permute-start | bytes 3145736 | tf_op jit(solution)/shard_map/ppermute | solution.py:302
  34.9 25.5 %collective-permute-start.8 = (bf16[2,256,1024]{2,1,0:T(8,128)(2,1)}, bf16[2,256,1024]{2,1,0:T(8,128)(2,1)S(1)}, u32[]{:S(2)}, u32[]{:S(2)}) collective-permute-start(bf16[2,256,1024]{2,1,0:T(8,128)(2,1)} %collective-permute-done.1.refs_1_), channel_id=1, source_target_pairs={{0,1},{1,0},{2,3},{3,2},{4,5},{5,4},{6,7},{7,6},{8,9},{9,8},{10,11... | collective-permute-start | bytes 3145736 | tf_op jit(solution)/shard_map/ppermute | solution.py:302
  56.7 3.8 %collective-permute-start.10 = (bf16[2,256,1024]{2,1,0:T(8,128)(2,1)S(1)}, bf16[2,256,1024]{2,1,0:T(8,128)(2,1)S(1)}, u32[]{:S(2)}, u32[]{:S(2)}) collective-permute-start(bf16[2,256,1024]{2,1,0:T(8,128)(2,1)S(1)} %collective-permute-done.3.refs_5_), channel_id=1, source_target_pairs={{0,1},{1,0},{2,3},{3,2},{4,5},{5,4},{6,7},{7,6},{8,9},{9,8},{10,11... | collective-permute-start | bytes 3145736 | tf_op jit(solution)/shard_map/ppermute | solution.py:302
  56.7 4.2 %collective-permute-start.9 = (bf16[2,256,1024]{2,1,0:T(8,128)(2,1)S(1)}, bf16[2,256,1024]{2,1,0:T(8,128)(2,1)S(1)}, u32[]{:S(2)}, u32[]{:S(2)}) collective-permute-start(bf16[2,256,1024]{2,1,0:T(8,128)(2,1)S(1)} %collective-permute-done.2.refs_4_), channel_id=1, source_target_pairs={{0,1},{1,0},{2,3},{3,2},{4,5},{5,4},{6,7},{7,6},{8,9},{9,8},{10,11... | collective-permute-start | bytes 3145736 | tf_op jit(solution)/shard_map/ppermute | solution.py:302
  57.2 26.5 %collective-permute-start.5 = (bf16[2,256,1024]{2,1,0:T(8,128)(2,1)}, bf16[2,256,1024]{2,1,0:T(8,128)(2,1)S(1)}, u32[]{:S(2)}, u32[]{:S(2)}) collective-permute-start(bf16[2,256,1024]{2,1,0:T(8,128)(2,1)} %collective-permute-done.refs_0_), channel_id=1, source_target_pairs={{0,2},{2,4},{4,6},{6,0},{1,3},{3,5},{5,7},{7,1},{8,10},{10,12},{12... | collective-permute-start | bytes 3145736 | tf_op jit(solution)/shard_map/ppermute | solution.py:303
  58.0 25.7 %collective-permute-start.6 = (bf16[2,256,1024]{2,1,0:T(8,128)(2,1)}, bf16[2,256,1024]{2,1,0:T(8,128)(2,1)S(1)}, u32[]{:S(2)}, u32[]{:S(2)}) collective-permute-start(bf16[2,256,1024]{2,1,0:T(8,128)(2,1)} %collective-permute-done.1.refs_1_), channel_id=1, source_target_pairs={{0,6},{2,0},{4,2},{6,4},{1,7},{3,1},{5,3},{7,5},{8,14},{10,8},{12,... | collective-permute-start | bytes 3145736 | tf_op jit(solution)/shard_map/ppermute | solution.py:304
  83.7 2.7 %collective-permute-start.11 = (bf16[2,256,1024]{2,1,0:T(8,128)(2,1)S(1)}, bf16[2,256,1024]{2,1,0:T(8,128)(2,1)S(1)}, u32[]{:S(2)}, u32[]{:S(2)}) collective-permute-start(bf16[2,256,1024]{2,1,0:T(8,128)(2,1)S(1)} %collective-permute-done.5.refs_0_), channel_id=1, source_target_pairs={{0,1},{1,0},{2,3},{3,2},{4,5},{5,4},{6,7},{7,6},{8,9},{9,8},{10,11... | collective-permute-start | bytes 3145736 | tf_op jit(solution)/shard_map/ppermute | solution.py:302
  83.7 4.2 %collective-permute-start.12 = (bf16[2,256,1024]{2,1,0:T(8,128)(2,1)S(1)}, bf16[2,256,1024]{2,1,0:T(8,128)(2,1)S(1)}, u32[]{:S(2)}, u32[]{:S(2)}) collective-permute-start(bf16[2,256,1024]{2,1,0:T(8,128)(2,1)S(1)} %collective-permute-done.6.refs_1_), channel_id=1, source_target_pairs={{0,1},{1,0},{2,3},{3,2},{4,5},{5,4},{6,7},{7,6},{8,9},{9,8},{10,11... | collective-permute-start | bytes 3145736 | tf_op jit(solution)/shard_map/ppermute | solution.py:302
  101.2 2.1 %copy-start = (f32[9,64,1024]{2,1,0:T(8,128)}, f32[9,64,1024]{2,1,0:T(8,128)S(1)}, u32[]{:S(2)}) copy-start(f32[9,64,1024]{2,1,0:T(8,128)S(1)} %get-tuple-element.116.push_out) | copy-start | bytes 7077892
  101.2 2.1 %copy-start.3 = (bf16[9,256,256]{2,1,0:T(8,128)(2,1)}, bf16[9,256,256]{2,1,0:T(8,128)(2,1)S(1)}, u32[]{:S(2)}) copy-start(bf16[9,256,256]{2,1,0:T(8,128)(2,1)S(1)} %get-tuple-element.114.pair) | copy-start | bytes 3538948
  101.2 2.1 %copy-start.5 = (bf16[2304,128]{1,0:T(8,128)(2,1)}, bf16[2304,128]{1,0:T(8,128)(2,1)S(1)}, u32[]{:S(2)}) copy-start(bf16[2304,128]{1,0:T(8,128)(2,1)S(1)} %get-tuple-element.111.keys) | copy-start | bytes 1769476
  103.3 1.3 copy-start.12
  104.6 0.8 copy-start.13
  105.4 18.7 %all-to-all-start = ((bf16[16,16,1024]{2,1,0:T(8,128)(2,1)}), bf16[16,16,1024]{2,1,0:T(8,128)(2,1)S(1)}, u32[]{:S(2)}, u32[]{:S(2)}) async-start(bf16[16,16,1024]{2,1,0:T(8,128)(2,1)} %get-tuple-element.120), calls=%async_computation | async-start | bytes 1048576 | tf_op jit(solution)/shard_map/all_to_all | solution.py:455
  162.9 4.6 %collective-permute-start.13 = (bf16[512,2176]{1,0:T(8,128)(2,1)}, bf16[512,2176]{1,0:T(8,128)(2,1)S(1)}, u32[]{:S(2)}, u32[]{:S(2)}) collective-permute-start(bf16[512,2176]{1,0:T(8,128)(2,1)} %get-tuple-element.122), channel_id=1, source_target_pairs={{0,1},{1,0},{2,3},{3,2},{4,5},{5,4},{6,7},{7,6},{8,9},{9,8},{10,11... | collective-permute-start | bytes 6684680 | tf_op jit(solution)/shard_map/ppermute | solution.py:280

commit v6 on v5

--- a/solution.py
+++ b/solution.py
@@ -191,29 +191,31 @@
 
     @pl.when(b == pl.num_programs(0) - 1)
     def _():
-        gain = state[128:]
+        gain = state[128:129]
         high = gain.astype(BF16).astype(F32)
-        top = lax.broadcasted_iota(jnp.int32, gain.shape, 0) == 0
-        gain = jnp.where(top, high, gain - high)
+        cut = lambda v: [v[:, 128 * c : 128 * c + 128] for c in range(D // 128)]
+        parts = cut(high) + cut(gain - high)
         for n in range(total.shape[0]):
-            total[n] = jnp.concatenate([state[8 * n : 8 * n + 8], gain], axis=0).astype(BF16)
+            total[n] = jnp.concatenate(cut(state[8 * n : 8 * n + 8]) + parts, axis=0).astype(BF16)
 
 
 def scan_kernel(which, terms, entering, forth):
     shards = terms.shape[0]
     part = lambda t: terms[t].astype(F32)
-    gain = lambda v: v[8:9] + v[9:10]
+    chunks = range(D // 128)
+    gain = lambda v: jnp.concatenate([v[64 + c : 65 + c] + v[72 + c : 73 + c] for c in chunks], axis=1)
+    rows = lambda v: jnp.concatenate([v[8 * c : 8 * c + 8] for c in chunks], axis=1)
     state = jnp.zeros((8, D), F32)
     for t in range(shards):
         forth[t] = state
         v = part(t)
-        state = state * gain(v) + v[:8]
+        state = state * gain(v) + rows(v)
     back = jnp.zeros((8, D), F32)
     ahead = jnp.full((8, D), which[0], jnp.int32) < shards // 2
     for t in reversed(range(shards)):
         entering[t] = jnp.where(ahead, forth[t], back).astype(BF16)
         v = part(t)
-        back = back * gain(v) + v[:8]
+        back = back * gain(v) + rows(v)
 
 
 def store_halves(core, acc, keep, give):
@@ -441,11 +443,11 @@
     starts, gains, total = call(
         local_kernel,
         "local",
-        (shape((blocks, STATE, D), F32), shape((blocks, 16, D), F32), shape((shards, 16, D), BF16)),
+        (shape((blocks, STATE, D), F32), shape((blocks, 16, D), F32), shape((shards, 80, 128), BF16)),
         pl.GridSpec(
             grid=(2,),
             in_specs=[some(STATE, D), some(STATE, D), whole(blocks, 8, 128)],
-            out_specs=[some(STATE, D), some(16, D), whole(shards, 16, D)],
+            out_specs=[some(STATE, D), some(16, D), whole(shards, 80, 128)],
             scratch_shapes=[vmem(F32, blocks * 8, D), vmem(F32, 136, D)],
         ),
         1 << 24,
@@ -460,7 +462,7 @@
         pltpu.PrefetchScalarGridSpec(
             num_scalar_prefetch=1,
             grid=(1,),
-            in_specs=[whole(shards, 16, D)],
+            in_specs=[whole(shards, 80, 128)],
             out_specs=whole(shards, 8, D),
             scratch_shapes=[vmem(F32, shards, 8, D)],
         ),

time: 209 us -> 208 us (level)
  waiting for transfers between devices: 47.2 us -> 41.7 us
  blocking collectives: 48.1 us -> 53.5 us
    all_to_all x1, blocking collectives: 36.1 us -> 41.5 us  [over_chips(): return lax.all_to_all(half, CHIPS, 0, 0).astype(F32).sum(0)]
    ppermute x3, waiting for transfers between devices: 27 us -> 23.6 us  [on_device(): up_z = lambda v: lax.ppermute(v, 'z', ring('z', 1))]
    all_to_all x1, waiting for transfers between devices: 11.6 us -> 9.48 us  [on_device(): terms = lax.all_to_all(total, TM, 0, 0)]
  transfers between devices with their start and end apart: 15 -> 15, of which waited for: 8 -> 8; matrix products, arithmetic and copies ran while one was open for 2% -> 2% of each run, Pallas kernels for 16% -> 18%
where the time goes in v6:
time: 208 us
  Pallas kernels  75.8 us (36%)
  blocking collectives  53.5 us (26%)
  waiting for transfers between devices  41.7 us (20%)
  starting transfers between devices  19.3 us (9%)
  local copies, waits for them, and re-layouts  10.7 us (5%)
  other arithmetic  6.01 us (3%)
    all_to_all x1, blocking collectives, over_chips(): return lax.all_to_all(half, CHIPS, 0, 0).astype(F32).sum(0)  41.5 us
    pallas_call x3, Pallas kernels, on_device(): pl.pallas_call(body, out_shape=(shape((room, D), BF16), shape((room, D),...  39.5 us
    pallas_call x1, Pallas kernels, on_device(): call(gradient_kernel, 'gradient', (shape((D // 2, both), F32), shape((D /...  26.6 us
    ppermute x3, waiting for transfers between devices, on_device(): up_z = lambda v: lax.ppermute(v, 'z', ring('z', 1))  23.6 us
    all_to_all x1, blocking collectives, on_device(): enter = lax.all_to_all(entering, TM, 0, 0).reshape(128, D)  12 us
    all_to_all x1, waiting for transfers between devices, on_device(): terms = lax.all_to_all(total, TM, 0, 0)  9.48 us
    pallas_call x1, Pallas kernels, on_device(): call(upstream_kernel, 'upstream', (shape((steps, D), BF16), shape((32, st...  7.48 us
    all_to_all x1, starting transfers between devices, on_device(): terms = lax.all_to_all(total, TM, 0, 0)  7.05 us
  transfers between devices with their start and end apart: 15, of which 8 were waited for; matrix products, arithmetic and copies ran while one was open for 2% of the time, Pallas kernels for 18%

profile of v6, /device:TPU:0, one launch (start us, length us, event | category | flops | bytes accessed | tf_op | source)
XLA Modules:
  0.0 207.8 jit_solution(16435233359854687129)
XLA Ops:
  0.6 0.0 copy-start.6
  0.6 0.0 copy-start.9
  0.7 0.0 copy-start.14
  0.7 0.0 copy-start.15
  0.7 2.8 %fusion.12 = (bf16[1,1,512,1024]{3,2,1,0:T(8,128)(2,1)}, bf16[1,1,512,1024]{3,2,1,0:T(8,128)(2,1)S(1)}) fusion(bf16[1,1,1024,1024]{3,2,1,0:T(8,128)(2,1)} %param.10), kind=kLoop, calls=%fused_computation.67 | loop fusion | bytes 4194304 | tf_op jit(solution)/shard_map/slice | solution.py:307
  3.5 2.0 collective-permute-start
  5.5 2.1 %collective-permute-start.1 = (bf16[2,256,1024]{2,1,0:T(8,128)(2,1)}, bf16[2,256,1024]{2,1,0:T(8,128)(2,1)}, u32[]{:S(2)}, u32[]{:S(2)}) collective-permute-start(bf16[2,256,1024]{2,1,0:T(8,128)(2,1)} %bitcast.10), channel_id=1, source_target_pairs={{0,6},{2,0},{4,2},{6,4},{1,7},{3,1},{5,3},{7,5},{8,14},{10,8},{12,... | collective-permute-start | bytes 3145736 | tf_op jit(solution)/shard_map/ppermute | solution.py:306
  7.6 0.0 collective-permute-start.4
  7.6 0.7 compare_select_fusion.11
  8.3 0.7 fusion.11
  9.0 0.7 fusion.10
  9.7 0.1 convert_reduce_fusion.2
  9.9 0.1 iota_minimum_fusion
  9.9 0.2 convert_reduce_fusion.1
  10.1 0.3 select_reduce_fusion
  10.5 0.1 broadcast_select_fusion
  10.5 0.0 copy-done.15
  10.5 0.0 copy-start.10
  10.6 2.2 %copy-done.10 = bf16[1,2048,1024]{2,1,0:T(8,128)(2,1)S(1)} copy-done((bf16[1,2048,1024]{2,1,0:T(8,128)(2,1)S(1)}, bf16[1,2048,1024]{2,1,0:T(8,128)(2,1)}, u32[]{:S(2)}) %copy-start.10) | copy-done | bytes 4194328
  12.7 1.6 copy-done.11
  14.3 7.5 %upstream.1 = (bf16[2048,1024]{1,0:T(8,128)(2,1)S(1)}, f32[32,2048]{1,0:T(8,128)S(1)}, f32[2048,128]{1,0:T(8,128)S(1)}, f32[8,8,128]{2,1,0:T(8,128)S(1)}) custom-call(s32[8]{0:T(128)S(1)} %bitcast.64, f32[16,2048]{1,0:T(8,128)S(1)} %bitcast.68, s32[8,1,256]{2,1,0:T(1,128)S(1)} %bitcast.69, bf16[1,2048,1024]{2,1,0:T(8,128)(2,1)S(1)} %copy-done.10, ...), custom_call_target="tpu_custom_call" | custom-call | flops 4294967296 | bytes 12582912 | tf_op jit(solution)/shard_map/upstream/pallas_call | solution.py:337
  21.8 0.0 copy-start.1
  21.8 9.0 %collective-permute-done.refs_0_ = bf16[2,256,1024]{2,1,0:T(8,128)(2,1)} collective-permute-done((bf16[2,256,1024]{2,1,0:T(8,128)(2,1)S(1)}, bf16[2,256,1024]{2,1,0:T(8,128)(2,1)}, u32[]{:S(2)}, u32[]{:S(2)}) %collective-permute-start) | collective-permute-done | bytes 1048608 | tf_op jit(solution)/shard_map/ppermute | solution.py:305
  30.9 0.0 collective-permute-done.1.refs_1_
  30.9 1.5 collective-permute-start.2
  32.4 1.8 collective-permute-start.3
  34.1 0.1 collective-permute-start.7
  34.2 0.7 fusion.14
  34.9 0.5 collective-permute-start.8
  35.4 0.0 collective-permute-done.4.refs_1_
  35.4 14.2 %stage_0.1 = (bf16[2304,1024]{1,0:T(8,128)(2,1)}, bf16[2304,1024]{1,0:T(8,128)(2,1)}, bf16[2304,128]{1,0:T(8,128)(2,1)S(1)}, bf16[2304,1024]{1,0:T(8,128)(2,1)},...) custom-call(s32[8]{0:T(128)S(1)} %get-tuple-element.139.block, ...), custom_call_target="tpu_custom_call" | custom-call | flops 5368709120 | bytes 16777216 | tf_op jit(solution)/shard_map/stage_0/pallas_call | solution.py:395
  49.6 7.0 %collective-permute-done.2.refs_4_ = bf16[2,256,1024]{2,1,0:T(8,128)(2,1)S(1)} collective-permute-done((bf16[2,256,1024]{2,1,0:T(8,128)(2,1)}, bf16[2,256,1024]{2,1,0:T(8,128)(2,1)S(1)}, u32[]{:S(2)}, u32[]{:S(2)}) %collective-permute-start.2) | collective-permute-done | bytes 1048608 | tf_op jit(solution)/shard_map/ppermute | solution.py:305
  56.7 0.0 collective-permute-done.3.refs_5_
  56.7 0.0 collective-permute-start.10
  56.7 0.5 collective-permute-start.9
  57.2 0.8 collective-permute-start.5
  58.0 0.0 collective-permute-done.7.refs_2_
  58.0 2.4 %collective-permute-start.6 = (bf16[2,256,1024]{2,1,0:T(8,128)(2,1)}, bf16[2,256,1024]{2,1,0:T(8,128)(2,1)S(1)}, u32[]{:S(2)}, u32[]{:S(2)}) collective-permute-start(bf16[2,256,1024]{2,1,0:T(8,128)(2,1)} %collective-permute-done.1.refs_1_), channel_id=1, source_target_pairs={{0,6},{2,0},{4,2},{6,4},{1,7},{3,1},{5,3},{7,5},{8,14},{10,8},{12,... | collective-permute-start | bytes 3145736 | tf_op jit(solution)/shard_map/ppermute | solution.py:306
  60.4 0.0 collective-permute-done.8.refs_3_
  60.4 0.0 collective-permute-done.10.refs_7_
  60.4 0.4 collective-permute-done.9.refs_6_
  60.8 15.3 %stage_1.1 = (bf16[2304,1024]{1,0:T(8,128)(2,1)}, bf16[2304,1024]{1,0:T(8,128)(2,1)}, bf16[2304,128]{1,0:T(8,128)(2,1)S(1)}, bf16[2304,1024]{1,0:T(8,128)(2,1)},...) custom-call(s32[8]{0:T(128)S(1)} %get-tuple-element.138.block, ...), custom_call_target="tpu_custom_call", output_to_operand_aliasing={{0}: (18, {}), {1}: (19, {}), {2}: (20, {}), {3}: (21, {}),... | custom-call | flops 5368709120 | bytes 16777216 | tf_op jit(solution)/shard_map/stage_1/pallas_call | solution.py:395
  76.1 7.6 %collective-permute-done.5.refs_0_ = bf16[2,256,1024]{2,1,0:T(8,128)(2,1)S(1)} collective-permute-done((bf16[2,256,1024]{2,1,0:T(8,128)(2,1)}, bf16[2,256,1024]{2,1,0:T(8,128)(2,1)S(1)}, u32[]{:S(2)}, u32[]{:S(2)}) %collective-permute-start.5) | collective-permute-done | bytes 1048608 | tf_op jit(solution)/shard_map/ppermute | solution.py:305
  83.7 0.0 collective-permute-done.6.refs_1_
  83.7 0.0 collective-permute-start.11
  83.7 0.5 collective-permute-start.12
  84.2 2.1 %collective-permute-done.11.refs_2_ = bf16[2,256,1024]{2,1,0:T(8,128)(2,1)S(1)} collective-permute-done((bf16[2,256,1024]{2,1,0:T(8,128)(2,1)S(1)}, bf16[2,256,1024]{2,1,0:T(8,128)(2,1)S(1)}, u32[]{:S(2)}, u32[]{:S(2)}) %collective-permute-start.11) | collective-permute-done | bytes 1048608 | tf_op jit(solution)/shard_map/ppermute | solution.py:304
  86.3 1.5 collective-permute-done.12.refs_3_
  87.8 10.0 %stage_2.1 = (bf16[2304,1024]{1,0:T(8,128)(2,1)}, bf16[2304,1024]{1,0:T(8,128)(2,1)}, bf16[2304,128]{1,0:T(8,128)(2,1)S(1)}, bf16[2304,1024]{1,0:T(8,128)(2,1)},...) custom-call(s32[8]{0:T(128)S(1)} %get-tuple-element.140.block, ...), custom_call_target="tpu_custom_call", output_to_operand_aliasing={{0}: (14, {}), {1}: (15, {}), {2}: (16, {}), {3}: (17, {}),... | custom-call | flops 5368709120 | bytes 16777216 | tf_op jit(solution)/shard_map/stage_2/pallas_call | solution.py:395
  97.8 2.1 %local.1 = (f32[8,64,1024]{2,1,0:T(8,128)S(1)}, f32[8,16,1024]{2,1,0:T(8,128)S(1)}, bf16[16,80,128]{2,1,0:T(8,128)(2,1)}) custom-call(f32[9,64,1024]{2,1,0:T(8,128)S(1)} %get-tuple-element.115.push_in, f32[9,64,1024]{2,1,0:T(8,128)S(1)} %get-tuple-element.116.push_out, f32[8,8,128]{2,1,0:T(8,128)S(1)} %get-tuple-element.117.ends), custom_call_target="tpu_custom_call" | custom-call | flops 16777216 | bytes 7340032 | tf_op jit(solution)/shard_map/local/pallas_call | solution.py:443
  99.9 1.3 copy-done.12
  101.2 0.8 copy-done.13
  102.0 7.0 %all-to-all-start = ((bf16[16,80,128]{2,1,0:T(8,128)(2,1)}), bf16[16,80,128]{2,1,0:T(8,128)(2,1)S(1)}, u32[]{:S(2)}, u32[]{:S(2)}) async-start(bf16[16,80,128]{2,1,0:T(8,128)(2,1)} %get-tuple-element.120), calls=%async_computation | async-start | bytes 655360 | tf_op jit(solution)/shard_map/all_to_all | solution.py:457
  109.1 9.5 %all-to-all-done.terms = bf16[16,80,128]{2,1,0:T(8,128)(2,1)S(1)} async-done(((bf16[16,80,128]{2,1,0:T(8,128)(2,1)}), bf16[16,80,128]{2,1,0:T(8,128)(2,1)S(1)}, u32[]{:S(2)}, u32[]{:S(2)}) %all-to-all-start) | async-done | bytes 327712 | tf_op jit(solution)/shard_map/all_to_all | solution.py:457
  118.6 0.2 scan.1
  118.8 12.0 %all_to_all.15 = bf16[16,8,1024]{2,1,0:T(8,128)(2,1)} all-to-all(bf16[16,8,1024]{2,1,0:T(8,128)(2,1)S(1)} %scan.1), channel_id=1, replica_groups=mesh['y'=4,'x'=4,'z'=4,'c'=2] {'y','x'}, dimensions={0} | all-to-all | bytes 524288 | tf_op jit(solution)/shard_map/all_to_all | solution.py:472
  130.7 26.6 %gradient.1 = (f32[512,2176]{1,0:T(8,128)}, bf16[512,2176]{1,0:T(8,128)(2,1)}) custom-call(s32[1]{0:T(128)} %bitcast.core, s32[8]{0:T(128)} %bitcast.63, bf16[1,2048,1024]{2,1,0:T(8,128)(2,1)} %cot.3, bf16[2304,1024]{1,0:T(8,128)(2,1)} %get-tuple-element.109.taken, bf16[2304,1024]{1,0:T(8,128)(2,1)} %get-tuple-element.110.inner, ...), custom_call_target="tpu_custom_call" | custom-call | flops 13958643712 | bytes 37748736 | tf_op jit(solution)/shard_map/gradient/pallas_call | solution.py:482
  157.3 0.1 collective-permute-start.13
  157.4 4.5 %collective-permute-done.13 = bf16[512,2176]{1,0:T(8,128)(2,1)S(1)} collective-permute-done((bf16[512,2176]{1,0:T(8,128)(2,1)}, bf16[512,2176]{1,0:T(8,128)(2,1)S(1)}, u32[]{:S(2)}, u32[]{:S(2)}) %collective-permute-start.13) | collective-permute-done | bytes 2228256 | tf_op jit(solution)/shard_map/ppermute | solution.py:282
  161.9 2.8 %fusion = bf16[64,8,2176]{2,1,0:T(8,128)(2,1)S(1)} fusion(f32[512,2176]{1,0:T(8,128)} %get-tuple-element.121, bf16[512,2176]{1,0:T(8,128)(2,1)S(1)} %collective-permute-done.13), kind=kLoop, calls=%fused_computation.2 | loop fusion | flops 3342336 | bytes 8912896 | tf_op jit(solution)/shard_map/reshape | solution.py:284
  164.7 41.5 %all_to_all.16 = bf16[64,8,2176]{2,1,0:T(8,128)(2,1)S(1)} all-to-all(bf16[64,8,2176]{2,1,0:T(8,128)(2,1)S(1)} %fusion), channel_id=1, replica_groups=mesh['y'=4,'x'=4,'z'=4,'c'=2] {'y','x','z'}, dimensions={0} | all-to-all | bytes 4456448 | tf_op jit(solution)/shard_map/all_to_all | solution.py:288
  206.2 0.3 convert_reduce_fusion
  206.6 0.6 fusion.13
  207.2 0.6 slice.77
  (26 shorter events, 0.1 us)
Async XLA Ops:
  0.6 7.0 %copy-start.6 = (bf16[1,1,1024,1024]{3,2,1,0:T(8,128)(2,1)S(1)}, bf16[1,1,1024,1024]{3,2,1,0:T(8,128)(2,1)}, u32[]{:S(2)}) copy-start(bf16[1,1,1024,1024]{3,2,1,0:T(8,128)(2,1)} %param.10) | copy-start | bytes 6291460
  0.6 9.9 %copy-start.9 = (s32[1,1,8]{2,1,0:T(1,128)S(1)}, s32[1,1,8]{2,1,0:T(1,128)}, u32[]{:S(2)}) copy-start(s32[1,1,8]{2,1,0:T(1,128)} %param.13) | copy-start | bytes 100
  0.7 9.9 %copy-start.14 = (f32[1,16,2048]{2,1,0:T(8,128)S(1)}, f32[1,16,2048]{2,1,0:T(8,128)}, u32[]{:S(2)}) copy-start(f32[1,16,2048]{2,1,0:T(8,128)} %param.14) | copy-start | bytes 393220
  0.7 9.9 %copy-start.15 = (s32[1,2048]{1,0:T(1,128)S(1)}, s32[1,2048]{1,0:T(1,128)}, u32[]{:S(2)}) copy-start(s32[1,2048]{1,0:T(1,128)} %param.15) | copy-start | bytes 24580
  3.5 27.4 %collective-permute-start = (bf16[2,256,1024]{2,1,0:T(8,128)(2,1)S(1)}, bf16[2,256,1024]{2,1,0:T(8,128)(2,1)}, u32[]{:S(2)}, u32[]{:S(2)}) collective-permute-start(bf16[2,256,1024]{2,1,0:T(8,128)(2,1)S(1)} %bitcast.70), channel_id=1, source_target_pairs={{0,2},{2,4},{4,6},{6,0},{1,3},{3,5},{5,7},{7,1},{8,10},{10,12},{12... | collective-permute-start | bytes 3145736 | tf_op jit(solution)/shard_map/ppermute | solution.py:305
  5.5 25.4 %collective-permute-start.1 = (bf16[2,256,1024]{2,1,0:T(8,128)(2,1)}, bf16[2,256,1024]{2,1,0:T(8,128)(2,1)}, u32[]{:S(2)}, u32[]{:S(2)}) collective-permute-start(bf16[2,256,1024]{2,1,0:T(8,128)(2,1)} %bitcast.10), channel_id=1, source_target_pairs={{0,6},{2,0},{4,2},{6,4},{1,7},{3,1},{5,3},{7,5},{8,14},{10,8},{12,... | collective-permute-start | bytes 3145736 | tf_op jit(solution)/shard_map/ppermute | solution.py:306
  7.6 27.8 %collective-permute-start.4 = (bf16[4,256,1024]{2,1,0:T(8,128)(2,1)S(1)}, bf16[4,256,1024]{2,1,0:T(8,128)(2,1)}, u32[]{:S(2)}, u32[]{:S(2)}) collective-permute-start(bf16[4,256,1024]{2,1,0:T(8,128)(2,1)S(1)} %bitcast.61), channel_id=1, source_target_pairs={{0,1},{1,0},{2,3},{3,2},{4,5},{5,4},{6,7},{7,6},{8,9},{9,8},{10,11... | collective-permute-start | bytes 6291464 | tf_op jit(solution)/shard_map/ppermute | solution.py:304
  10.5 2.2 %copy-start.10 = (bf16[1,2048,1024]{2,1,0:T(8,128)(2,1)S(1)}, bf16[1,2048,1024]{2,1,0:T(8,128)(2,1)}, u32[]{:S(2)}) copy-start(bf16[1,2048,1024]{2,1,0:T(8,128)(2,1)} %cot.3) | copy-start | bytes 12582916
  12.7 1.6 copy-start.11
  14.3 21.1 %copy-start.2 = (bf16[1024,1024]{1,0:T(8,128)(2,1)S(1)}, bf16[1024,1024]{1,0:T(8,128)(2,1)}, u32[]{:S(2)}) copy-start(bf16[1024,1024]{1,0:T(8,128)(2,1)} %refs_4_.1) | copy-start | bytes 6291460
  14.3 21.1 %copy-start.7 = (bf16[1,1,1024,1024]{3,2,1,0:T(8,128)(2,1)S(1)}, bf16[1,1,1024,1024]{3,2,1,0:T(8,128)(2,1)}, u32[]{:S(2)}) copy-start(bf16[1,1,1024,1024]{3,2,1,0:T(8,128)(2,1)} %param.10) | copy-start | bytes 6291460
  14.3 21.1 %copy-start.8 = (bf16[1024,128]{1,0:T(8,128)(2,1)S(1)}, bf16[1024,128]{1,0:T(8,128)(2,1)}, u32[]{:S(2)}) copy-start(bf16[1024,128]{1,0:T(8,128)(2,1)} %refs_5_.1) | copy-start | bytes 786436
  21.8 66.0 %copy-start.1 = (bf16[2048,1024]{1,0:T(8,128)(2,1)}, bf16[2048,1024]{1,0:T(8,128)(2,1)S(1)}, u32[]{:S(2)}) copy-start(bf16[2048,1024]{1,0:T(8,128)(2,1)S(1)} %get-tuple-element.68.refs_4_.refs_10_.refs_6_.up) | copy-start | bytes 12582916
  21.8 66.0 %copy-start.4 = (f32[2048,128]{1,0:T(8,128)}, f32[2048,128]{1,0:T(8,128)S(1)}, u32[]{:S(2)}) copy-start(f32[2048,128]{1,0:T(8,128)S(1)} %get-tuple-element.70.refs_6_.refs_12_.refs_8_.cols) | copy-start | bytes 3145732
  30.9 25.8 %collective-permute-start.2 = (bf16[2,256,1024]{2,1,0:T(8,128)(2,1)}, bf16[2,256,1024]{2,1,0:T(8,128)(2,1)S(1)}, u32[]{:S(2)}, u32[]{:S(2)}) collective-permute-start(bf16[2,256,1024]{2,1,0:T(8,128)(2,1)} %bitcast.10), channel_id=1, source_target_pairs={{0,2},{2,4},{4,6},{6,0},{1,3},{3,5},{5,7},{7,1},{8,10},{10,12},{12... | collective-permute-start | bytes 3145736 | tf_op jit(solution)/shard_map/ppermute | solution.py:305
  32.4 24.3 %collective-permute-start.3 = (bf16[2,256,1024]{2,1,0:T(8,128)(2,1)S(1)}, bf16[2,256,1024]{2,1,0:T(8,128)(2,1)S(1)}, u32[]{:S(2)}, u32[]{:S(2)}) collective-permute-start(bf16[2,256,1024]{2,1,0:T(8,128)(2,1)S(1)} %bitcast.71), channel_id=1, source_target_pairs={{0,6},{2,0},{4,2},{6,4},{1,7},{3,1},{5,3},{7,5},{8,14},{10,8},{12,... | collective-permute-start | bytes 3145736 | tf_op jit(solution)/shard_map/ppermute | solution.py:306
  34.1 23.9 %collective-permute-start.7 = (bf16[2,256,1024]{2,1,0:T(8,128)(2,1)}, bf16[2,256,1024]{2,1,0:T(8,128)(2,1)S(1)}, u32[]{:S(2)}, u32[]{:S(2)}) collective-permute-start(bf16[2,256,1024]{2,1,0:T(8,128)(2,1)} %collective-permute-done.refs_0_), channel_id=1, source_target_pairs={{0,1},{1,0},{2,3},{3,2},{4,5},{5,4},{6,7},{7,6},{8,9},{9,8},{10,11... | collective-permute-start | bytes 3145736 | tf_op jit(solution)/shard_map/ppermute | solution.py:304
  34.9 25.5 %collective-permute-start.8 = (bf16[2,256,1024]{2,1,0:T(8,128)(2,1)}, bf16[2,256,1024]{2,1,0:T(8,128)(2,1)S(1)}, u32[]{:S(2)}, u32[]{:S(2)}) collective-permute-start(bf16[2,256,1024]{2,1,0:T(8,128)(2,1)} %collective-permute-done.1.refs_1_), channel_id=1, source_target_pairs={{0,1},{1,0},{2,3},{3,2},{4,5},{5,4},{6,7},{7,6},{8,9},{9,8},{10,11... | collective-permute-start | bytes 3145736 | tf_op jit(solution)/shard_map/ppermute | solution.py:304
  56.7 3.8 %collective-permute-start.10 = (bf16[2,256,1024]{2,1,0:T(8,128)(2,1)S(1)}, bf16[2,256,1024]{2,1,0:T(8,128)(2,1)S(1)}, u32[]{:S(2)}, u32[]{:S(2)}) collective-permute-start(bf16[2,256,1024]{2,1,0:T(8,128)(2,1)S(1)} %collective-permute-done.3.refs_5_), channel_id=1, source_target_pairs={{0,1},{1,0},{2,3},{3,2},{4,5},{5,4},{6,7},{7,6},{8,9},{9,8},{10,11... | collective-permute-start | bytes 3145736 | tf_op jit(solution)/shard_map/ppermute | solution.py:304
  56.7 4.2 %collective-permute-start.9 = (bf16[2,256,1024]{2,1,0:T(8,128)(2,1)S(1)}, bf16[2,256,1024]{2,1,0:T(8,128)(2,1)S(1)}, u32[]{:S(2)}, u32[]{:S(2)}) collective-permute-start(bf16[2,256,1024]{2,1,0:T(8,128)(2,1)S(1)} %collective-permute-done.2.refs_4_), channel_id=1, source_target_pairs={{0,1},{1,0},{2,3},{3,2},{4,5},{5,4},{6,7},{7,6},{8,9},{9,8},{10,11... | collective-permute-start | bytes 3145736 | tf_op jit(solution)/shard_map/ppermute | solution.py:304
  57.2 26.5 %collective-permute-start.5 = (bf16[2,256,1024]{2,1,0:T(8,128)(2,1)}, bf16[2,256,1024]{2,1,0:T(8,128)(2,1)S(1)}, u32[]{:S(2)}, u32[]{:S(2)}) collective-permute-start(bf16[2,256,1024]{2,1,0:T(8,128)(2,1)} %collective-permute-done.refs_0_), channel_id=1, source_target_pairs={{0,2},{2,4},{4,6},{6,0},{1,3},{3,5},{5,7},{7,1},{8,10},{10,12},{12... | collective-permute-start | bytes 3145736 | tf_op jit(solution)/shard_map/ppermute | solution.py:305
  58.0 25.7 %collective-permute-start.6 = (bf16[2,256,1024]{2,1,0:T(8,128)(2,1)}, bf16[2,256,1024]{2,1,0:T(8,128)(2,1)S(1)}, u32[]{:S(2)}, u32[]{:S(2)}) collective-permute-start(bf16[2,256,1024]{2,1,0:T(8,128)(2,1)} %collective-permute-done.1.refs_1_), channel_id=1, source_target_pairs={{0,6},{2,0},{4,2},{6,4},{1,7},{3,1},{5,3},{7,5},{8,14},{10,8},{12,... | collective-permute-start | bytes 3145736 | tf_op jit(solution)/shard_map/ppermute | solution.py:306
  83.7 2.7 %collective-permute-start.11 = (bf16[2,256,1024]{2,1,0:T(8,128)(2,1)S(1)}, bf16[2,256,1024]{2,1,0:T(8,128)(2,1)S(1)}, u32[]{:S(2)}, u32[]{:S(2)}) collective-permute-start(bf16[2,256,1024]{2,1,0:T(8,128)(2,1)S(1)} %collective-permute-done.5.refs_0_), channel_id=1, source_target_pairs={{0,1},{1,0},{2,3},{3,2},{4,5},{5,4},{6,7},{7,6},{8,9},{9,8},{10,11... | collective-permute-start | bytes 3145736 | tf_op jit(solution)/shard_map/ppermute | solution.py:304
  83.7 4.2 %collective-permute-start.12 = (bf16[2,256,1024]{2,1,0:T(8,128)(2,1)S(1)}, bf16[2,256,1024]{2,1,0:T(8,128)(2,1)S(1)}, u32[]{:S(2)}, u32[]{:S(2)}) collective-permute-start(bf16[2,256,1024]{2,1,0:T(8,128)(2,1)S(1)} %collective-permute-done.6.refs_1_), channel_id=1, source_target_pairs={{0,1},{1,0},{2,3},{3,2},{4,5},{5,4},{6,7},{7,6},{8,9},{9,8},{10,11... | collective-permute-start | bytes 3145736 | tf_op jit(solution)/shard_map/ppermute | solution.py:304
  97.8 2.1 %copy-start = (f32[9,64,1024]{2,1,0:T(8,128)}, f32[9,64,1024]{2,1,0:T(8,128)S(1)}, u32[]{:S(2)}) copy-start(f32[9,64,1024]{2,1,0:T(8,128)S(1)} %get-tuple-element.116.push_out) | copy-start | bytes 7077892
  97.8 2.1 %copy-start.3 = (bf16[9,256,256]{2,1,0:T(8,128)(2,1)}, bf16[9,256,256]{2,1,0:T(8,128)(2,1)S(1)}, u32[]{:S(2)}) copy-start(bf16[9,256,256]{2,1,0:T(8,128)(2,1)S(1)} %get-tuple-element.114.pair) | copy-start | bytes 3538948
  97.8 2.1 %copy-start.5 = (bf16[2304,128]{1,0:T(8,128)(2,1)}, bf16[2304,128]{1,0:T(8,128)(2,1)S(1)}, u32[]{:S(2)}) copy-start(bf16[2304,128]{1,0:T(8,128)(2,1)S(1)} %get-tuple-element.111.keys) | copy-start | bytes 1769476
  99.9 1.3 copy-start.12
  101.2 0.8 copy-start.13
  102.0 16.5 %all-to-all-start = ((bf16[16,80,128]{2,1,0:T(8,128)(2,1)}), bf16[16,80,128]{2,1,0:T(8,128)(2,1)S(1)}, u32[]{:S(2)}, u32[]{:S(2)}) async-start(bf16[16,80,128]{2,1,0:T(8,128)(2,1)} %get-tuple-element.120), calls=%async_computation | async-start | bytes 655360 | tf_op jit(solution)/shard_map/all_to_all | solution.py:457
  157.3 4.6 %collective-permute-start.13 = (bf16[512,2176]{1,0:T(8,128)(2,1)}, bf16[512,2176]{1,0:T(8,128)(2,1)S(1)}, u32[]{:S(2)}, u32[]{:S(2)}) collective-permute-start(bf16[512,2176]{1,0:T(8,128)(2,1)} %get-tuple-element.122), channel_id=1, source_target_pairs={{0,1},{1,0},{2,3},{3,2},{4,5},{5,4},{6,7},{7,6},{8,9},{9,8},{10,11... | collective-permute-start | bytes 6684680 | tf_op jit(solution)/shard_map/ppermute | solution.py:282
